TPU v7x, 512 devices: a whole 4x8x8 slice. The times are simulated.
512 devices in a mesh: depth: 8 (over z_lo, x), lat: 64 (over z_hi, y, core).
Axes of the slice: x: 4, y: 8, z: 8 (z_hi: 4, z_lo: 2; z = z_hi * 2 + z_lo), core: 2. Of those that a mesh axis runs over, the one named last changes fastest.
Arguments:
- fin_mask: int32 [32, 1024, 1024], P('depth', 'lat'), may hold values from 0 to 1, as said below
- stopping_power: bfloat16 [32, 1024, 1024], P('depth', 'lat'), may hold values from 0.25 to 4
- pairs_before: bfloat16 [32, 1024, 1024], P('depth', 'lat'), may hold values from 0.19921875 to 2
- clusters_before: bfloat16 [32, 1024, 1024], P('depth', 'lat'), may hold values from 0.19921875 to 2
- taps_across: bfloat16 [4, 32, 97], P(None, 'depth'), may hold values from 0 to 0.25
- taps_along: bfloat16 [4, 32, 97], P(None, 'depth'), may hold values from 0 to 0.25
- tilt_shift: int32 [32], P('depth'), may hold values from 0 to 16
- layer_doses: float32 [4, 32], P(None, 'depth'), may hold values from 0.5 to 2.5
- diffusivity: float32 [3], replicated, may hold values from 0.08 to 0.16
- reaction_rates: float32 [5], replicated, may hold values from 0.01 to 0.04
Outputs:
- concentrations: float32 [5, 32, 1024, 1024], P(None, 'depth', 'lat')
Inputs may be any that keep to these rules, and one draw needn't show every extreme that they name: `fin_mask`: 1 marks silicon, 0 oxide or empty space.
All inputs are finite; a program needn't handle non-finite values.
Results may differ from a plain program's by a relative error of at most 0.00035.
Values may be sent and summed in bfloat16 or wider, within the bound.
No kernel may reach another device: no remote copies, remote signals or barrier semaphores. Data moves between devices by JAX's collectives and lax.ppermute only.
A program may use at most 64 MiB of HBM per device.

v0:
```python
import jax
import jax.numpy as jnp
from jax import lax
from jax.sharding import PartitionSpec as P

TAPS = 97
SHIFT_MAX = 16
SUBSTEPS = 2


BLOCK = 128


def padded_2(array, sides, width):
    for axis, dim in sides:
        size, length = (lax.axis_size(axis), array.shape[dim])
        up = [(i, (i + 1) % size) for i in range(size - 1)]
        down = [(j, i) for i, j in up]
        last = lax.slice_in_dim(array, length - width, length, axis=dim)
        leading = lax.slice_in_dim(array, 0, width, axis=dim)
        before = lax.ppermute(last, axis, up)
        after = lax.ppermute(leading, axis, down)
        array = jnp.concatenate([before, array, after], axis=dim)
    return array


def passed_along(block, axis, distance):
    devices = range(lax.axis_size(axis))
    route = [(i - distance, i) for i in devices if i - distance in devices]
    return lax.ppermute(block, axis, route)


def band_matrix(tap_values):
    half_width = (tap_values.shape[0] - 1) // 2
    lead_zeros = BLOCK - half_width + SHIFT_MAX
    tail_zeros = 4 * BLOCK - (BLOCK - half_width) - tap_values.shape[0]
    band_line = jnp.concatenate(
        [
            jnp.zeros((lead_zeros,), tap_values.dtype),
            tap_values,
            jnp.zeros((tail_zeros,), tap_values.dtype),
        ]
    )
    band_line = lax.dynamic_slice_in_dim(band_line, SHIFT_MAX, 4 * BLOCK)
    tiled_line = jnp.tile(band_line, BLOCK)[: BLOCK * (4 * BLOCK - 1)].reshape(BLOCK, 4 * BLOCK - 1)
    return tiled_line[:, : 3 * BLOCK]


def band_fixed(tap_values):
    return band_matrix(tap_values)


def band_windows(values, axis):
    pad_width = [(0, 0)] * values.ndim
    pad_width[axis] = (BLOCK, BLOCK)
    padded = jnp.pad(values, pad_width)
    count = values.shape[axis] // BLOCK + 2
    shaped = padded.reshape(values.shape[:axis] + (count, BLOCK) + values.shape[axis + 1 :])
    parts = [lax.slice_in_dim(shaped, start, start + count - 2, axis=axis) for start in range(3)]
    return jnp.concatenate(parts, axis=axis + 1)


def mobile_laplace(mobile):
    padded = padded_2(mobile, (("depth", 1), ("lat", 2)), 1)
    center = padded[:, 1:-1, 1:-1, :]
    near = padded[:, 2:, 1:-1, :] + padded[:, :-2, 1:-1, :]
    near = near + padded[:, 1:-1, 2:, :] + padded[:, 1:-1, :-2, :]
    zero_column = jnp.zeros_like(center[..., :1])
    near = near + jnp.concatenate([center[..., 1:], zero_column], axis=-1)
    near = near + jnp.concatenate([zero_column, center[..., :-1]], axis=-1)
    return near - 6.0 * center


def body(
    fin_mask,
    stopping_power,
    pairs_before,
    clusters_before,
    taps_across,
    taps_along,
    tilt_shift,
    layer_doses,
    diffusivity,
    reaction_rates,
):
    source = fin_mask.astype(jnp.bfloat16) * stopping_power
    layers, width, length = source.shape
    half_width = (TAPS - 1) // 2
    left_reach = (half_width + width - 1) // width
    right_reach = (half_width + SHIFT_MAX + width - 1) // width
    positions = jnp.arange(width)
    total = jnp.zeros((4, layers, width, length), jnp.float32)
    for offset in range(-left_reach, right_reach + 1):
        if offset == 0:
            block_piece = source
        else:
            block_piece = passed_along(source, "lat", -offset)
        tap_index = (
            offset * width
            + positions[None, None, :]
            - positions[None, :, None]
            + half_width
            - tilt_shift[:, None, None]
        )
        selector = (tap_index[..., None] == jnp.arange(TAPS)).astype(jnp.bfloat16)
        matrix_x = jnp.einsum(
            "zxwi,szi->szxw", selector, taps_across, preferred_element_type=jnp.float32
        ).astype(jnp.bfloat16)
        total = total + jnp.einsum(
            "szxw,zwy->szxy", matrix_x, block_piece, preferred_element_type=jnp.float32
        )
    spread = total.astype(jnp.bfloat16)
    matrix_y = jax.vmap(jax.vmap(band_fixed))(taps_along)
    windows_y = band_windows(spread, 3)
    implanted = jnp.einsum(
        "szxca,szba->szxcb", windows_y, matrix_y, preferred_element_type=jnp.float32
    )
    implanted = implanted.reshape(4, layers, width, length) * layer_doses[:, :, None, None]
    silicon = fin_mask.astype(jnp.float32)
    arsenic = silicon * implanted[0]
    interstitial = silicon * implanted[1]
    vacancy = silicon * implanted[2]
    pair_field = silicon * pairs_before.astype(jnp.float32)
    clusters = silicon * (clusters_before.astype(jnp.float32) + implanted[3])
    for repeat in range(SUBSTEPS):
        laplaces = mobile_laplace(jnp.stack([interstitial, vacancy, pair_field]))
        recombine = reaction_rates[0] * interstitial * vacancy
        pairing = reaction_rates[1] * arsenic * interstitial - reaction_rates[2] * pair_field
        clustering = reaction_rates[3] * interstitial * interstitial - reaction_rates[4] * clusters
        new_inter = interstitial + silicon * (
            diffusivity[0] * laplaces[0] - recombine - pairing - 2.0 * clustering
        )
        new_vacancy = vacancy + silicon * (diffusivity[1] * laplaces[1] - recombine)
        new_arsenic = arsenic - silicon * pairing
        new_pair = pair_field + silicon * (diffusivity[2] * laplaces[2] + pairing)
        new_clusters = clusters + silicon * clustering
        interstitial, vacancy, arsenic, pair_field, clusters = (
            new_inter,
            new_vacancy,
            new_arsenic,
            new_pair,
            new_clusters,
        )
    return jnp.stack([arsenic, interstitial, vacancy, pair_field, clusters])


def solution(mesh):
    return jax.shard_map(
        body,
        mesh=mesh,
        in_specs=(
            P("depth", "lat", None),
            P("depth", "lat", None),
            P("depth", "lat", None),
            P("depth", "lat", None),
            P(None, "depth", None),
            P(None, "depth", None),
            P("depth"),
            P(None, "depth"),
            P(),
            P(),
        ),
        out_specs=P(None, "depth", "lat", None),
        check_vma=False,
    )
```

profile of v0, /device:TPU:320, one launch (start us, length us, event | category | flops | bytes accessed | tf_op | source)
XLA Modules:
  0.0 132.3 jit_solution(3791341713441151861)
XLA Ops:
  0.0 1.1 convert_multiply_fusion.1
  1.1 1.9 %collective-permute-start.2 = (bf16[4,16,1024]{2,1,0:T(8,128)(2,1)S(1)}, bf16[4,16,1024]{2,1,0:T(8,128)(2,1)}, u32[]{:S(2)}, u32[]{:S(2)}) collective-permute-start(bf16[4,16,1024]{2,1,0:T(8,128)(2,1)S(1)} %convert_multiply_fusion.1), channel_id=1, source_target_pairs={{0,1},{1,2},{2,3},{3,4},{4,5},{5,6},{6,7},{7,8},{8,9},{9,10},{10,1... | collective-permute-start | bytes 393224 | tf_op jit(solution)/shard_map/ppermute | solution.py:30
  3.0 3.5 %collective-permute-start.1 = (bf16[4,16,1024]{2,1,0:T(8,128)(2,1)S(1)}, bf16[4,16,1024]{2,1,0:T(8,128)(2,1)}, u32[]{:S(2)}, u32[]{:S(2)}) collective-permute-start(bf16[4,16,1024]{2,1,0:T(8,128)(2,1)S(1)} %convert_multiply_fusion.1), channel_id=1, source_target_pairs={{0,2},{1,3},{2,4},{3,5},{4,6},{5,7},{6,8},{7,9},{8,10},{9,11},{10,... | collective-permute-start | bytes 393224 | tf_op jit(solution)/shard_map/ppermute | solution.py:30
  6.5 4.5 %collective-permute-start = (bf16[4,16,1024]{2,1,0:T(8,128)(2,1)S(1)}, bf16[4,16,1024]{2,1,0:T(8,128)(2,1)}, u32[]{:S(2)}, u32[]{:S(2)}) collective-permute-start(bf16[4,16,1024]{2,1,0:T(8,128)(2,1)S(1)} %convert_multiply_fusion.1), channel_id=1, source_target_pairs={{0,3},{1,4},{2,5},{3,6},{4,7},{5,8},{6,9},{7,10},{8,11},{9,12},{10... | collective-permute-start | bytes 393224 | tf_op jit(solution)/shard_map/ppermute | solution.py:30
  11.0 6.5 %collective-permute-start.6 = (bf16[4,16,1024]{2,1,0:T(8,128)(2,1)S(1)}, bf16[4,16,1024]{2,1,0:T(8,128)(2,1)S(1)}, u32[]{:S(2)}, u32[]{:S(2)}) collective-permute-start(bf16[4,16,1024]{2,1,0:T(8,128)(2,1)S(1)} %convert_multiply_fusion.1), channel_id=1, source_target_pairs={{4,0},{5,1},{6,2},{7,3},{8,4},{9,5},{10,6},{11,7},{12,8},{13,9},{1... | collective-permute-start | bytes 393224 | tf_op jit(solution)/shard_map/ppermute | solution.py:30
  17.4 1.9 %collective-permute-start.5 = (bf16[4,16,1024]{2,1,0:T(8,128)(2,1)S(1)}, bf16[4,16,1024]{2,1,0:T(8,128)(2,1)S(1)}, u32[]{:S(2)}, u32[]{:S(2)}) collective-permute-start(bf16[4,16,1024]{2,1,0:T(8,128)(2,1)S(1)} %convert_multiply_fusion.1), channel_id=1, source_target_pairs={{3,0},{4,1},{5,2},{6,3},{7,4},{8,5},{9,6},{10,7},{11,8},{12,9},{13... | collective-permute-start | bytes 393224 | tf_op jit(solution)/shard_map/ppermute | solution.py:30
  19.5 1.4 %broadcast_subtract_fusion.3 = (s32[4,16,16]{2,1,0:T(8,128)}, s32[4,16,16]{2,1,0:T(8,128)S(1)}, s32[4,16,16]{2,1,0:T(8,128)S(1)}, s32[4,16,16]{2,1,0:T(8,128)S(1...) fusion(s32[16,16]{1,0:T(8,128)S(1)} %get-tuple-element.46, ...), kind=kLoop, calls=%fused_computation.198 | loop fusion | flops 8192 | bytes 40976 | tf_op jit(solution)/shard_map/sub | solution.py:99
  20.9 1.4 %fusion.27 = bf16[4,16,16,4]{2,3,1,0:T(4,128)(2,1)} fusion(s32[4,16,16]{2,1,0:T(8,128)S(1)} %get-tuple-element.37, bf16[4,4,97,1]{2,1,0,3:T(4,128)(2,1)S(1)} %bitcast.257), kind=kOutput, calls=%fused_computation.73 | convolution fusion | flops 893952 | bytes 15392 | tf_op jit(solution)/shard_map/zxwi,szi->szxw/dot_general | solution.py:106
  22.3 1.4 %fusion.26 = bf16[4,16,16,4]{2,3,1,0:T(4,128)(2,1)} fusion(s32[4,16,16]{2,1,0:T(8,128)S(1)} %get-tuple-element.36, bf16[4,4,97,1]{2,1,0,3:T(4,128)(2,1)S(1)} %bitcast.258), kind=kOutput, calls=%fused_computation.72 | convolution fusion | flops 893952 | bytes 15392 | tf_op jit(solution)/shard_map/zxwi,szi->szxw/dot_general | solution.py:106
  23.7 0.8 fusion.28
  24.5 0.3 fusion.92
  24.8 1.4 %fusion.25 = bf16[4,16,16,4]{2,3,1,0:T(4,128)(2,1)} fusion(s32[4,16,16]{2,1,0:T(8,128)S(1)} %get-tuple-element.42, bf16[4,4,97,1]{2,1,0,3:T(4,128)(2,1)S(1)} %bitcast.251), kind=kOutput, calls=%fused_computation.71 | convolution fusion | flops 893952 | bytes 15392 | tf_op jit(solution)/shard_map/zxwi,szi->szxw/dot_general | solution.py:106
  26.2 1.4 %fusion.32 = bf16[4,16,16,4]{2,3,1,0:T(4,128)(2,1)} fusion(s32[4,16,16]{2,1,0:T(8,128)S(1)} %get-tuple-element.41, bf16[4,4,97,1]{2,1,0,3:T(4,128)(2,1)S(1)} %bitcast.252), kind=kOutput, calls=%fused_computation.78 | convolution fusion | flops 893952 | bytes 15392 | tf_op jit(solution)/shard_map/zxwi,szi->szxw/dot_general | solution.py:106
  27.6 1.4 %fusion.31 = bf16[4,16,16,4]{2,3,1,0:T(4,128)(2,1)} fusion(s32[4,16,16]{2,1,0:T(8,128)S(1)} %get-tuple-element.40, bf16[4,4,97,1]{2,1,0,3:T(4,128)(2,1)S(1)} %bitcast.253), kind=kOutput, calls=%fused_computation.77 | convolution fusion | flops 893952 | bytes 15392 | tf_op jit(solution)/shard_map/zxwi,szi->szxw/dot_general | solution.py:106
  29.0 1.4 %fusion.30 = bf16[4,16,16,4]{2,3,1,0:T(4,128)(2,1)} fusion(s32[4,16,16]{2,1,0:T(8,128)S(1)} %get-tuple-element.39, bf16[4,4,97,1]{2,1,0,3:T(4,128)(2,1)S(1)} %bitcast.254), kind=kOutput, calls=%fused_computation.76 | convolution fusion | flops 893952 | bytes 15392 | tf_op jit(solution)/shard_map/zxwi,szi->szxw/dot_general | solution.py:106
  30.6 0.2 tile.4
  30.8 2.8 %tile.10 = bf16[4,4,65536]{2,1,0:T(4,128)(2,1)} reshape(bf16[4,4,128,512]{3,2,1,0:T(8,128)(2,1)S(1)} %tile.4) | data formatting | bytes 4194304 | tf_op jit(solution)/shard_map/vmap(vmap())/tile | solution.py:45
  33.6 1.6 %slice-done = bf16[4,4,65408]{2,1,0:T(4,128)(2,1)S(1)} async-done(((bf16[4,4,65536]{2,1,0:T(4,128)(2,1)}), bf16[4,4,65408]{2,1,0:T(4,128)(2,1)S(1)}, s32[]{:S(2)}) %slice-start) | async-done | bytes 2093080 | tf_op jit(solution)/shard_map/vmap(vmap())/slice | solution.py:45
  35.2 4.6 %reshape.264 = bf16[4,4,128,511]{3,2,1,0:T(8,128)(2,1)} reshape(bf16[4,4,65408]{2,1,0:T(4,128)(2,1)S(1)} %slice-done) | data formatting | bytes 4186112 | tf_op jit(solution)/shard_map/vmap(vmap())/reshape | solution.py:45
  39.8 1.6 %fusion.29 = bf16[4,16,16,4]{2,3,1,0:T(4,128)(2,1)S(1)} fusion(s32[4,16,16]{2,1,0:T(8,128)} %get-tuple-element.35, bf16[4,4,97,1]{2,1,0,3:T(4,128)(2,1)S(1)} %bitcast.255), kind=kOutput, calls=%fused_computation.75 | convolution fusion | flops 893952 | bytes 15392 | tf_op jit(solution)/shard_map/zxwi,szi->szxw/dot_general | solution.py:106
  41.4 2.4 %collective-permute-start.4 = (bf16[4,16,1024]{2,1,0:T(8,128)(2,1)S(1)}, bf16[4,16,1024]{2,1,0:T(8,128)(2,1)S(1)}, u32[]{:S(2)}, u32[]{:S(2)}) collective-permute-start(bf16[4,16,1024]{2,1,0:T(8,128)(2,1)S(1)} %convert_multiply_fusion.1), channel_id=1, source_target_pairs={{2,0},{3,1},{4,2},{5,3},{6,4},{7,5},{8,6},{9,7},{10,8},{11,9},{12,... | collective-permute-start | bytes 393224 | tf_op jit(solution)/shard_map/ppermute | solution.py:30
  43.8 1.2 fusion.94
  45.0 2.2 %collective-permute-start.3 = (bf16[4,16,1024]{2,1,0:T(8,128)(2,1)S(1)}, bf16[4,16,1024]{2,1,0:T(8,128)(2,1)S(1)}, u32[]{:S(2)}, u32[]{:S(2)}) collective-permute-start(bf16[4,16,1024]{2,1,0:T(8,128)(2,1)S(1)} %convert_multiply_fusion.1), channel_id=1, source_target_pairs={{1,0},{2,1},{3,2},{4,3},{5,4},{6,5},{7,6},{8,7},{9,8},{10,9},{11,1... | collective-permute-start | bytes 393224 | tf_op jit(solution)/shard_map/ppermute | solution.py:30
  47.2 1.2 fusion.96
  48.4 1.2 fusion.7
  49.7 0.3 fusion.85
  50.0 0.3 fusion.87
  50.3 0.2 copy-done.6
  50.5 0.3 fusion.89
  50.8 0.3 fusion.12
  51.2 0.4 reshape.263
  51.6 0.3 fusion.127
  51.9 1.3 copy-done.3
  53.2 0.8 fusion
  54.0 0.2 reshape.265
  54.2 0.5 copy-done.14
  54.8 0.8 copy-done.1
  55.9 4.4 %collective-permute-start.7 = (f32[3,1,16,1024]{3,2,1,0:T(8,128)S(1)}, f32[3,1,16,1024]{3,2,1,0:T(8,128)S(1)}, u32[]{:S(2)}, u32[]{:S(2)}) collective-permute-start(f32[3,1,16,1024]{3,2,1,0:T(8,128)S(1)} %get-tuple-element.25), channel_id=1, source_target_pairs={{64,0},{128,64},{192,128},{256,192},{320,256},{384,320},{448,384},... | collective-permute-start | bytes 589832 | tf_op jit(solution)/shard_map/ppermute | solution.py:22
  60.2 1.9 %collective-permute-start.8 = (f32[3,1,16,1024]{3,2,1,0:T(8,128)S(1)}, f32[3,1,16,1024]{3,2,1,0:T(8,128)S(1)}, u32[]{:S(2)}, u32[]{:S(2)}) collective-permute-start(f32[3,1,16,1024]{3,2,1,0:T(8,128)S(1)} %get-tuple-element.24), channel_id=1, source_target_pairs={{0,64},{64,128},{128,192},{192,256},{256,320},{320,384},{384,448},... | collective-permute-start | bytes 589832 | tf_op jit(solution)/shard_map/ppermute | solution.py:21
  62.2 0.6 fusion.132
  62.8 0.7 fusion.133
  63.5 2.0 %collective-permute-done.7 = f32[3,1,16,1024]{3,2,1,0:T(8,128)S(1)} collective-permute-done((f32[3,1,16,1024]{3,2,1,0:T(8,128)S(1)}, f32[3,1,16,1024]{3,2,1,0:T(8,128)S(1)}, u32[]{:S(2)}, u32[]{:S(2)}) %collective-permute-start.7) | collective-permute-done | bytes 196640 | tf_op jit(solution)/shard_map/ppermute | solution.py:22
  65.4 6.2 %collective-permute-done.8 = f32[3,1,16,1024]{3,2,1,0:T(8,128)S(1)} collective-permute-done((f32[3,1,16,1024]{3,2,1,0:T(8,128)S(1)}, f32[3,1,16,1024]{3,2,1,0:T(8,128)S(1)}, u32[]{:S(2)}, u32[]{:S(2)}) %collective-permute-start.8) | collective-permute-done | bytes 196640 | tf_op jit(solution)/shard_map/ppermute | solution.py:21
  71.8 1.9 %collective-permute-start.10 = (f32[3,6,1,1024]{3,2,1,0:T(1,128)S(1)}, f32[3,6,1,1024]{3,2,1,0:T(1,128)S(1)}, u32[]{:S(2)}, u32[]{:S(2)}) collective-permute-start(f32[3,6,1,1024]{3,2,1,0:T(1,128)S(1)} %get-tuple-element.14), channel_id=1, source_target_pairs={{0,1},{1,2},{2,3},{3,4},{4,5},{5,6},{6,7},{7,8},{8,9},{9,10},{10,1... | collective-permute-start | bytes 221192 | tf_op jit(solution)/shard_map/ppermute | solution.py:21
  73.7 7.9 %collective-permute-start.9 = (f32[3,6,1,1024]{3,2,1,0:T(1,128)S(1)}, f32[3,6,1,1024]{3,2,1,0:T(1,128)S(1)}, u32[]{:S(2)}, u32[]{:S(2)}) collective-permute-start(f32[3,6,1,1024]{3,2,1,0:T(1,128)S(1)} %get-tuple-element.13), channel_id=1, source_target_pairs={{1,0},{2,1},{3,2},{4,3},{5,4},{6,5},{7,6},{8,7},{9,8},{10,9},{11,1... | collective-permute-start | bytes 221192 | tf_op jit(solution)/shard_map/ppermute | solution.py:22
  81.6 0.3 fusion.130
  81.9 1.6 %collective-permute-done.9 = f32[3,6,1,1024]{3,2,1,0:T(1,128)S(1)} collective-permute-done((f32[3,6,1,1024]{3,2,1,0:T(1,128)S(1)}, f32[3,6,1,1024]{3,2,1,0:T(1,128)S(1)}, u32[]{:S(2)}, u32[]{:S(2)}) %collective-permute-start.9) | collective-permute-done | bytes 73760 | tf_op jit(solution)/shard_map/ppermute | solution.py:22
  83.5 0.4 fusion.22
  84.0 3.4 %fusion.58 = (f32[4,16,1024]{2,1,0:T(8,128)S(1)}, f32[1,4,16,1024]{3,2,1,0:T(8,128)S(1)}) fusion(f32[3,4,16,1024]{3,2,1,0:T(8,128)S(1)} %fusion.22, s32[4,16,1024]{2,1,0:T(8,128)S(1)} %copy-done.1, f32[4,4,16,1024]{3,2,1,0:T(8,128)S(1)} %broadcast_multiply_fusion, f32[]{:T(128)} %bitcast.46, f32[]{:T(128)} %bitcast.38, f32[]{:T(128)} %bitcast.31, ...), kind=kLoop, calls=%fused_computation.110 | loop fusion | flops 1310720 | bytes 2228244 | tf_op jit(solution)/shard_map/add | solution.py:133
  87.4 4.7 %bitcast_dynamic-update-slice_fusion.1 = (f32[5,4,16,1024]{3,2,1,0:T(8,128)S(1)}, f32[4,16,1024]{2,1,0:T(8,128)S(1)}) fusion(f32[3,4,16,1024]{3,2,1,0:T(8,128)S(1)} %fusion.22, f32[4,4,16,1024]{3,2,1,0:T(8,128)S(1)} %broadcast_multiply_fusion, bf16[4,16,1024]{2,1,0:T(8,128)(2,1)S(1)} %copy-done.2, s32[4,16,1024]{2,1,0:T(8,128)S(1)} %copy-done.1, ...), kind=kLoop, calls=%fused_computation.133 | loop fusion | flops 2490367 | bytes 2621468
  92.1 1.9 %collective-permute-start.11 = (f32[3,1,16,1024]{3,2,1,0:T(8,128)S(1)}, f32[3,1,16,1024]{3,2,1,0:T(8,128)S(1)}, u32[]{:S(2)}, u32[]{:S(2)}) collective-permute-start(f32[3,1,16,1024]{3,2,1,0:T(8,128)S(1)} %get-tuple-element.21), channel_id=1, source_target_pairs={{64,0},{128,64},{192,128},{256,192},{320,256},{384,320},{448,384},... | collective-permute-start | bytes 589832 | tf_op jit(solution)/shard_map/ppermute | solution.py:22
  94.1 3.9 %collective-permute-start.12 = (f32[3,1,16,1024]{3,2,1,0:T(8,128)S(1)}, f32[3,1,16,1024]{3,2,1,0:T(8,128)S(1)}, u32[]{:S(2)}, u32[]{:S(2)}) collective-permute-start(f32[3,1,16,1024]{3,2,1,0:T(8,128)S(1)} %get-tuple-element.20), channel_id=1, source_target_pairs={{0,64},{64,128},{128,192},{192,256},{256,320},{320,384},{384,448},... | collective-permute-start | bytes 589832 | tf_op jit(solution)/shard_map/ppermute | solution.py:21
  98.0 1.7 %collective-permute-done.11 = f32[3,1,16,1024]{3,2,1,0:T(8,128)S(1)} collective-permute-done((f32[3,1,16,1024]{3,2,1,0:T(8,128)S(1)}, f32[3,1,16,1024]{3,2,1,0:T(8,128)S(1)}, u32[]{:S(2)}, u32[]{:S(2)}) %collective-permute-start.11) | collective-permute-done | bytes 196640 | tf_op jit(solution)/shard_map/ppermute | solution.py:22
  99.7 4.0 %collective-permute-done.12 = f32[3,1,16,1024]{3,2,1,0:T(8,128)S(1)} collective-permute-done((f32[3,1,16,1024]{3,2,1,0:T(8,128)S(1)}, f32[3,1,16,1024]{3,2,1,0:T(8,128)S(1)}, u32[]{:S(2)}, u32[]{:S(2)}) %collective-permute-start.12) | collective-permute-done | bytes 196640 | tf_op jit(solution)/shard_map/ppermute | solution.py:21
  103.9 6.8 %collective-permute-start.13 = (f32[3,6,1,1024]{3,2,1,0:T(1,128)S(1)}, f32[3,6,1,1024]{3,2,1,0:T(1,128)S(1)}, u32[]{:S(2)}, u32[]{:S(2)}) collective-permute-start(f32[3,6,1,1024]{3,2,1,0:T(1,128)S(1)} %get-tuple-element.11), channel_id=1, source_target_pairs={{1,0},{2,1},{3,2},{4,3},{5,4},{6,5},{7,6},{8,7},{9,8},{10,9},{11,1... | collective-permute-start | bytes 221192 | tf_op jit(solution)/shard_map/ppermute | solution.py:22
  110.6 1.9 %collective-permute-start.14 = (f32[3,6,1,1024]{3,2,1,0:T(1,128)S(1)}, f32[3,6,1,1024]{3,2,1,0:T(1,128)S(1)}, u32[]{:S(2)}, u32[]{:S(2)}) collective-permute-start(f32[3,6,1,1024]{3,2,1,0:T(1,128)S(1)} %get-tuple-element.12), channel_id=1, source_target_pairs={{0,1},{1,2},{2,3},{3,4},{4,5},{5,6},{6,7},{7,8},{8,9},{9,10},{10,1... | collective-permute-start | bytes 221192 | tf_op jit(solution)/shard_map/ppermute | solution.py:21
  112.6 0.3 fusion.128
  112.9 7.6 %collective-permute-done.14 = f32[3,6,1,1024]{3,2,1,0:T(1,128)S(1)} collective-permute-done((f32[3,6,1,1024]{3,2,1,0:T(1,128)S(1)}, f32[3,6,1,1024]{3,2,1,0:T(1,128)S(1)}, u32[]{:S(2)}, u32[]{:S(2)}) %collective-permute-start.14) | collective-permute-done | bytes 73760 | tf_op jit(solution)/shard_map/ppermute | solution.py:21
  120.5 0.4 fusion.16
  121.0 4.7 %fusion.54 = f32[5,4,16,1024]{3,2,1,0:T(8,128)S(1)} fusion(f32[5,4,16,1024]{3,2,1,0:T(8,128)S(1)} %get-tuple-element.5, f32[4,16,1024]{2,1,0:T(8,128)S(1)} %get-tuple-element.6, f32[3,4,16,1024]{3,2,1,0:T(8,128)S(1)} %fusion.16, f32[4,16,1024]{2,1,0:T(8,128)S(1)} %get-tuple-element.7, f32[3,4,16,1024]{3,2,1,0:T(8,128)S(1)} %fusion.22, ...), kind=kLoop, calls=%fused_computation.105 | loop fusion | flops 2686976 | bytes 2621468
  125.7 1.3 %fusion.46 = f32[5,4,16,1024]{3,2,1,0:T(8,128)S(1)} fusion(f32[5,4,16,1024]{3,2,1,0:T(8,128)S(1)} %fusion.54, f32[4,16,1024]{2,1,0:T(8,128)S(1)} %get-tuple-element.7, f32[3,4,16,1024]{3,2,1,0:T(8,128)S(1)} %fusion.16, f32[4,16,1024]{2,1,0:T(8,128)S(1)} %get-tuple-element.6, s32[4,16,1024]{2,1,0:T(8,128)S(1)} %copy-done.1, f32[]{:T(128)} %bitcast.46, f32[]{:T(128)} %bitcast.38), kind=kLoop, calls=%fused_computation.96 | loop fusion | flops 458752 | bytes 1310728
  127.0 2.1 %fusion.40 = f32[5,4,16,1024]{3,2,1,0:T(8,128)S(1)} fusion(f32[5,4,16,1024]{3,2,1,0:T(8,128)S(1)} %fusion.46, f32[3,4,16,1024]{3,2,1,0:T(8,128)S(1)} %fusion.16, f32[4,16,1024]{2,1,0:T(8,128)S(1)} %get-tuple-element.6, f32[3,4,16,1024]{3,2,1,0:T(8,128)S(1)} %fusion.22, f32[4,4,16,1024]{3,2,1,0:T(8,128)S(1)} %broadcast_multiply_fusion, ...), kind=kLoop, calls=%fused_computation.89 | loop fusion | flops 1507328 | bytes 1966092
  129.1 1.0 copy-done.10
  130.2 2.1 %bitcast_dynamic-update-slice_fusion = f32[5,4,16,1024]{3,2,1,0:T(8,128)} fusion(f32[5,4,16,1024]{3,2,1,0:T(8,128)} %copy-done.10, f32[4,16,1024]{2,1,0:T(8,128)S(1)} %get-tuple-element.6, s32[4,16,1024]{2,1,0:T(8,128)S(1)} %copy-done.1, f32[4,4,16,1024]{3,2,1,0:T(8,128)S(1)} %broadcast_multiply_fusion, bf16[4,16,1024]{2,1,0:T(8,128)(2,1)S(1)} %copy-done.4, ...), kind=kLoop, calls=%fused_computation.132 | loop fusion | flops 1114112 | bytes 1442816 | tf_op jit(solution)/shard_map/stack | solution.py:144
  (60 shorter events, 1.1 us)
Async XLA Ops:
  0.0 20.9 %copy-start = (bf16[4,4,97]{2,1,0:T(4,128)(2,1)S(1)}, bf16[4,4,97]{2,1,0:T(4,128)(2,1)}, u32[]{:S(2)}) copy-start(bf16[4,4,97]{2,1,0:T(4,128)(2,1)} %param.14) | copy-start | bytes 9316
  1.1 40.3 %collective-permute-start.2 = (bf16[4,16,1024]{2,1,0:T(8,128)(2,1)S(1)}, bf16[4,16,1024]{2,1,0:T(8,128)(2,1)}, u32[]{:S(2)}, u32[]{:S(2)}) collective-permute-start(bf16[4,16,1024]{2,1,0:T(8,128)(2,1)S(1)} %convert_multiply_fusion.1), channel_id=1, source_target_pairs={{0,1},{1,2},{2,3},{3,4},{4,5},{5,6},{6,7},{7,8},{8,9},{9,10},{10,1... | collective-permute-start | bytes 393224 | tf_op jit(solution)/shard_map/ppermute | solution.py:30
  3.0 42.0 %collective-permute-start.1 = (bf16[4,16,1024]{2,1,0:T(8,128)(2,1)S(1)}, bf16[4,16,1024]{2,1,0:T(8,128)(2,1)}, u32[]{:S(2)}, u32[]{:S(2)}) collective-permute-start(bf16[4,16,1024]{2,1,0:T(8,128)(2,1)S(1)} %convert_multiply_fusion.1), channel_id=1, source_target_pairs={{0,2},{1,3},{2,4},{3,5},{4,6},{5,7},{6,8},{7,9},{8,10},{9,11},{10,... | collective-permute-start | bytes 393224 | tf_op jit(solution)/shard_map/ppermute | solution.py:30
  6.5 41.9 %collective-permute-start = (bf16[4,16,1024]{2,1,0:T(8,128)(2,1)S(1)}, bf16[4,16,1024]{2,1,0:T(8,128)(2,1)}, u32[]{:S(2)}, u32[]{:S(2)}) collective-permute-start(bf16[4,16,1024]{2,1,0:T(8,128)(2,1)S(1)} %convert_multiply_fusion.1), channel_id=1, source_target_pairs={{0,3},{1,4},{2,5},{3,6},{4,7},{5,8},{6,9},{7,10},{8,11},{9,12},{10... | collective-permute-start | bytes 393224 | tf_op jit(solution)/shard_map/ppermute | solution.py:30
  11.0 38.7 %collective-permute-start.6 = (bf16[4,16,1024]{2,1,0:T(8,128)(2,1)S(1)}, bf16[4,16,1024]{2,1,0:T(8,128)(2,1)S(1)}, u32[]{:S(2)}, u32[]{:S(2)}) collective-permute-start(bf16[4,16,1024]{2,1,0:T(8,128)(2,1)S(1)} %convert_multiply_fusion.1), channel_id=1, source_target_pairs={{4,0},{5,1},{6,2},{7,3},{8,4},{9,5},{10,6},{11,7},{12,8},{13,9},{1... | collective-permute-start | bytes 393224 | tf_op jit(solution)/shard_map/ppermute | solution.py:30
  17.4 32.5 %collective-permute-start.5 = (bf16[4,16,1024]{2,1,0:T(8,128)(2,1)S(1)}, bf16[4,16,1024]{2,1,0:T(8,128)(2,1)S(1)}, u32[]{:S(2)}, u32[]{:S(2)}) collective-permute-start(bf16[4,16,1024]{2,1,0:T(8,128)(2,1)S(1)} %convert_multiply_fusion.1), channel_id=1, source_target_pairs={{3,0},{4,1},{5,2},{6,3},{7,4},{8,5},{9,6},{10,7},{11,8},{12,9},{13... | collective-permute-start | bytes 393224 | tf_op jit(solution)/shard_map/ppermute | solution.py:30
  24.5 6.1 %copy-start.13 = (bf16[4,4,97]{2,1,0:T(4,128)(2,1)S(1)}, bf16[4,4,97]{2,1,0:T(4,128)(2,1)}, u32[]{:S(2)}) copy-start(bf16[4,4,97]{2,1,0:T(4,128)(2,1)} %param.15) | copy-start | bytes 9316
  33.6 1.6 %slice-start = ((bf16[4,4,65536]{2,1,0:T(4,128)(2,1)}), bf16[4,4,65408]{2,1,0:T(4,128)(2,1)S(1)}, s32[]{:S(2)}) async-start(bf16[4,4,65536]{2,1,0:T(4,128)(2,1)} %tile.10), calls=%async_computation | async-start | bytes 4186112 | tf_op jit(solution)/shard_map/vmap(vmap())/slice | solution.py:45
  39.8 7.4 %copy-start.9 = (bf16[4,16,16,4]{2,3,1,0:T(4,128)(2,1)S(1)}, bf16[4,16,16,4]{2,3,1,0:T(4,128)(2,1)}, u32[]{:S(2)}) copy-start(bf16[4,16,16,4]{2,3,1,0:T(4,128)(2,1)} %fusion.26) | copy-start | bytes 24580
  39.8 8.6 %copy-start.5 = (bf16[4,16,16,4]{2,3,1,0:T(4,128)(2,1)S(1)}, bf16[4,16,16,4]{2,3,1,0:T(4,128)(2,1)}, u32[]{:S(2)}) copy-start(bf16[4,16,16,4]{2,3,1,0:T(4,128)(2,1)} %fusion.25) | copy-start | bytes 24580
  41.4 8.9 %collective-permute-start.4 = (bf16[4,16,1024]{2,1,0:T(8,128)(2,1)S(1)}, bf16[4,16,1024]{2,1,0:T(8,128)(2,1)S(1)}, u32[]{:S(2)}, u32[]{:S(2)}) collective-permute-start(bf16[4,16,1024]{2,1,0:T(8,128)(2,1)S(1)} %convert_multiply_fusion.1), channel_id=1, source_target_pairs={{2,0},{3,1},{4,2},{5,3},{6,4},{7,5},{8,6},{9,7},{10,8},{11,9},{12,... | collective-permute-start | bytes 393224 | tf_op jit(solution)/shard_map/ppermute | solution.py:30
  45.0 5.8 %collective-permute-start.3 = (bf16[4,16,1024]{2,1,0:T(8,128)(2,1)S(1)}, bf16[4,16,1024]{2,1,0:T(8,128)(2,1)S(1)}, u32[]{:S(2)}, u32[]{:S(2)}) collective-permute-start(bf16[4,16,1024]{2,1,0:T(8,128)(2,1)S(1)} %convert_multiply_fusion.1), channel_id=1, source_target_pairs={{1,0},{2,1},{3,2},{4,3},{5,4},{6,5},{7,6},{8,7},{9,8},{10,9},{11,1... | collective-permute-start | bytes 393224 | tf_op jit(solution)/shard_map/ppermute | solution.py:30
  48.4 1.3 copy-start.8
  48.4 1.6 %copy-start.7 = (bf16[4,16,16,4]{2,3,1,0:T(4,128)(2,1)S(1)}, bf16[4,16,16,4]{2,3,1,0:T(4,128)(2,1)}, u32[]{:S(2)}) copy-start(bf16[4,16,16,4]{2,3,1,0:T(4,128)(2,1)} %fusion.31) | copy-start | bytes 24580
  49.6 0.8 copy-start.6
  51.6 1.6 %copy-start.3 = (bf16[4,4,128,511]{3,2,1,0:T(8,128)(2,1)S(1)}, bf16[4,4,128,511]{3,2,1,0:T(8,128)(2,1)}, u32[]{:S(2)}) copy-start(bf16[4,4,128,511]{3,2,1,0:T(8,128)(2,1)} %reshape.264) | copy-start | bytes 6279172
  54.0 0.7 copy-start.14
  54.7 0.9 copy-start.1
  54.7 1.0 copy-start.2
  55.8 6.4 %copy-start.12 = (f32[3]{0:T(128)S(1)}, f32[3]{0:T(128)}, u32[]{:S(2)}) copy-start(f32[3]{0:T(128)} %param.18) | copy-start | bytes 40
  55.8 7.0 %copy-start.11 = (f32[5]{0:T(128)S(1)}, f32[5]{0:T(128)}, u32[]{:S(2)}) copy-start(f32[5]{0:T(128)} %param.19) | copy-start | bytes 64
  55.9 9.5 %collective-permute-start.7 = (f32[3,1,16,1024]{3,2,1,0:T(8,128)S(1)}, f32[3,1,16,1024]{3,2,1,0:T(8,128)S(1)}, u32[]{:S(2)}, u32[]{:S(2)}) collective-permute-start(f32[3,1,16,1024]{3,2,1,0:T(8,128)S(1)} %get-tuple-element.25), channel_id=1, source_target_pairs={{64,0},{128,64},{192,128},{256,192},{320,256},{384,320},{448,384},... | collective-permute-start | bytes 589832 | tf_op jit(solution)/shard_map/ppermute | solution.py:22
  60.2 11.4 %collective-permute-start.8 = (f32[3,1,16,1024]{3,2,1,0:T(8,128)S(1)}, f32[3,1,16,1024]{3,2,1,0:T(8,128)S(1)}, u32[]{:S(2)}, u32[]{:S(2)}) collective-permute-start(f32[3,1,16,1024]{3,2,1,0:T(8,128)S(1)} %get-tuple-element.24), channel_id=1, source_target_pairs={{0,64},{64,128},{128,192},{192,256},{256,320},{320,384},{384,448},... | collective-permute-start | bytes 589832 | tf_op jit(solution)/shard_map/ppermute | solution.py:21
  71.8 10.1 %collective-permute-start.10 = (f32[3,6,1,1024]{3,2,1,0:T(1,128)S(1)}, f32[3,6,1,1024]{3,2,1,0:T(1,128)S(1)}, u32[]{:S(2)}, u32[]{:S(2)}) collective-permute-start(f32[3,6,1,1024]{3,2,1,0:T(1,128)S(1)} %get-tuple-element.14), channel_id=1, source_target_pairs={{0,1},{1,2},{2,3},{3,4},{4,5},{5,6},{6,7},{7,8},{8,9},{9,10},{10,1... | collective-permute-start | bytes 221192 | tf_op jit(solution)/shard_map/ppermute | solution.py:21
  73.7 9.8 %collective-permute-start.9 = (f32[3,6,1,1024]{3,2,1,0:T(1,128)S(1)}, f32[3,6,1,1024]{3,2,1,0:T(1,128)S(1)}, u32[]{:S(2)}, u32[]{:S(2)}) collective-permute-start(f32[3,6,1,1024]{3,2,1,0:T(1,128)S(1)} %get-tuple-element.13), channel_id=1, source_target_pairs={{1,0},{2,1},{3,2},{4,3},{5,4},{6,5},{7,6},{8,7},{9,8},{10,9},{11,1... | collective-permute-start | bytes 221192 | tf_op jit(solution)/shard_map/ppermute | solution.py:22
  84.0 3.4 %copy-start.4 = (bf16[4,16,1024]{2,1,0:T(8,128)(2,1)S(1)}, bf16[4,16,1024]{2,1,0:T(8,128)(2,1)}, u32[]{:S(2)}) copy-start(bf16[4,16,1024]{2,1,0:T(8,128)(2,1)} %param.13) | copy-start | bytes 393220
  92.1 7.6 %collective-permute-start.11 = (f32[3,1,16,1024]{3,2,1,0:T(8,128)S(1)}, f32[3,1,16,1024]{3,2,1,0:T(8,128)S(1)}, u32[]{:S(2)}, u32[]{:S(2)}) collective-permute-start(f32[3,1,16,1024]{3,2,1,0:T(8,128)S(1)} %get-tuple-element.21), channel_id=1, source_target_pairs={{64,0},{128,64},{192,128},{256,192},{320,256},{384,320},{448,384},... | collective-permute-start | bytes 589832 | tf_op jit(solution)/shard_map/ppermute | solution.py:22
  94.1 9.7 %collective-permute-start.12 = (f32[3,1,16,1024]{3,2,1,0:T(8,128)S(1)}, f32[3,1,16,1024]{3,2,1,0:T(8,128)S(1)}, u32[]{:S(2)}, u32[]{:S(2)}) collective-permute-start(f32[3,1,16,1024]{3,2,1,0:T(8,128)S(1)} %get-tuple-element.20), channel_id=1, source_target_pairs={{0,64},{64,128},{128,192},{192,256},{256,320},{320,384},{384,448},... | collective-permute-start | bytes 589832 | tf_op jit(solution)/shard_map/ppermute | solution.py:21
  103.9 9.0 %collective-permute-start.13 = (f32[3,6,1,1024]{3,2,1,0:T(1,128)S(1)}, f32[3,6,1,1024]{3,2,1,0:T(1,128)S(1)}, u32[]{:S(2)}, u32[]{:S(2)}) collective-permute-start(f32[3,6,1,1024]{3,2,1,0:T(1,128)S(1)} %get-tuple-element.11), channel_id=1, source_target_pairs={{1,0},{2,1},{3,2},{4,3},{5,4},{6,5},{7,6},{8,7},{9,8},{10,9},{11,1... | collective-permute-start | bytes 221192 | tf_op jit(solution)/shard_map/ppermute | solution.py:22
  110.6 9.9 %collective-permute-start.14 = (f32[3,6,1,1024]{3,2,1,0:T(1,128)S(1)}, f32[3,6,1,1024]{3,2,1,0:T(1,128)S(1)}, u32[]{:S(2)}, u32[]{:S(2)}) collective-permute-start(f32[3,6,1,1024]{3,2,1,0:T(1,128)S(1)} %get-tuple-element.12), channel_id=1, source_target_pairs={{0,1},{1,2},{2,3},{3,4},{4,5},{5,6},{6,7},{7,8},{8,9},{9,10},{10,1... | collective-permute-start | bytes 221192 | tf_op jit(solution)/shard_map/ppermute | solution.py:21
  129.1 1.1 copy-start.10
where the time goes:
time: 133 us; the launch traced here: 132 us
  starting transfers between devices  53.5 us (40%)
  waiting for transfers between devices  23.3 us (18%)
  other arithmetic  22.2 us (17%)
  matrix products  16.6 us (12%)
  local copies, waits for them, and re-layouts  16.1 us (12%)
    ppermute x7, starting transfers between devices, passed_along(): return lax.ppermute(block, axis, route)  22.9 us
    ppermute x4, starting transfers between devices, padded_2(): after = lax.ppermute(leading, axis, down)  20.9 us
    ppermute x4, waiting for transfers between devices, padded_2(): before = lax.ppermute(last, axis, up)  17.9 us
    unnamed x4, other arithmetic  12.8 us
    dot_general x8, matrix products, body(): jnp.einsum('zxwi,szi->szxw', selector, taps_across, preferred_element_typ...  10.8 us
    ppermute x4, starting transfers between devices, padded_2(): before = lax.ppermute(last, axis, up)  9.68 us
    ppermute x4, waiting for transfers between devices, padded_2(): after = lax.ppermute(leading, axis, down)  5.32 us
    dot_general x8, matrix products, body(): jnp.einsum('szxw,zwy->szxy', matrix_x, block_piece, preferred_element_typ...  4.99 us
  transfers between devices with their start and end apart: 15, of which 6 were waited for; matrix products, arithmetic and copies ran while one was open for 20% of the time, Pallas kernels for 0%

commit v1 on v0

v1 whole, which is shorter than its diff:
```python
import jax
import jax.numpy as jnp
from jax import lax
from jax.experimental import pallas as pl
from jax.experimental.pallas import tpu as pltpu
from jax.sharding import PartitionSpec as P

TAPS = 97
HALF = 48
LAYERS = 4
ROWS = 16
LENGTH = 1024
GROUP = 24
WINDOW = 176
LATS = 64
DEPTHS = 8
F32 = jnp.float32
BF16 = jnp.bfloat16
MEMORY = 32 * 1024 * 1024


def call(kernel, outs, args, scalars=0, scratch=(), flops=1000000, size=2000000):
    specs = [pl.BlockSpec(memory_space=pltpu.SMEM)] * scalars
    specs += [pl.BlockSpec(memory_space=pltpu.VMEM)] * (len(args) - scalars)
    return pl.pallas_call(
        kernel,
        out_shape=outs,
        in_specs=specs,
        out_specs=jax.tree.map(lambda _: pl.BlockSpec(memory_space=pltpu.VMEM), outs),
        scratch_shapes=list(scratch),
        compiler_params=pltpu.CompilerParams(vmem_limit_bytes=MEMORY),
        cost_estimate=pl.CostEstimate(flops=flops, bytes_accessed=size, transcendentals=0),
    )(*args)


def shape(dims, dtype):
    return jax.ShapeDtypeStruct(dims, dtype)


def source_kernel(mask, power, pairs, clusters, packed, corner):
    sub = lax.broadcasted_iota(jnp.int32, (8, LENGTH), 0)
    edges = []
    firsts = []
    for z in range(LAYERS):
        silicon = mask[z].astype(F32)
        src = silicon * power[z].astype(F32)
        packed[pl.ds(ROWS * z, ROWS), :] = src.astype(BF16)
        pair = silicon * pairs[z].astype(F32)
        cluster = clusters[z].astype(F32)
        edge = jnp.where(sub < 2, pair[:8], jnp.where(sub >= 6, pair[8:], 0.0))
        edge = jnp.where(sub == 2, pltpu.roll(cluster[:8], 2, 0), edge)
        edge = jnp.where(sub == 5, pltpu.roll(cluster[8:], 6, 0), edge)
        edges.append(edge)
        first = jnp.where(sub < 2, src[:8], 0.0)
        firsts.append(first if z % 2 == 0 else pltpu.roll(first, 4, 0))
    packed[pl.ds(64, 16), :] = jnp.concatenate(edges[:2], 0).astype(BF16)
    packed[pl.ds(80, 16), :] = jnp.concatenate(edges[2:], 0).astype(BF16)
    corner[...] = jnp.concatenate([firsts[0] + firsts[1], firsts[2] + firsts[3]], 0).astype(BF16)


def along_matrix(line):
    wide = jnp.concatenate([line, jnp.zeros_like(line)], 1)
    wide = jnp.broadcast_to(wide, (128, 256))
    return pltpu.roll(wide, 16, 1, stride=1, stride_axis=0).astype(BF16)


def band_kernel(offset, across, along, across_bands, along_bands):
    lane = lax.broadcasted_iota(jnp.int32, (GROUP, 256), 1)
    for z in range(LAYERS):
        for s in range(4):
            line = across[pl.ds(s * LAYERS + z, 1), :]
            wide = jnp.concatenate([line, jnp.zeros_like(line)], 1)
            wide = jnp.broadcast_to(wide, (32, 256))
            band = pltpu.roll(wide, 0, 1, stride=1, stride_axis=0)
            band = pltpu.roll(band, offset[z] - 8, 1)
            group = lax.broadcasted_iota(jnp.int32, (8, 256), 0)
            last = jnp.where(group < 2, band[24:], band[:8])
            band = jnp.concatenate([band[8:24], last], 0)
            tail = pltpu.roll(band, 4 * z, 1) if z else band
            tail = jnp.where((lane >= 160 + 4 * z) & (lane < 162 + 4 * z), tail, 0.0)
            band = jnp.where(lane < 160, band, tail)
            across_bands[z, pl.ds(s * GROUP, GROUP), :] = band
            along_bands[s * LAYERS + z] = along_matrix(along[pl.ds(s * LAYERS + z, 1), :])


def pair_edge(core, z, near, mine):
    following = jnp.where(core == 0, mine[1, 0], near[1, 0])
    previous = jnp.where(core == 0, near[0, 1], mine[0, 1])
    return following, previous


def edge_of(core, z, near, mine):
    at = pl.ds(64 + 16 * (z // 2), 16)
    half = slice(8 * (z % 2), 8 * (z % 2) + 8)
    following = jnp.where(core == 0, mine[1, at, :].astype(F32), near[1, 0, at, :].astype(F32))[half]
    previous = jnp.where(core == 0, near[0, 1, at, :].astype(F32), mine[0, at, :].astype(F32))[half]
    return following, previous


def pair_edges(following, previous):
    sub = lax.broadcasted_iota(jnp.int32, (8, LENGTH), 0)
    return jnp.where(sub < 2, following, jnp.where(sub >= 6, previous, 0.0))


def cluster_edges(following, previous):
    sub = lax.broadcasted_iota(jnp.int32, (8, LENGTH), 0)
    following = pltpu.roll(following, 6, 0)
    previous = pltpu.roll(previous, 2, 0)
    return jnp.where(sub == 0, following, jnp.where(sub == 7, previous, 0.0))


def across_kernel(core_ref, mine, near, far, corner, bands, mask, pairs, clusters, lines, spread, down, up, window):
    core = core_ref[0]
    for z in range(LAYERS):
        at = pl.ds(ROWS * z, ROWS)
        parts = [far[0, 0, at, :], far[0, 1, at, :], near[0, 0, at, :], near[0, 1, at, :]]
        parts += [mine[0, at, :], mine[1, at, :]]
        parts += [near[1, 0, at, :], near[1, 1, at, :], far[1, 0, at, :], far[1, 1, at, :], corner[...]]
        for i, part in enumerate(parts):
            window[z, pl.ds(16 * i, 16), :] = part
        band = bands[z].astype(BF16)[:, :WINDOW]
        x = jnp.dot(band, window[z], preferred_element_type=F32)
        spread[z] = x.astype(BF16)
        out = down if z < 2 else up
        pair = mask[z].astype(F32) * pairs[z].astype(F32)

        def own(s):
            return x[GROUP * s : GROUP * s + ROWS].astype(BF16)

        def rim(s):
            return x[GROUP * s + ROWS : GROUP * s + GROUP]

        if z in (0, 3):
            following, previous = edge_of(core, z, near, mine)
            out[pl.ds(0, 16), :] = own(1)
            out[pl.ds(16, 16), :] = own(2)
            out[pl.ds(32, 16), :] = own(0)
            out[pl.ds(48, 16), :] = own(3)
            out[pl.ds(64, 16), :] = pair.astype(BF16)
            out[pl.ds(80, 16), :] = clusters[z]
            out[pl.ds(96, 16), :] = jnp.concatenate([rim(1), rim(2)], 0).astype(BF16)
            rows = lines[0 if z == 0 else 1].astype(F32)
            out[pl.ds(112, 16), :] = jnp.concatenate([pair_edges(following, previous), rows], 0).astype(BF16)
        else:
            out[pl.ds(128, 16), :] = own(1)
            out[pl.ds(144, 16), :] = own(2)
            out[pl.ds(160, 16), :] = pair.astype(BF16)


def along_sum(x, matrix):
    rows = x.shape[0]
    zeros = jnp.zeros((rows, 64), F32)
    wide = jnp.concatenate([zeros, x, zeros], 1)
    blocks = LENGTH // 128
    stacked = jnp.concatenate([wide[:, 128 * b : 128 * b + 256] for b in range(blocks)], 0).astype(BF16)
    y = lax.dot_general(stacked, matrix, (((1,), (1,)), ((), ())), preferred_element_type=F32)
    return jnp.concatenate([y[rows * b : rows * (b + 1)] for b in range(blocks)], 1)


def along_kernel(core_ref, doses, spread, matrices, mask, pairs, clusters, near, mine, fields):
    core = core_ref[0]
    for z in range(LAYERS):
        x = spread[z].astype(F32)
        following, previous = edge_of(core, z, near, mine)
        pair_rim = pair_edges(following, previous)
        silicon = jnp.concatenate([mask[z].astype(F32), (pair_rim > 0.0).astype(F32)], 0)
        pair = silicon * jnp.concatenate([pairs[z].astype(F32), pair_rim], 0)
        before = jnp.concatenate([clusters[z].astype(F32), cluster_edges(following, previous)], 0)
        sums = []
        for s in range(4):
            y = along_sum(x[GROUP * s : GROUP * (s + 1)], matrices[s * LAYERS + z])
            sums.append(doses[s, z] * y)
        fields[0, z] = silicon * sums[0]
        fields[1, z] = silicon * sums[1]
        fields[2, z] = silicon * sums[2]
        fields[3, z] = pair
        fields[4, z] = silicon * (before + sums[3])


def laplace(center, below, above, rows):
    total = center.shape[0]
    lane = lax.broadcasted_iota(jnp.int32, (rows, LENGTH), 1)
    inner = center[:rows]
    near = above[:rows] + below[:rows]
    near = near + pltpu.roll(center, total - 1, 0)[:rows] + pltpu.roll(center, 1, 0)[:rows]
    near = near + jnp.where(lane == LENGTH - 1, 0.0, pltpu.roll(inner, LENGTH - 1, 1))
    near = near + jnp.where(lane == 0, 0.0, pltpu.roll(inner, 1, 1))
    return near - 6.0 * inner


def react_kernel(spreads, rates, fields, below, above, result, mobile, still, late):
    for side, payload in ((0, below), (1, above)):
        near, far = (1, 0) if side == 0 else (6, 7)
        rows = payload[pl.ds(112, 16), :].astype(F32)
        pair_rim, lines = rows[:8], rows[8:]

        def implanted(i, x):
            line = lines[i : i + 1]
            dose = line[:, 128:129] + line[:, 256:257] + line[:, 384:385]
            return dose * along_sum(x, along_matrix(line[:, :128]))

        rims = payload[pl.ds(96, 16), :].astype(F32)
        pair = jnp.concatenate([payload[pl.ds(64, 16), :].astype(F32), pair_rim], 0)
        silicon = (pair > 0.0).astype(F32)
        mobile[2, near] = pair
        mobile[0, near] = silicon * implanted(0, jnp.concatenate([payload[pl.ds(0, 16), :].astype(F32), rims[:8]], 0))
        mobile[1, near] = silicon * implanted(1, jnp.concatenate([payload[pl.ds(16, 16), :].astype(F32), rims[8:]], 0))
        silicon = silicon[:ROWS]
        at = 0 if side == 0 else 5
        still[0, at, :ROWS] = silicon * implanted(2, payload[pl.ds(32, 16), :].astype(F32))
        sums = implanted(3, payload[pl.ds(48, 16), :].astype(F32))
        still[1, at, :ROWS] = silicon * (payload[pl.ds(80, 16), :].astype(F32) + sums)
        pair = payload[pl.ds(160, 16), :].astype(F32)
        silicon = (pair > 0.0).astype(F32)
        mobile[2, far, :ROWS] = pair
        mobile[0, far, :ROWS] = silicon * implanted(4, payload[pl.ds(128, 16), :].astype(F32))
        mobile[1, far, :ROWS] = silicon * implanted(5, payload[pl.ds(144, 16), :].astype(F32))
    for z in range(LAYERS):
        mobile[0, z + 2] = fields[1, z]
        mobile[1, z + 2] = fields[2, z]
        mobile[2, z + 2] = fields[3, z]
        still[0, z + 1] = fields[0, z]
        still[1, z + 1] = fields[4, z]

    def substep(silicon, centers, belows, aboves, arsenic, clusters, rows):
        inter, vacancy, pair = (c[:rows] for c in centers)
        laplaces = [laplace(c, b, a, rows) for c, b, a in zip(centers, belows, aboves)]
        recombine = rates[0] * inter * vacancy
        pairing = rates[1] * arsenic * inter - rates[2] * pair
        clustering = rates[3] * inter * inter - rates[4] * clusters
        new_inter = inter + silicon * (spreads[0] * laplaces[0] - recombine - pairing - 2.0 * clustering)
        new_vacancy = vacancy + silicon * (spreads[1] * laplaces[1] - recombine)
        new_arsenic = arsenic - silicon * pairing
        new_pair = pair + silicon * (spreads[2] * laplaces[2] + pairing)
        new_clusters = clusters + silicon * clustering
        return new_arsenic, new_inter, new_vacancy, new_pair, new_clusters

    for layer in range(1, 7):
        rows = ROWS if layer in (1, 6) else GROUP
        silicon = (mobile[2, layer, :rows] > 0.0).astype(F32)
        centers = [mobile[f, layer] for f in range(3)]
        belows = [mobile[f, layer - 1, :rows] for f in range(3)]
        aboves = [mobile[f, layer + 1, :rows] for f in range(3)]
        arsenic, clusters = still[0, layer - 1, :rows], still[1, layer - 1, :rows]
        new = substep(silicon, centers, belows, aboves, arsenic, clusters, rows)
        for f in range(3):
            late[f, layer - 1, :rows] = new[f + 1]
        still[0, layer - 1, :rows] = new[0]
        still[1, layer - 1, :rows] = new[4]
    for z in range(LAYERS):
        silicon = (mobile[2, z + 2, :ROWS] > 0.0).astype(F32)
        centers = [late[f, z + 1] for f in range(3)]
        belows = [late[f, z, :ROWS] for f in range(3)]
        aboves = [late[f, z + 2, :ROWS] for f in range(3)]
        new = substep(silicon, centers, belows, aboves, still[0, z + 1, :ROWS], still[1, z + 1, :ROWS], ROWS)
        for f in range(5):
            result[f, z] = new[f]


def moved(array, axis, size, source):
    route = [(source(i), i) for i in range(size) if source(i) is not None and 0 <= source(i) < size]
    return lax.ppermute(array, axis, route)


def lanes(core0, core1):
    return lambda i: i + core0 if i % 2 == 0 else (None if core1 is None else i + core1)


def split3(values):
    high = values.astype(BF16)
    rest = values - high.astype(F32)
    middle = rest.astype(BF16)
    return high, middle, (rest - middle.astype(F32)).astype(BF16)


def body(
    fin_mask,
    stopping_power,
    pairs_before,
    clusters_before,
    taps_across,
    taps_along,
    tilt_shift,
    layer_doses,
    diffusivity,
    reaction_rates,
):
    core = lax.rem(lax.axis_index("lat"), 2)
    core_ref = core.reshape(1)
    couples = [[2 * i, 2 * i + 1] for i in range(LATS // 2)]

    packed, first = call(
        source_kernel,
        (shape((96, LENGTH), BF16), shape((16, LENGTH), BF16)),
        (fin_mask, stopping_power, pairs_before, clusters_before),
    )
    corner = moved(first, "lat", LATS, lambda i: None if i % 2 == 0 else i + 5)
    mine = lax.all_gather(packed, "lat", axis_index_groups=couples)
    near = moved(mine, "lat", LATS, lanes(-2, 2))
    far = moved(mine[:, :64], "lat", LATS, lanes(-4, 4))

    wide = ((0, 0), (0, 0), (0, 128 - TAPS))
    across = jnp.pad(taps_across.astype(F32), wide).reshape(16, 128)
    along_taps = jnp.pad(taps_along, wide)
    along = along_taps.astype(F32).reshape(16, 128)
    offset = ROWS + ROWS * core + tilt_shift
    across_bands, along_bands = call(
        band_kernel,
        (shape((LAYERS, 4 * GROUP, 256), F32), shape((16, 128, 256), BF16)),
        (offset, across, along),
        scalars=1,
    )
    pieces = [along_taps] + [jnp.broadcast_to(d[:, :, None], (4, LAYERS, 128)) for d in split3(layer_doses)]
    table = jnp.concatenate(pieces, 2)
    order = ((1, 0), (2, 0), (0, 0), (3, 0), (1, 1), (2, 1), (1, 1), (2, 1))
    lines = jnp.stack(
        [
            jnp.stack([table[s, far_layer] for s, far_layer in order]),
            jnp.stack([table[s, 3 - far_layer] for s, far_layer in order]),
        ]
    )
    lines = jnp.pad(lines, ((0, 0), (0, 0), (0, 512)))

    near = lax.all_gather(near, "lat", axis_index_groups=couples)
    far = lax.all_gather(far, "lat", axis_index_groups=couples)
    spread, down, up = call(
        across_kernel,
        (shape((LAYERS, 4 * GROUP, LENGTH), BF16), shape((176, LENGTH), BF16), shape((176, LENGTH), BF16)),
        (core_ref, mine, near, far, corner, across_bands, fin_mask, pairs_before, clusters_before, lines),
        scalars=1,
        scratch=[pltpu.VMEM((LAYERS, WINDOW, LENGTH), BF16)],
    )
    below = moved(up, "depth", DEPTHS, lambda i: i - 1)
    above = moved(down, "depth", DEPTHS, lambda i: i + 1)
    fields = call(
        along_kernel,
        shape((5, LAYERS, GROUP, LENGTH), F32),
        (core_ref, layer_doses, spread, along_bands, fin_mask, pairs_before, clusters_before, near, mine),
        scalars=2,
    )
    return call(
        react_kernel,
        shape((5, LAYERS, ROWS, LENGTH), F32),
        (diffusivity, reaction_rates, fields, below, above),
        scalars=2,
        scratch=[
            pltpu.VMEM((3, 8, GROUP, LENGTH), F32),
            pltpu.VMEM((2, 6, GROUP, LENGTH), F32),
            pltpu.VMEM((3, 6, GROUP, LENGTH), F32),
        ],
    )


def solution(mesh):
    return jax.shard_map(
        body,
        mesh=mesh,
        in_specs=(
            P("depth", "lat", None),
            P("depth", "lat", None),
            P("depth", "lat", None),
            P("depth", "lat", None),
            P(None, "depth", None),
            P(None, "depth", None),
            P("depth"),
            P(None, "depth"),
            P(),
            P(),
        ),
        out_specs=P(None, "depth", "lat", None),
        check_vma=False,
    )
```

time: 133 us -> 64.8 us (0.49)
  the two profiles are of different devices: /device:TPU:320 before, /device:TPU:270 now
where the time goes in v1:
time: 64.8 us; the launch traced here: 64.4 us
  waiting for transfers between devices  26.2 us (40%)
  starting transfers between devices  16.7 us (26%)
  Pallas kernels  8.33 us (13%)
  blocking collectives  6.75 us (10%)
  local copies, waits for them, and re-layouts  5.42 us (8%)
  other arithmetic  0.79 us (1%)
    ppermute x5, waiting for transfers between devices, moved(): return lax.ppermute(array, axis, route)  26.2 us
    ppermute x5, starting transfers between devices, moved(): return lax.ppermute(array, axis, route)  16.7 us
    pallas_call x5, Pallas kernels, call(): pl.pallas_call(kernel, out_shape=outs, in_specs=specs, out_specs=jax.tree...  8.33 us
    unnamed x22, local copies, waits for them, and re-layouts  3.69 us
    all_gather x1, blocking collectives, body(): near = lax.all_gather(near, 'lat', axis_index_groups=couples)  2.49 us
    all_gather x1, blocking collectives, body(): far = lax.all_gather(far, 'lat', axis_index_groups=couples)  2.17 us
    all_gather x1, blocking collectives, body(): mine = lax.all_gather(packed, 'lat', axis_index_groups=couples)  2.09 us
  transfers between devices with their start and end apart: 5, of which 3 were waited for; matrix products, arithmetic and copies ran while one was open for 4% of the time, Pallas kernels for 6%

profile of v1, /device:TPU:270, one launch (start us, length us, event | category | flops | bytes accessed | tf_op | source)
XLA Modules:
  0.0 64.4 jit_solution(1834176641502197684)
XLA Ops:
  0.0 0.0 copy-start
  0.0 0.9 %copy-done = s32[4,16,1024]{2,1,0:T(8,128)S(1)} copy-done((s32[4,16,1024]{2,1,0:T(8,128)S(1)}, s32[4,16,1024]{2,1,0:T(8,128)}, u32[]{:S(2)}) %copy-start) | copy-done | bytes 262168
  1.0 0.0 copy-start.2
  1.0 0.9 %copy-done.2 = bf16[4,16,1024]{2,1,0:T(8,128)(2,1)S(1)} copy-done((bf16[4,16,1024]{2,1,0:T(8,128)(2,1)S(1)}, bf16[4,16,1024]{2,1,0:T(8,128)(2,1)}, u32[]{:S(2)}) %copy-start.2) | copy-done | bytes 131096
  1.9 0.0 copy-start.4
  1.9 0.9 %copy-done.4 = bf16[4,16,1024]{2,1,0:T(8,128)(2,1)S(1)} copy-done((bf16[4,16,1024]{2,1,0:T(8,128)(2,1)S(1)}, bf16[4,16,1024]{2,1,0:T(8,128)(2,1)}, u32[]{:S(2)}) %copy-start.4) | copy-done | bytes 131096
  2.8 0.0 copy-start.6
  2.8 0.9 %copy-done.6 = bf16[4,16,1024]{2,1,0:T(8,128)(2,1)S(1)} copy-done((bf16[4,16,1024]{2,1,0:T(8,128)(2,1)S(1)}, bf16[4,16,1024]{2,1,0:T(8,128)(2,1)}, u32[]{:S(2)}) %copy-start.6) | copy-done | bytes 131096
  3.7 0.0 copy-start.10
  3.7 0.0 copy-start.1
  3.7 0.0 copy-start.3
  3.7 0.0 copy-start.5
  3.7 0.1 shard_map.100
  3.8 3.8 %collective-permute-start.2 = (bf16[16,1024]{1,0:T(8,128)(2,1)S(1)}, bf16[16,1024]{1,0:T(8,128)(2,1)S(1)}, u32[]{:S(2)}, u32[]{:S(2)}) collective-permute-start(bf16[16,1024]{1,0:T(8,128)(2,1)S(1)} %get-tuple-element.13), channel_id=1, source_target_pairs={{6,1},{8,3},{10,5},{12,7},{14,9},{16,11},{18,13},{20,15},{22,17},{... | collective-permute-start | bytes 98312 | tf_op jit(solution)/shard_map/ppermute | solution.py:262
  7.6 2.1 %all-gather = bf16[192,1024]{1,0:T(8,128)(2,1)S(1)} all-gather(bf16[96,1024]{1,0:T(8,128)(2,1)S(1)} %get-tuple-element.12), channel_id=2, replica_groups={{0,1},{2,3},{4,5},{6,7},{8,9},{10,11},{12,13},{14,15},{16,17},{18,19},{..., dimensions={0}, use_global_device_ids=true | all-gather | bytes 589824 | tf_op jit(solution)/shard_map/all_gather | solution.py:298
  9.7 2.6 %collective-permute-start = (bf16[2,96,1024]{2,1,0:T(8,128)(2,1)S(1)}, bf16[2,96,1024]{2,1,0:T(8,128)(2,1)S(1)}, u32[]{:S(2)}, u32[]{:S(2)}) collective-permute-start(bf16[2,96,1024]{2,1,0:T(8,128)(2,1)S(1)} %bitcast.36), channel_id=1, source_target_pairs={{3,1},{0,2},{5,3},{2,4},{7,5},{4,6},{9,7},{6,8},{11,9},{8,10},{13,... | collective-permute-start | bytes 1179656 | tf_op jit(solution)/shard_map/ppermute | solution.py:262
  12.3 4.5 %collective-permute-start.1 = (bf16[2,64,1024]{2,1,0:T(8,128)(2,1)S(1)}, bf16[2,64,1024]{2,1,0:T(8,128)(2,1)S(1)}, u32[]{:S(2)}, u32[]{:S(2)}) collective-permute-start(bf16[2,64,1024]{2,1,0:T(8,128)(2,1)S(1)} %slice.56), channel_id=1, source_target_pairs={{5,1},{7,3},{0,4},{9,5},{2,6},{11,7},{4,8},{13,9},{6,10},{15,11},{... | collective-permute-start | bytes 786440 | tf_op jit(solution)/shard_map/ppermute | solution.py:262
  16.8 0.8 %fusion.4 = (bf16[4,4]{1,0:T(4,128)(2,1)S(1)}, bf16[4,4]{1,0:T(4,128)(2,1)S(1)}, bf16[4,4]{1,0:T(4,128)(2,1)S(1)}) fusion(f32[4,4]{1,0:T(4,128)} %doses.1), kind=kLoop, calls=%fused_computation.21 | loop fusion | flops 112 | bytes 160 | tf_op jit(solution)/shard_map/convert_element_type | solution.py:270
  17.6 0.7 %pad.14 = bf16[4,4,128]{2,1,0:T(4,128)(2,1)S(1)} pad(bf16[4,4,97]{2,1,0:T(4,128)(2,1)} %param.15, bf16[]{:T(256)} %constant.15.clone.1), padding=0_0x0_0x0_31 | pad | bytes 7202 | tf_op jit(solution)/shard_map/jit(_pad)/pad | solution.py:304
  18.3 0.7 %pad.13 = bf16[4,4,128]{2,1,0:T(4,128)(2,1)S(1)} pad(bf16[4,4,97]{2,1,0:T(4,128)(2,1)} %param.14, bf16[]{:T(256)} %constant.15.clone.1), padding=0_0x0_0x0_31 | pad | bytes 7202 | tf_op jit(solution)/shard_map/jit(_pad)/pad | solution.py:303
  19.0 0.1 broadcast_in_dim.6
  19.0 0.1 broadcast_in_dim.8
  19.1 0.1 broadcast_in_dim.7
  19.3 0.0 copy-done.10
  19.3 2.4 %shard_map.101 = (f32[4,96,256]{2,1,0:T(8,128)S(1)}, bf16[16,128,256]{2,1,0:T(8,128)(2,1)S(1)}) custom-call(s32[4]{0:T(128)S(1)} %broadcast_add_fusion.offset, f32[16,128]{1,0:T(8,128)S(1)} %convert.4.across, f32[16,128]{1,0:T(8,128)S(1)} %convert.5.along), custom_call_target="tpu_custom_call" | custom-call | flops 1000000 | bytes 2000000 | tf_op jit(solution)/shard_map/pallas_call | solution.py:25
  21.8 15.3 %collective-permute-done.1 = bf16[2,64,1024]{2,1,0:T(8,128)(2,1)S(1)} collective-permute-done((bf16[2,64,1024]{2,1,0:T(8,128)(2,1)S(1)}, bf16[2,64,1024]{2,1,0:T(8,128)(2,1)S(1)}, u32[]{:S(2)}, u32[]{:S(2)}) %collective-permute-start.1) | collective-permute-done | bytes 262176 | tf_op jit(solution)/shard_map/ppermute | solution.py:262
  37.1 2.2 %all-gather.2 = bf16[4,64,1024]{2,1,0:T(8,128)(2,1)S(1)} all-gather(bf16[2,64,1024]{2,1,0:T(8,128)(2,1)S(1)} %collective-permute-done.1), channel_id=4, replica_groups={{0,1},{2,3},{4,5},{6,7},{8,9},{10,11},{12,13},{14,15},{16,17},{18,19},{..., dimensions={0}, use_global_device_ids=true | all-gather | bytes 786432 | tf_op jit(solution)/shard_map/all_gather | solution.py:325
  39.3 0.0 copy-start.7
  39.3 0.0 collective-permute-done
  39.3 2.5 %all-gather.1 = bf16[4,96,1024]{2,1,0:T(8,128)(2,1)S(1)} all-gather(bf16[2,96,1024]{2,1,0:T(8,128)(2,1)S(1)} %collective-permute-done), channel_id=3, replica_groups={{0,1},{2,3},{4,5},{6,7},{8,9},{10,11},{12,13},{14,15},{16,17},{18,19},{..., dimensions={0}, use_global_device_ids=true | all-gather | bytes 1179648 | tf_op jit(solution)/shard_map/all_gather | solution.py:324
  41.8 0.0 collective-permute-done.2.corner
  41.8 0.0 copy-done.1
  41.8 0.0 copy-done.3
  41.8 0.0 copy-done.5
  41.8 0.4 shard_map.102
  42.2 3.8 %collective-permute-start.3 = (bf16[176,1024]{1,0:T(8,128)(2,1)S(1)}, bf16[176,1024]{1,0:T(8,128)(2,1)S(1)}, u32[]{:S(2)}, u32[]{:S(2)}) collective-permute-start(bf16[176,1024]{1,0:T(8,128)(2,1)S(1)} %get-tuple-element.17), channel_id=1, source_target_pairs={{0,64},{64,128},{128,192},{192,256},{256,320},{320,384},{384,448},... | collective-permute-start | bytes 1081352 | tf_op jit(solution)/shard_map/ppermute | solution.py:262
  46.1 2.0 %collective-permute-start.4 = (bf16[176,1024]{1,0:T(8,128)(2,1)S(1)}, bf16[176,1024]{1,0:T(8,128)(2,1)S(1)}, u32[]{:S(2)}, u32[]{:S(2)}) collective-permute-start(bf16[176,1024]{1,0:T(8,128)(2,1)S(1)} %get-tuple-element.18), channel_id=1, source_target_pairs={{64,0},{128,64},{192,128},{256,192},{320,256},{384,320},{448,384},... | collective-permute-start | bytes 1081352 | tf_op jit(solution)/shard_map/ppermute | solution.py:262
  48.1 0.0 copy-done.7
  48.1 0.0 copy-start.8
  48.1 0.0 copy-start.9
  48.1 1.2 %shard_map.103.fields = f32[5,4,24,1024]{3,2,1,0:T(8,128)S(1)} custom-call(s32[1]{0:T(128)} %bitcast.core_ref, f32[4,4]{1,0:T(4,128)S(1)} %copy-done.7, bf16[4,96,1024]{2,1,0:T(8,128)(2,1)S(1)} %get-tuple-element.15.spread, bf16[16,128,256]{2,1,0:T(8,128)(2,1)S(1)} %get-tuple-element.16.matrices, s32[4,16,1024]{2,1,0:T(8,128)S(1)} %copy-done.1, ...), custom_call_target="tpu_custom_call" | custom-call | flops 1000000 | bytes 2000000 | tf_op jit(solution)/shard_map/pallas_call | solution.py:25
  49.4 5.2 %collective-permute-done.3.below = bf16[176,1024]{1,0:T(8,128)(2,1)S(1)} collective-permute-done((bf16[176,1024]{1,0:T(8,128)(2,1)S(1)}, bf16[176,1024]{1,0:T(8,128)(2,1)S(1)}, u32[]{:S(2)}, u32[]{:S(2)}) %collective-permute-start.3) | collective-permute-done | bytes 360480 | tf_op jit(solution)/shard_map/ppermute | solution.py:262
  54.6 5.7 %collective-permute-done.4.above = bf16[176,1024]{1,0:T(8,128)(2,1)S(1)} collective-permute-done((bf16[176,1024]{1,0:T(8,128)(2,1)S(1)}, bf16[176,1024]{1,0:T(8,128)(2,1)S(1)}, u32[]{:S(2)}, u32[]{:S(2)}) %collective-permute-start.4) | collective-permute-done | bytes 360480 | tf_op jit(solution)/shard_map/ppermute | solution.py:262
  60.2 0.0 copy-done.8
  60.2 0.0 copy-done.9
  60.2 4.2 %shard_map.104 = f32[5,4,16,1024]{3,2,1,0:T(8,128)} custom-call(f32[3]{0:T(128)S(1)} %copy-done.8, f32[5]{0:T(128)S(1)} %copy-done.9, f32[5,4,24,1024]{3,2,1,0:T(8,128)S(1)} %shard_map.103.fields, bf16[176,1024]{1,0:T(8,128)(2,1)S(1)} %collective-permute-done.3.below, bf16[176,1024]{1,0:T(8,128)(2,1)S(1)} %collective-permute-done.4.above), custom_call_target="tpu_custom_call" | custom-call | flops 1000000 | bytes 2000000 | tf_op jit(solution)/shard_map/pallas_call | solution.py:25
  (9 shorter events, 0.2 us)
Async XLA Ops:
  0.0 0.9 %copy-start = (s32[4,16,1024]{2,1,0:T(8,128)S(1)}, s32[4,16,1024]{2,1,0:T(8,128)}, u32[]{:S(2)}) copy-start(s32[4,16,1024]{2,1,0:T(8,128)} %mask.5) | copy-start | bytes 786436
  1.0 0.9 %copy-start.2 = (bf16[4,16,1024]{2,1,0:T(8,128)(2,1)S(1)}, bf16[4,16,1024]{2,1,0:T(8,128)(2,1)}, u32[]{:S(2)}) copy-start(bf16[4,16,1024]{2,1,0:T(8,128)(2,1)} %pairs.5) | copy-start | bytes 393220
  1.9 0.9 %copy-start.4 = (bf16[4,16,1024]{2,1,0:T(8,128)(2,1)S(1)}, bf16[4,16,1024]{2,1,0:T(8,128)(2,1)}, u32[]{:S(2)}) copy-start(bf16[4,16,1024]{2,1,0:T(8,128)(2,1)} %clusters.5) | copy-start | bytes 393220
  2.8 0.9 %copy-start.6 = (bf16[4,16,1024]{2,1,0:T(8,128)(2,1)S(1)}, bf16[4,16,1024]{2,1,0:T(8,128)(2,1)}, u32[]{:S(2)}) copy-start(bf16[4,16,1024]{2,1,0:T(8,128)(2,1)} %power.1) | copy-start | bytes 393220
  3.7 15.7 %copy-start.10 = (s32[4]{0:T(128)S(1)}, s32[4]{0:T(128)}, u32[]{:S(2)}) copy-start(s32[4]{0:T(128)} %param.16) | copy-start | bytes 52
  3.7 38.1 %copy-start.1 = (s32[4,16,1024]{2,1,0:T(8,128)S(1)}, s32[4,16,1024]{2,1,0:T(8,128)}, u32[]{:S(2)}) copy-start(s32[4,16,1024]{2,1,0:T(8,128)} %mask.5) | copy-start | bytes 786436
  3.7 38.1 %copy-start.3 = (bf16[4,16,1024]{2,1,0:T(8,128)(2,1)S(1)}, bf16[4,16,1024]{2,1,0:T(8,128)(2,1)}, u32[]{:S(2)}) copy-start(bf16[4,16,1024]{2,1,0:T(8,128)(2,1)} %pairs.5) | copy-start | bytes 393220
  3.7 38.1 %copy-start.5 = (bf16[4,16,1024]{2,1,0:T(8,128)(2,1)S(1)}, bf16[4,16,1024]{2,1,0:T(8,128)(2,1)}, u32[]{:S(2)}) copy-start(bf16[4,16,1024]{2,1,0:T(8,128)(2,1)} %clusters.5) | copy-start | bytes 393220
  3.8 38.0 %collective-permute-start.2 = (bf16[16,1024]{1,0:T(8,128)(2,1)S(1)}, bf16[16,1024]{1,0:T(8,128)(2,1)S(1)}, u32[]{:S(2)}, u32[]{:S(2)}) collective-permute-start(bf16[16,1024]{1,0:T(8,128)(2,1)S(1)} %get-tuple-element.13), channel_id=1, source_target_pairs={{6,1},{8,3},{10,5},{12,7},{14,9},{16,11},{18,13},{20,15},{22,17},{... | collective-permute-start | bytes 98312 | tf_op jit(solution)/shard_map/ppermute | solution.py:262
  9.7 29.6 %collective-permute-start = (bf16[2,96,1024]{2,1,0:T(8,128)(2,1)S(1)}, bf16[2,96,1024]{2,1,0:T(8,128)(2,1)S(1)}, u32[]{:S(2)}, u32[]{:S(2)}) collective-permute-start(bf16[2,96,1024]{2,1,0:T(8,128)(2,1)S(1)} %bitcast.36), channel_id=1, source_target_pairs={{3,1},{0,2},{5,3},{2,4},{7,5},{4,6},{9,7},{6,8},{11,9},{8,10},{13,... | collective-permute-start | bytes 1179656 | tf_op jit(solution)/shard_map/ppermute | solution.py:262
  12.3 24.8 %collective-permute-start.1 = (bf16[2,64,1024]{2,1,0:T(8,128)(2,1)S(1)}, bf16[2,64,1024]{2,1,0:T(8,128)(2,1)S(1)}, u32[]{:S(2)}, u32[]{:S(2)}) collective-permute-start(bf16[2,64,1024]{2,1,0:T(8,128)(2,1)S(1)} %slice.56), channel_id=1, source_target_pairs={{5,1},{7,3},{0,4},{9,5},{2,6},{11,7},{4,8},{13,9},{6,10},{15,11},{... | collective-permute-start | bytes 786440 | tf_op jit(solution)/shard_map/ppermute | solution.py:262
  39.3 8.8 %copy-start.7 = (f32[4,4]{1,0:T(4,128)S(1)}, f32[4,4]{1,0:T(4,128)}, u32[]{:S(2)}) copy-start(f32[4,4]{1,0:T(4,128)} %doses.1) | copy-start | bytes 196
  42.2 12.3 %collective-permute-start.3 = (bf16[176,1024]{1,0:T(8,128)(2,1)S(1)}, bf16[176,1024]{1,0:T(8,128)(2,1)S(1)}, u32[]{:S(2)}, u32[]{:S(2)}) collective-permute-start(bf16[176,1024]{1,0:T(8,128)(2,1)S(1)} %get-tuple-element.17), channel_id=1, source_target_pairs={{0,64},{64,128},{128,192},{192,256},{256,320},{320,384},{384,448},... | collective-permute-start | bytes 1081352 | tf_op jit(solution)/shard_map/ppermute | solution.py:262
  46.1 14.2 %collective-permute-start.4 = (bf16[176,1024]{1,0:T(8,128)(2,1)S(1)}, bf16[176,1024]{1,0:T(8,128)(2,1)S(1)}, u32[]{:S(2)}, u32[]{:S(2)}) collective-permute-start(bf16[176,1024]{1,0:T(8,128)(2,1)S(1)} %get-tuple-element.18), channel_id=1, source_target_pairs={{64,0},{128,64},{192,128},{256,192},{320,256},{384,320},{448,384},... | collective-permute-start | bytes 1081352 | tf_op jit(solution)/shard_map/ppermute | solution.py:262
  48.1 12.2 %copy-start.8 = (f32[3]{0:T(128)S(1)}, f32[3]{0:T(128)}, u32[]{:S(2)}) copy-start(f32[3]{0:T(128)} %spreads.1) | copy-start | bytes 40
  48.1 12.1 %copy-start.9 = (f32[5]{0:T(128)S(1)}, f32[5]{0:T(128)}, u32[]{:S(2)}) copy-start(f32[5]{0:T(128)} %rates.1) | copy-start | bytes 64

commit v2 on v0

v2 whole, which is shorter than its diff:
```python
import functools

import jax
import jax.numpy as jnp
from jax import lax
from jax.experimental import pallas as pl
from jax.experimental.pallas import tpu as pltpu
from jax.sharding import PartitionSpec as P

TAPS = 97
HALF = 48
LAYERS = 4
ROWS = 16
LENGTH = 1024
GROUP = 24
WINDOW = 176
LATS = 64
DEPTHS = 8
F32 = jnp.float32
BF16 = jnp.bfloat16
MEMORY = 32 * 1024 * 1024


def call(kernel, outs, args, scalars=0, hbm=(), hbm_out=False, scratch=(), aliases={}, flops=1000000, size=2000000):
    def space(i):
        return pltpu.SMEM if i < scalars else pltpu.HBM if i in hbm else pltpu.VMEM

    out_space = pltpu.HBM if hbm_out else pltpu.VMEM
    return pl.pallas_call(
        kernel,
        out_shape=outs,
        in_specs=[pl.BlockSpec(memory_space=space(i)) for i in range(len(args))],
        out_specs=jax.tree.map(lambda _: pl.BlockSpec(memory_space=out_space), outs),
        scratch_shapes=list(scratch),
        input_output_aliases=aliases,
        compiler_params=pltpu.CompilerParams(vmem_limit_bytes=MEMORY),
        cost_estimate=pl.CostEstimate(flops=flops, bytes_accessed=size, transcendentals=0),
    )(*args)


def shape(dims, dtype):
    return jax.ShapeDtypeStruct(dims, dtype)


def tile(z):
    return pl.ds(ROWS * z, ROWS)


def along_matrix(line):
    wide = jnp.concatenate([line, jnp.zeros_like(line)], 1)
    wide = jnp.broadcast_to(wide, (128, 256))
    return pltpu.roll(wide, 16, 1, stride=1, stride_axis=0).astype(BF16)


def own_core():
    return lax.rem(lax.axis_index("lat"), 2)


def wide_taps(taps, lines):
    lines[...] = jnp.zeros_like(lines)
    for s in range(4):
        lines[pl.ds(s * LAYERS, LAYERS), :TAPS] = taps[s].astype(F32)


def band_kernel(tilt, taps_across, across_bands, across):
    wide_taps(taps_across, across)
    lane = lax.broadcasted_iota(jnp.int32, (GROUP, 256), 1)
    group = lax.broadcasted_iota(jnp.int32, (8, 256), 0)
    for z in range(LAYERS):
        offset = ROWS - 8 + ROWS * own_core() + tilt[z]
        for s in range(4):
            line = across[pl.ds(s * LAYERS + z, 1), :]
            wide = jnp.concatenate([line, jnp.zeros_like(line)], 1)
            wide = jnp.broadcast_to(wide, (32, 256))
            band = pltpu.roll(wide, 0, 1, stride=1, stride_axis=0)
            band = pltpu.roll(band, offset, 1)
            last = jnp.where(group < 2, band[24:], band[:8])
            band = jnp.concatenate([band[8:24], last], 0)
            tail = pltpu.roll(band, 4 * z, 1) if z else band
            tail = jnp.where((lane >= 160 + 4 * z) & (lane < 162 + 4 * z), tail, 0.0)
            across_bands[z, pl.ds(s * GROUP, GROUP), :] = jnp.where(lane < 160, band, tail)


def pair_edges(following, previous):
    sub = lax.broadcasted_iota(jnp.int32, (8, LENGTH), 0)
    return jnp.where(sub < 2, following, jnp.where(sub >= 6, previous, 0.0))


def cluster_edges(following, previous):
    sub = lax.broadcasted_iota(jnp.int32, (8, LENGTH), 0)
    following = pltpu.roll(following, 6, 0)
    previous = pltpu.roll(previous, 2, 0)
    return jnp.where(sub == 0, following, jnp.where(sub == 7, previous, 0.0))


SENT = ((1, 0), (2, 0), (0, 0), (3, 0), (1, 1), (2, 1))


def early_kernel(doses, pair, clusters, taps_along, down, up, taps, lines):
    wide_taps(taps_along, taps)
    lines[...] = jnp.zeros_like(lines)
    for side, (out, near, far) in enumerate(((down, 0, 1), (up, 3, 2))):
        for i, (s, distance) in enumerate(SENT):
            z = far if distance else near
            row = pl.ds(16 * side + 8 + i, 1)
            lines[row, pl.ds(0, 128)] = taps[pl.ds(s * LAYERS + z, 1), :]
            dose = jnp.full((1, 128), doses[s, z], F32)
            for part in range(1, 4):
                rounded = dose.astype(BF16).astype(F32)
                lines[row, pl.ds(128 * part, 128)] = rounded
                dose = dose - rounded
        out[pl.ds(0, 16), :] = pair[tile(near), :]
        out[pl.ds(16, 16), :] = clusters[near]
        out[pl.ds(32, 16), :] = pair[tile(far), :]
        out[pl.ds(48, 16), :] = lines[pl.ds(16 * side, 16), :].astype(BF16)


def across_kernel(
    mine, near, far, corner, bands, edges, others, early_down, early_up, spread, down, up, rims, window
):
    core = own_core()
    for out, early in ((down, early_down), (up, early_up)):
        out[pl.ds(112, 48), :] = early[pl.ds(0, 48), :]
    for z in range(LAYERS):
        at, also = tile(z), pl.ds(64 + ROWS * z, ROWS)
        parts = [far[0, at, :], far[0, also, :], near[0, at, :], near[0, also, :]]
        parts += [mine[0, at, :], mine[1, at, :], near[1, at, :], near[1, also, :]]
        parts += [far[1, at, :], far[1, also, :], corner[...]]
        for i, part in enumerate(parts):
            window[z, pl.ds(16 * i, 16), :] = part
        x = jnp.dot(bands[z].astype(BF16)[:, :WINDOW], window[z], preferred_element_type=F32)
        spread[z] = x.astype(BF16)
        half = slice(8 * (z % 2), 8 * (z % 2) + 8)
        at = pl.ds(16 * (z // 2), 16)
        other = others[at, :].astype(F32)
        following = jnp.where(core == 0, edges[1, at, :].astype(F32), other)[half]
        previous = jnp.where(core == 0, other, edges[0, at, :].astype(F32))[half]
        rims[0, z] = pair_edges(following, previous)
        rims[1, z] = cluster_edges(following, previous)
        out = down if z < 2 else up
        own = [x[GROUP * s : GROUP * s + ROWS].astype(BF16) for s in range(4)]
        rim = [x[GROUP * s + ROWS : GROUP * s + GROUP] for s in range(4)]
        if z in (0, 3):
            for i, s in enumerate((1, 2, 0, 3)):
                out[pl.ds(16 * i, 16), :] = own[s]
            out[pl.ds(64, 16), :] = jnp.concatenate([rim[1], rim[2]], 0).astype(BF16)
            lines = (early_down if z < 2 else early_up)[pl.ds(48, 16), :].astype(F32)[8:]
            out[pl.ds(160, 16), :] = jnp.concatenate([rims[0, z], lines], 0).astype(BF16)
        else:
            out[pl.ds(80, 16), :] = own[1]
            out[pl.ds(96, 16), :] = own[2]


def along_sum(x, matrix):
    rows = x.shape[0]
    zeros = jnp.zeros((rows, 64), F32)
    wide = jnp.concatenate([zeros, x, zeros], 1)
    blocks = LENGTH // 128
    stacked = jnp.concatenate([wide[:, 128 * b : 128 * b + 256] for b in range(blocks)], 0).astype(BF16)
    y = lax.dot_general(stacked, matrix, (((1,), (1,)), ((), ())), preferred_element_type=F32)
    return jnp.concatenate([y[rows * b : rows * (b + 1)] for b in range(blocks)], 1)


def laplace(center, below, above, rows):
    total = center.shape[0]
    inner = center[:rows]
    lane = lax.broadcasted_iota(jnp.int32, (rows, 128), 1)
    right = pltpu.roll(inner, LENGTH - 1, 1)
    left = pltpu.roll(inner, 1, 1)
    right = jnp.concatenate([right[:, :-128], jnp.where(lane == 127, 0.0, right[:, -128:])], 1)
    left = jnp.concatenate([jnp.where(lane == 0, 0.0, left[:, :128]), left[:, 128:]], 1)
    near = right + left
    near = near + pltpu.roll(center, total - 1, 0)[:rows] + pltpu.roll(center, 1, 0)[:rows]
    for layer in (below, above):
        if layer is not None:
            near = near + layer[:rows]
    return near - 6.0 * inner


def substep(spreads, rates, silicon, centers, belows, aboves, arsenic, clusters, rows):
    inter, vacancy, pair = (c[:rows] for c in centers)
    flows = [
        silicon * (spreads[f] * laplace(centers[f], belows[f], aboves[f], rows)) for f in range(3)
    ]
    recombine = rates[0] * inter * vacancy
    pairing = rates[1] * arsenic * inter - rates[2] * pair
    clustering = rates[3] * inter * inter - rates[4] * clusters
    new_inter = inter + (flows[0] - recombine - pairing - 2.0 * clustering)
    new_vacancy = vacancy + (flows[1] - recombine)
    new_pair = pair + (flows[2] + pairing)
    return (new_inter, new_vacancy, new_pair), (arsenic - pairing, clusters + clustering)


NONE = (None, None, None)


def along_kernel(spreads, rates, doses, spread, taps_along, pairs, clusters, rims, outer, late, still, fields, fixed, along):
    wide_taps(taps_along, along)
    for z in range(LAYERS):
        x = spread[z].astype(F32)
        pair = jnp.concatenate([pairs[tile(z), :].astype(F32), rims[0, z]], 0)
        silicon = (pair > 0.0).astype(F32)
        before = jnp.concatenate([clusters[z].astype(F32), rims[1, z]], 0)
        sums = []
        for s in range(4):
            matrix = along_matrix(along[pl.ds(s * LAYERS + z, 1), :])
            y = along_sum(x[GROUP * s : GROUP * (s + 1)], matrix)
            sums.append(doses[s, z] * y)
        fields[0, z] = silicon * sums[1]
        fields[1, z] = silicon * sums[2]
        fields[2, z] = pair
        fixed[0, z] = silicon * sums[0]
        fixed[1, z] = silicon * (before + sums[3])
    for z in range(LAYERS):
        silicon = (fields[2, z] > 0.0).astype(F32)
        belows = [fields[f, z - 1] for f in range(3)] if z > 0 else NONE
        aboves = [fields[f, z + 1] for f in range(3)] if z < LAYERS - 1 else NONE
        centers = [fields[f, z] for f in range(3)]
        mobile, others = substep(spreads, rates, silicon, centers, belows, aboves, fixed[0, z], fixed[1, z], GROUP)
        for f in range(3):
            late[f, z] = mobile[f]
            if z in (0, 3):
                outer[f, z // 3] = fields[f, z, :ROWS]
        for f in range(2):
            still[f, z] = others[f][:ROWS]


def react_kernel(side, spreads, rates, outer, late, still, pairs, rims_own, payload, *refs):
    result, near_late, own_late, done, sems = refs[-5:]

    def sent(i):
        return payload[pl.ds(16 * i, 16), :].astype(F32)

    rows = sent(10)
    pair_rim, lines = rows[:8], rows[8:]

    def implanted(i, x):
        line = lines[i : i + 1]
        dose = line[:, 128:129] + line[:, 256:257] + line[:, 384:385]
        return dose * along_sum(x, along_matrix(line[:, :128]))

    rims = sent(4)
    pair = jnp.concatenate([sent(7), pair_rim], 0)
    silicon = (pair > 0.0).astype(F32)
    near = [
        silicon * implanted(0, jnp.concatenate([sent(0), rims[:8]], 0)),
        silicon * implanted(1, jnp.concatenate([sent(1), rims[8:]], 0)),
        pair,
    ]
    silicon = silicon[:ROWS]
    arsenic = silicon * implanted(2, sent(2))
    clusters = silicon * (sent(8) + implanted(3, sent(3)))
    far_pair = sent(9)
    far_silicon = (far_pair > 0.0).astype(F32)
    far = [far_silicon * implanted(4, sent(5)), far_silicon * implanted(5, sent(6)), far_pair]
    beside = [outer[f, side] for f in range(3)]
    mobile, _ = substep(spreads, rates, silicon, near, far, beside, arsenic, clusters, ROWS)
    z = 3 * side
    own_pair = jnp.concatenate([pairs[tile(z), :].astype(F32), rims_own[0, z]], 0)
    own_silicon = (own_pair > 0.0).astype(F32)
    for f in range(3):
        near_late[f] = mobile[f]
        own_late[f] = late[f, z] + own_silicon * (spreads[f] * near[f])

    def layer(f, at):
        if at in (-1, LAYERS):
            return near_late[f]
        return own_late[f] if at == z else late[f, at]

    for i in range(2):
        at = 2 * side + i
        silicon = (pairs[tile(at), :].astype(F32) > 0.0).astype(F32)
        centers = [layer(f, at) for f in range(3)]
        belows = [layer(f, at - 1) for f in range(3)]
        aboves = [layer(f, at + 1) for f in range(3)]
        mobile, others = substep(spreads, rates, silicon, centers, belows, aboves, still[0, at], still[1, at], ROWS)
        for f, new in enumerate((others[0], *mobile, others[1])):
            done[f, i] = new
        pltpu.make_async_copy(done.at[:, i], result.at[:, at], sems.at[i]).start()
    for i in range(2):
        pltpu.make_async_copy(done.at[:, i], result.at[:, 2 * side + i], sems.at[i]).wait()


def moved(array, axis, size, source):
    route = [(source(i), i) for i in range(size) if source(i) is not None and 0 <= source(i) < size]
    return lax.ppermute(array, axis, route)


def lanes(core0, core1):
    return lambda i: i + core0 if i % 2 == 0 else (None if core1 is None else i + core1)


def body(
    fin_mask,
    stopping_power,
    pairs_before,
    clusters_before,
    taps_across,
    taps_along,
    tilt_shift,
    layer_doses,
    diffusivity,
    reaction_rates,
):
    couples = [[2 * i, 2 * i + 1] for i in range(LATS // 2)]

    def shared(array):
        return lax.all_gather(array, "lat", axis_index_groups=couples)

    silicon = fin_mask.astype(BF16)
    source = silicon * stopping_power
    pair = silicon * pairs_before
    edges = [pair[:, :2], clusters_before[:, :1], pair[:, 3:5], clusters_before[:, 15:], pair[:, 14:]]
    edges = jnp.concatenate(edges, 1).reshape(32, LENGTH)
    others = moved(edges, "lat", LATS, lanes(-1, 1))
    pair = pair.reshape(64, LENGTH)
    mine = shared(source.reshape(64, LENGTH)).reshape(128, LENGTH)
    near = moved(mine, "lat", LATS, lanes(-2, 2))
    far = moved(mine, "lat", LATS, lanes(-4, 4))
    corner = jnp.pad(source[:, :2], ((0, 0), (0, 2), (0, 0))).reshape(16, LENGTH)
    corner = moved(corner, "lat", LATS, lambda i: None if i % 2 == 0 else i + 5)
    edges, corner = lax.optimization_barrier((edges, corner))
    edges = shared(edges)
    early_down, early_up = call(
        early_kernel,
        (shape((64, LENGTH), BF16), shape((64, LENGTH), BF16)),
        (layer_doses, pair, clusters_before, taps_along),
        scalars=1,
        scratch=[pltpu.VMEM((16, 128), F32), pltpu.VMEM((32, LENGTH), F32)],
    )
    across_bands = call(
        band_kernel,
        shape((LAYERS, 4 * GROUP, 256), F32),
        (tilt_shift, taps_across),
        scalars=1,
        scratch=[pltpu.VMEM((16, 128), F32)],
    )
    near = shared(near)
    far, near, early_down, early_up = lax.optimization_barrier((far, near, early_down, early_up))
    far = shared(far)
    others, far = lax.optimization_barrier((others, far))
    spread, down, up, rims = call(
        across_kernel,
        (
            shape((LAYERS, 4 * GROUP, LENGTH), BF16),
            shape((176, LENGTH), BF16),
            shape((176, LENGTH), BF16),
            shape((2, LAYERS, 8, LENGTH), F32),
        ),
        (
            mine.reshape(2, 64, LENGTH),
            near.reshape(2, 128, LENGTH),
            far,
            corner,
            across_bands,
            edges,
            others,
            early_down,
            early_up,
        ),
        scratch=[pltpu.VMEM((LAYERS, WINDOW, LENGTH), BF16)],
    )
    below = moved(up, "depth", DEPTHS, lambda i: i - 1)
    above = moved(down, "depth", DEPTHS, lambda i: i + 1)
    outer, late, still = call(
        along_kernel,
        (
            shape((3, 2, ROWS, LENGTH), F32),
            shape((3, LAYERS, GROUP, LENGTH), F32),
            shape((2, LAYERS, ROWS, LENGTH), F32),
        ),
        (diffusivity, reaction_rates, layer_doses, spread, taps_along, pair, clusters_before, rims),
        scalars=3,
        scratch=[
            pltpu.VMEM((3, LAYERS, GROUP, LENGTH), F32),
            pltpu.VMEM((2, LAYERS, GROUP, LENGTH), F32),
            pltpu.VMEM((16, 128), F32),
        ],
    )
    scratch = [
        pltpu.VMEM((3, ROWS, LENGTH), F32),
        pltpu.VMEM((3, GROUP, LENGTH), F32),
        pltpu.VMEM((5, 2, ROWS, LENGTH), F32),
        pltpu.SemaphoreType.DMA((2,)),
    ]
    given = (diffusivity, reaction_rates, outer, late, still, pair, rims)
    for side, payload in enumerate((below, above)):
        args = (*given, payload) if side == 0 else (*given, payload, result)
        result = call(
            functools.partial(react_kernel, side),
            shape((5, LAYERS, ROWS, LENGTH), F32),
            args,
            scalars=2,
            hbm=(8,),
            hbm_out=True,
            scratch=scratch,
            aliases={8: 0} if side else {},
        )
    return result


def solution(mesh):
    return jax.shard_map(
        body,
        mesh=mesh,
        in_specs=(
            P("depth", "lat", None),
            P("depth", "lat", None),
            P("depth", "lat", None),
            P("depth", "lat", None),
            P(None, "depth", None),
            P(None, "depth", None),
            P("depth"),
            P(None, "depth"),
            P(),
            P(),
        ),
        out_specs=P(None, "depth", "lat", None),
        check_vma=False,
    )
```

time: 133 us -> 50.6 us (0.38)
  the two profiles are of different devices: /device:TPU:320 before, /device:TPU:62 now
where the time goes in v2:
time: 50.6 us; the launch traced here: 50.3 us
  starting transfers between devices  19.8 us (39%)
  blocking collectives  11.1 us (22%)
  Pallas kernels  8.94 us (18%)
  waiting for transfers between devices  8.08 us (16%)
  other arithmetic  1.92 us (4%)
    ppermute x6, starting transfers between devices, moved(): return lax.ppermute(array, axis, route)  19.8 us
    all_gather x4, blocking collectives, shared(): return lax.all_gather(array, 'lat', axis_index_groups=couples)  11.1 us
    pallas_call x6, Pallas kernels, call(): pl.pallas_call(kernel, out_shape=outs, in_specs=[pl.BlockSpec(memory_spac...  8.94 us
    ppermute x6, waiting for transfers between devices, moved(): return lax.ppermute(array, axis, route)  8.08 us
    mul x1, other arithmetic, body(): pair = silicon * pairs_before  1.17 us
  transfers between devices with their start and end apart: 6, of which 2 were waited for; matrix products, arithmetic and copies ran while one was open for 2% of the time, Pallas kernels for 13%

profile of v2, /device:TPU:62, one launch (start us, length us, event | category | flops | bytes accessed | tf_op | source)
XLA Modules:
  0.0 50.3 jit_solution(13255510398377483102)
XLA Ops:
  0.0 0.0 copy-start
  0.0 0.0 copy-start.6
  0.0 0.0 copy-start.5
  0.0 0.0 copy-start.2
  0.0 0.0 copy-start.1
  0.0 1.2 %convert_multiply_fusion = (bf16[4,16,1024]{2,1,0:T(8,128)(2,1)S(1)}, bf16[4,16,1024]{2,1,0:T(8,128)(2,1)S(1)}) fusion(bf16[4,16,1024]{2,1,0:T(8,128)(2,1)} %param.12, s32[4,16,1024]{2,1,0:T(8,128)} %param.10, bf16[4,16,1024]{2,1,0:T(8,128)(2,1)} %param.11), kind=kLoop, calls=%fused_computation | loop fusion | flops 196608 | bytes 786432 | tf_op jit(solution)/shard_map/mul | solution.py:312
  1.2 2.0 %all_gather.21.mine = bf16[2,64,1024]{2,1,0:T(8,128)(2,1)S(1)} all-gather(bf16[1,64,1024]{2,1,0:T(8,128)(2,1)S(1)} %bitcast.16), channel_id=1, replica_groups={{0,1},{2,3},{4,5},{6,7},{8,9},{10,11},{12,13},{14,15},{16,17},{18,19},{..., dimensions={0}, use_global_device_ids=true | all-gather | bytes 393216 | tf_op jit(solution)/shard_map/all_gather | solution.py:308
  3.2 5.3 %collective-permute-start.1 = (bf16[128,1024]{1,0:T(8,128)(2,1)S(1)}, bf16[128,1024]{1,0:T(8,128)(2,1)S(1)}, u32[]{:S(2)}, u32[]{:S(2)}) collective-permute-start(bf16[128,1024]{1,0:T(8,128)(2,1)S(1)} %bitcast.13), channel_id=1, source_target_pairs={{3,1},{0,2},{5,3},{2,4},{7,5},{4,6},{9,7},{6,8},{11,9},{8,10},{13,... | collective-permute-start | bytes 786440 | tf_op jit(solution)/shard_map/ppermute | solution.py:286
  8.5 4.5 %collective-permute-start = (bf16[128,1024]{1,0:T(8,128)(2,1)S(1)}, bf16[128,1024]{1,0:T(8,128)(2,1)S(1)}, u32[]{:S(2)}, u32[]{:S(2)}) collective-permute-start(bf16[128,1024]{1,0:T(8,128)(2,1)S(1)} %bitcast.14), channel_id=1, source_target_pairs={{5,1},{7,3},{0,4},{9,5},{2,6},{11,7},{4,8},{13,9},{6,10},{15,11},{... | collective-permute-start | bytes 786440 | tf_op jit(solution)/shard_map/ppermute | solution.py:286
  13.0 0.7 %slice_select_fusion = bf16[4,4,1024]{2,1,0:T(4,128)(2,1)S(1)} fusion(bf16[4,16,1024]{2,1,0:T(8,128)(2,1)S(1)} %get-tuple-element.40, pred[4]{0:T(512)(128)(4,1)} %constant.3.clone.1), kind=kLoop, calls=%fused_computation.2 | loop fusion | flops 16384 | bytes 65540 | tf_op jit(solution)/shard_map/jit(_pad)/pad | solution.py:320
  13.8 1.3 %collective-permute-start.3 = (bf16[16,1024]{1,0:T(8,128)(2,1)S(1)}, bf16[16,1024]{1,0:T(8,128)(2,1)S(1)}, u32[]{:S(2)}, u32[]{:S(2)}) collective-permute-start(bf16[16,1024]{1,0:T(8,128)(2,1)S(1)} %reshape.15), channel_id=1, source_target_pairs={{6,1},{8,3},{10,5},{12,7},{14,9},{16,11},{18,13},{20,15},{22,17},{... | collective-permute-start | bytes 98312 | tf_op jit(solution)/shard_map/ppermute | solution.py:286
  15.1 0.0 copy-done
  15.2 0.1 concatenate.3
  15.3 1.9 %collective-permute-start.2 = (bf16[32,1024]{1,0:T(8,128)(2,1)S(1)}, bf16[32,1024]{1,0:T(8,128)(2,1)S(1)}, u32[]{:S(2)}, u32[]{:S(2)}) collective-permute-start(bf16[32,1024]{1,0:T(8,128)(2,1)S(1)} %bitcast.17), channel_id=1, source_target_pairs={{2,1},{1,2},{4,3},{3,4},{6,5},{5,6},{8,7},{7,8},{10,9},{9,10},{12,... | collective-permute-start | bytes 196616 | tf_op jit(solution)/shard_map/ppermute | solution.py:286
  17.2 0.0 copy-done.6
  17.2 0.0 copy-done.5
  17.2 1.5 %shard_map.101.bands = f32[4,96,256]{2,1,0:T(8,128)S(1)} custom-call(s32[4]{0:T(128)S(1)} %copy-done.6, bf16[4,4,97]{2,1,0:T(4,128)(2,1)S(1)} %copy-done.5), custom_call_target="tpu_custom_call" | custom-call | flops 1000000 | bytes 2000000 | tf_op jit(solution)/shard_map/pallas_call | solution.py:29
  18.7 0.0 copy-done.2
  18.7 0.0 copy-done.1
  18.7 0.6 %shard_map.100 = (bf16[64,1024]{1,0:T(8,128)(2,1)S(1)}, bf16[64,1024]{1,0:T(8,128)(2,1)S(1)}) custom-call(f32[4,4]{1,0:T(4,128)S(1)} %copy-done.2, bf16[64,1024]{1,0:T(8,128)(2,1)S(1)} %bitcast.7, bf16[4,16,1024]{2,1,0:T(8,128)(2,1)S(1)} %copy-done, bf16[4,4,97]{2,1,0:T(4,128)(2,1)S(1)} %copy-done.1), custom_call_target="tpu_custom_call" | custom-call | flops 1000000 | bytes 2000000 | tf_op jit(solution)/shard_map/pallas_call | solution.py:29
  19.4 0.0 collective-permute-done.3.corner
  19.4 4.6 %all-gather.2 = bf16[64,1024]{1,0:T(8,128)(2,1)S(1)} all-gather(bf16[32,1024]{1,0:T(8,128)(2,1)S(1)} %bitcast.18), channel_id=4, replica_groups={{0,1},{2,3},{4,5},{6,7},{8,9},{10,11},{12,13},{14,15},{16,17},{18,19},{..., dimensions={0}, use_global_device_ids=true | all-gather | bytes 196608 | tf_op jit(solution)/shard_map/all_gather | solution.py:308
  24.0 0.0 collective-permute-done.1
  24.0 2.2 %all-gather = bf16[256,1024]{1,0:T(8,128)(2,1)S(1)} all-gather(bf16[128,1024]{1,0:T(8,128)(2,1)S(1)} %collective-permute-done.1), channel_id=2, replica_groups={{0,1},{2,3},{4,5},{6,7},{8,9},{10,11},{12,13},{14,15},{16,17},{18,19},{..., dimensions={0}, use_global_device_ids=true | all-gather | bytes 786432 | tf_op jit(solution)/shard_map/all_gather | solution.py:308
  26.2 0.0 collective-permute-done
  26.2 0.0 copy-start.3
  26.2 0.0 copy-start.4
  26.2 2.3 %all-gather.1 = bf16[256,1024]{1,0:T(8,128)(2,1)S(1)} all-gather(bf16[128,1024]{1,0:T(8,128)(2,1)S(1)} %collective-permute-done), channel_id=3, replica_groups={{0,1},{2,3},{4,5},{6,7},{8,9},{10,11},{12,13},{14,15},{16,17},{18,19},{..., dimensions={0}, use_global_device_ids=true | all-gather | bytes 786432 | tf_op jit(solution)/shard_map/all_gather | solution.py:308
  28.5 0.0 collective-permute-done.2.others
  28.5 0.4 shard_map.102
  28.9 4.9 %collective-permute-start.5 = (bf16[176,1024]{1,0:T(8,128)(2,1)S(1)}, bf16[176,1024]{1,0:T(8,128)(2,1)S(1)}, u32[]{:S(2)}, u32[]{:S(2)}) collective-permute-start(bf16[176,1024]{1,0:T(8,128)(2,1)S(1)} %get-tuple-element.38), channel_id=1, source_target_pairs={{0,64},{64,128},{128,192},{192,256},{256,320},{320,384},{384,448},... | collective-permute-start | bytes 1081352 | tf_op jit(solution)/shard_map/ppermute | solution.py:286
  33.8 1.9 %collective-permute-start.4 = (bf16[176,1024]{1,0:T(8,128)(2,1)S(1)}, bf16[176,1024]{1,0:T(8,128)(2,1)S(1)}, u32[]{:S(2)}, u32[]{:S(2)}) collective-permute-start(bf16[176,1024]{1,0:T(8,128)(2,1)S(1)} %get-tuple-element.37), channel_id=1, source_target_pairs={{64,0},{128,64},{192,128},{256,192},{320,256},{384,320},{448,384},... | collective-permute-start | bytes 1081352 | tf_op jit(solution)/shard_map/ppermute | solution.py:286
  35.7 0.0 copy-done.3
  35.7 0.0 copy-done.4
  35.8 2.2 %shard_map.103 = (f32[3,2,16,1024]{3,2,1,0:T(8,128)S(1)}, f32[3,4,24,1024]{3,2,1,0:T(8,128)S(1)}, f32[2,4,16,1024]{3,2,1,0:T(8,128)S(1)}) custom-call(f32[3]{0:T(128)S(1)} %copy-done.3, f32[5]{0:T(128)S(1)} %copy-done.4, f32[4,4]{1,0:T(4,128)S(1)} %copy-done.2, bf16[4,96,1024]{2,1,0:T(8,128)(2,1)S(1)} %get-tuple-element.32.spread, ...), custom_call_target="tpu_custom_call" | custom-call | flops 1000000 | bytes 2000000 | tf_op jit(solution)/shard_map/pallas_call | solution.py:29
  38.0 4.0 %collective-permute-done.5.payload = bf16[176,1024]{1,0:T(8,128)(2,1)S(1)} collective-permute-done((bf16[176,1024]{1,0:T(8,128)(2,1)S(1)}, bf16[176,1024]{1,0:T(8,128)(2,1)S(1)}, u32[]{:S(2)}, u32[]{:S(2)}) %collective-permute-start.5) | collective-permute-done | bytes 360480 | tf_op jit(solution)/shard_map/ppermute | solution.py:286
  42.0 2.1 %shard_map.104.refs_0_ = f32[5,4,16,1024]{3,2,1,0:T(8,128)} custom-call(f32[3]{0:T(128)S(1)} %copy-done.3, f32[5]{0:T(128)S(1)} %copy-done.4, f32[3,2,16,1024]{3,2,1,0:T(8,128)S(1)} %get-tuple-element.34.outer, f32[3,4,24,1024]{3,2,1,0:T(8,128)S(1)} %get-tuple-element.35.late, f32[2,4,16,1024]{3,2,1,0:T(8,128)S(1)} %get-tuple-element.36.still, ...), custom_call_target="tpu_custom_call" | custom-call | flops 1000000 | bytes 2000000 | tf_op jit(solution)/shard_map/pallas_call | solution.py:29
  44.1 4.1 %collective-permute-done.4.payload = bf16[176,1024]{1,0:T(8,128)(2,1)S(1)} collective-permute-done((bf16[176,1024]{1,0:T(8,128)(2,1)S(1)}, bf16[176,1024]{1,0:T(8,128)(2,1)S(1)}, u32[]{:S(2)}, u32[]{:S(2)}) %collective-permute-start.4) | collective-permute-done | bytes 360480 | tf_op jit(solution)/shard_map/ppermute | solution.py:286
  48.2 2.1 %shard_map.105 = f32[5,4,16,1024]{3,2,1,0:T(8,128)} custom-call(f32[3]{0:T(128)S(1)} %copy-done.3, f32[5]{0:T(128)S(1)} %copy-done.4, f32[3,2,16,1024]{3,2,1,0:T(8,128)S(1)} %get-tuple-element.34.outer, f32[3,4,24,1024]{3,2,1,0:T(8,128)S(1)} %get-tuple-element.35.late, ...), custom_call_target="tpu_custom_call", output_to_operand_aliasing={{}: (8, {})} | custom-call | flops 1000000 | bytes 2000000 | tf_op jit(solution)/shard_map/pallas_call | solution.py:29
  (3 shorter events, 0.1 us)
Async XLA Ops:
  0.0 15.1 %copy-start = (bf16[4,16,1024]{2,1,0:T(8,128)(2,1)S(1)}, bf16[4,16,1024]{2,1,0:T(8,128)(2,1)}, u32[]{:S(2)}) copy-start(bf16[4,16,1024]{2,1,0:T(8,128)(2,1)} %clusters.3) | copy-start | bytes 393220
  0.0 17.2 %copy-start.6 = (s32[4]{0:T(128)S(1)}, s32[4]{0:T(128)}, u32[]{:S(2)}) copy-start(s32[4]{0:T(128)} %tilt.1) | copy-start | bytes 52
  0.0 17.2 %copy-start.5 = (bf16[4,4,97]{2,1,0:T(4,128)(2,1)S(1)}, bf16[4,4,97]{2,1,0:T(4,128)(2,1)}, u32[]{:S(2)}) copy-start(bf16[4,4,97]{2,1,0:T(4,128)(2,1)} %taps_across.1) | copy-start | bytes 9316
  0.0 18.7 %copy-start.2 = (f32[4,4]{1,0:T(4,128)S(1)}, f32[4,4]{1,0:T(4,128)}, u32[]{:S(2)}) copy-start(f32[4,4]{1,0:T(4,128)} %doses.3) | copy-start | bytes 196
  0.0 18.7 %copy-start.1 = (bf16[4,4,97]{2,1,0:T(4,128)(2,1)S(1)}, bf16[4,4,97]{2,1,0:T(4,128)(2,1)}, u32[]{:S(2)}) copy-start(bf16[4,4,97]{2,1,0:T(4,128)(2,1)} %taps_along.3) | copy-start | bytes 9316
  3.2 20.8 %collective-permute-start.1 = (bf16[128,1024]{1,0:T(8,128)(2,1)S(1)}, bf16[128,1024]{1,0:T(8,128)(2,1)S(1)}, u32[]{:S(2)}, u32[]{:S(2)}) collective-permute-start(bf16[128,1024]{1,0:T(8,128)(2,1)S(1)} %bitcast.13), channel_id=1, source_target_pairs={{3,1},{0,2},{5,3},{2,4},{7,5},{4,6},{9,7},{6,8},{11,9},{8,10},{13,... | collective-permute-start | bytes 786440 | tf_op jit(solution)/shard_map/ppermute | solution.py:286
  8.5 17.7 %collective-permute-start = (bf16[128,1024]{1,0:T(8,128)(2,1)S(1)}, bf16[128,1024]{1,0:T(8,128)(2,1)S(1)}, u32[]{:S(2)}, u32[]{:S(2)}) collective-permute-start(bf16[128,1024]{1,0:T(8,128)(2,1)S(1)} %bitcast.14), channel_id=1, source_target_pairs={{5,1},{7,3},{0,4},{9,5},{2,6},{11,7},{4,8},{13,9},{6,10},{15,11},{... | collective-permute-start | bytes 786440 | tf_op jit(solution)/shard_map/ppermute | solution.py:286
  13.8 5.6 %collective-permute-start.3 = (bf16[16,1024]{1,0:T(8,128)(2,1)S(1)}, bf16[16,1024]{1,0:T(8,128)(2,1)S(1)}, u32[]{:S(2)}, u32[]{:S(2)}) collective-permute-start(bf16[16,1024]{1,0:T(8,128)(2,1)S(1)} %reshape.15), channel_id=1, source_target_pairs={{6,1},{8,3},{10,5},{12,7},{14,9},{16,11},{18,13},{20,15},{22,17},{... | collective-permute-start | bytes 98312 | tf_op jit(solution)/shard_map/ppermute | solution.py:286
  15.3 13.2 %collective-permute-start.2 = (bf16[32,1024]{1,0:T(8,128)(2,1)S(1)}, bf16[32,1024]{1,0:T(8,128)(2,1)S(1)}, u32[]{:S(2)}, u32[]{:S(2)}) collective-permute-start(bf16[32,1024]{1,0:T(8,128)(2,1)S(1)} %bitcast.17), channel_id=1, source_target_pairs={{2,1},{1,2},{4,3},{3,4},{6,5},{5,6},{8,7},{7,8},{10,9},{9,10},{12,... | collective-permute-start | bytes 196616 | tf_op jit(solution)/shard_map/ppermute | solution.py:286
  26.2 9.5 %copy-start.3 = (f32[3]{0:T(128)S(1)}, f32[3]{0:T(128)}, u32[]{:S(2)}) copy-start(f32[3]{0:T(128)} %spreads.5) | copy-start | bytes 40
  26.2 9.5 %copy-start.4 = (f32[5]{0:T(128)S(1)}, f32[5]{0:T(128)}, u32[]{:S(2)}) copy-start(f32[5]{0:T(128)} %rates.5) | copy-start | bytes 64
  28.9 13.1 %collective-permute-start.5 = (bf16[176,1024]{1,0:T(8,128)(2,1)S(1)}, bf16[176,1024]{1,0:T(8,128)(2,1)S(1)}, u32[]{:S(2)}, u32[]{:S(2)}) collective-permute-start(bf16[176,1024]{1,0:T(8,128)(2,1)S(1)} %get-tuple-element.38), channel_id=1, source_target_pairs={{0,64},{64,128},{128,192},{192,256},{256,320},{320,384},{384,448},... | collective-permute-start | bytes 1081352 | tf_op jit(solution)/shard_map/ppermute | solution.py:286
  33.8 14.4 %collective-permute-start.4 = (bf16[176,1024]{1,0:T(8,128)(2,1)S(1)}, bf16[176,1024]{1,0:T(8,128)(2,1)S(1)}, u32[]{:S(2)}, u32[]{:S(2)}) collective-permute-start(bf16[176,1024]{1,0:T(8,128)(2,1)S(1)} %get-tuple-element.37), channel_id=1, source_target_pairs={{64,0},{128,64},{192,128},{256,192},{320,256},{384,320},{448,384},... | collective-permute-start | bytes 1081352 | tf_op jit(solution)/shard_map/ppermute | solution.py:286

commit v3 on v2

--- a/solution.py
+++ b/solution.py
@@ -62,7 +62,22 @@
         lines[pl.ds(s * LAYERS, LAYERS), :TAPS] = taps[s].astype(F32)
 
 
-def band_kernel(tilt, taps_across, across_bands, across):
+def pair_edges(following, previous):
+    sub = lax.broadcasted_iota(jnp.int32, (8, LENGTH), 0)
+    return jnp.where(sub < 2, following, jnp.where(sub >= 6, previous, 0.0))
+
+
+def cluster_edges(following, previous):
+    sub = lax.broadcasted_iota(jnp.int32, (8, LENGTH), 0)
+    following = pltpu.roll(following, 6, 0)
+    previous = pltpu.roll(previous, 2, 0)
+    return jnp.where(sub == 0, following, jnp.where(sub == 7, previous, 0.0))
+
+
+SENT = ((1, 0), (2, 0), (0, 0), (3, 0), (1, 1), (2, 1))
+
+
+def prepare_kernel(tilt, doses, taps_across, taps_along, pair, clusters, across_bands, down, up, across, taps, lines):
     wide_taps(taps_across, across)
     lane = lax.broadcasted_iota(jnp.int32, (GROUP, 256), 1)
     group = lax.broadcasted_iota(jnp.int32, (8, 256), 0)
@@ -71,32 +86,13 @@
         for s in range(4):
             line = across[pl.ds(s * LAYERS + z, 1), :]
             wide = jnp.concatenate([line, jnp.zeros_like(line)], 1)
-            wide = jnp.broadcast_to(wide, (32, 256))
-            band = pltpu.roll(wide, 0, 1, stride=1, stride_axis=0)
-            band = pltpu.roll(band, offset, 1)
+            wide = pltpu.roll(jnp.broadcast_to(wide, (8, 256)), offset, 1)
+            band = pltpu.roll(jnp.broadcast_to(wide[:1], (32, 256)), 0, 1, stride=1, stride_axis=0)
             last = jnp.where(group < 2, band[24:], band[:8])
             band = jnp.concatenate([band[8:24], last], 0)
             tail = pltpu.roll(band, 4 * z, 1) if z else band
             tail = jnp.where((lane >= 160 + 4 * z) & (lane < 162 + 4 * z), tail, 0.0)
             across_bands[z, pl.ds(s * GROUP, GROUP), :] = jnp.where(lane < 160, band, tail)
-
-
-def pair_edges(following, previous):
-    sub = lax.broadcasted_iota(jnp.int32, (8, LENGTH), 0)
-    return jnp.where(sub < 2, following, jnp.where(sub >= 6, previous, 0.0))
-
-
-def cluster_edges(following, previous):
-    sub = lax.broadcasted_iota(jnp.int32, (8, LENGTH), 0)
-    following = pltpu.roll(following, 6, 0)
-    previous = pltpu.roll(previous, 2, 0)
-    return jnp.where(sub == 0, following, jnp.where(sub == 7, previous, 0.0))
-
-
-SENT = ((1, 0), (2, 0), (0, 0), (3, 0), (1, 1), (2, 1))
-
-
-def early_kernel(doses, pair, clusters, taps_along, down, up, taps, lines):
     wide_taps(taps_along, taps)
     lines[...] = jnp.zeros_like(lines)
     for side, (out, near, far) in enumerate(((down, 0, 1), (up, 3, 2))):
@@ -115,12 +111,29 @@
         out[pl.ds(48, 16), :] = lines[pl.ds(16 * side, 16), :].astype(BF16)
 
 
+def packed_rims(fields):
+    sub = lax.broadcasted_iota(jnp.int32, (8, LENGTH), 0)
+    total = jnp.where((sub == 0) | (sub == 7), fields[0], 0.0)
+    for i, field in enumerate(fields[1:], 1):
+        total = jnp.where(sub == i, pltpu.roll(field, i, 0), total)
+        total = jnp.where(sub == 7 - i, pltpu.roll(field, 8 - i, 0), total)
+    return total
+
+
+def unpacked_rim(packed, i):
+    sub = lax.broadcasted_iota(jnp.int32, (8, LENGTH), 0)
+    following = pltpu.roll(packed, 8 - i, 0) if i else packed
+    previous = pltpu.roll(packed, i, 0) if i else packed
+    return jnp.where(sub == 0, following, jnp.where(sub == 7, previous, 0.0))
+
+
 def across_kernel(
-    mine, near, far, corner, bands, edges, others, early_down, early_up, spread, down, up, rims, window
+    mine, near, received, far, corner, bands, early_down, early_up, spread, across_even, across_odd, rims, window
 ):
     core = own_core()
-    for out, early in ((down, early_down), (up, early_up)):
-        out[pl.ds(112, 48), :] = early[pl.ds(0, 48), :]
+    payloads = ({}, {})
+    for payload, early in zip(payloads, (early_down, early_up)):
+        payload[112, 48] = early[pl.ds(0, 48), :]
     for z in range(LAYERS):
         at, also = tile(z), pl.ds(64 + ROWS * z, ROWS)
         parts = [far[0, at, :], far[0, also, :], near[0, at, :], near[0, also, :]]
@@ -130,25 +143,45 @@
             window[z, pl.ds(16 * i, 16), :] = part
         x = jnp.dot(bands[z].astype(BF16)[:, :WINDOW], window[z], preferred_element_type=F32)
         spread[z] = x.astype(BF16)
-        half = slice(8 * (z % 2), 8 * (z % 2) + 8)
-        at = pl.ds(16 * (z // 2), 16)
-        other = others[at, :].astype(F32)
-        following = jnp.where(core == 0, edges[1, at, :].astype(F32), other)[half]
-        previous = jnp.where(core == 0, other, edges[0, at, :].astype(F32))[half]
+        half = slice(8 * (z // 2), 8 * (z // 2) + 8)
+        at = pl.ds(128, 16)
+        other = received[at, :].astype(F32)
+        following = jnp.where(core == 0, near[1, at, :].astype(F32), other)[half]
+        previous = jnp.where(core == 0, other, near[0, at, :].astype(F32))[half]
+        if z % 2:
+            following = pltpu.roll(following, 4, 0)
+        else:
+            previous = pltpu.roll(previous, 4, 0)
         rims[0, z] = pair_edges(following, previous)
         rims[1, z] = cluster_edges(following, previous)
-        out = down if z < 2 else up
+        payload = payloads[z // 2]
         own = [x[GROUP * s : GROUP * s + ROWS].astype(BF16) for s in range(4)]
         rim = [x[GROUP * s + ROWS : GROUP * s + GROUP] for s in range(4)]
         if z in (0, 3):
             for i, s in enumerate((1, 2, 0, 3)):
-                out[pl.ds(16 * i, 16), :] = own[s]
-            out[pl.ds(64, 16), :] = jnp.concatenate([rim[1], rim[2]], 0).astype(BF16)
+                payload[16 * i, 16] = own[s]
             lines = (early_down if z < 2 else early_up)[pl.ds(48, 16), :].astype(F32)[8:]
-            out[pl.ds(160, 16), :] = jnp.concatenate([rims[0, z], lines], 0).astype(BF16)
+            packed = packed_rims((rim[1], rim[2], rims[0, z]))
+            payload[64, 16] = jnp.concatenate([packed, lines], 0).astype(BF16)
         else:
-            out[pl.ds(80, 16), :] = own[1]
-            out[pl.ds(96, 16), :] = own[2]
+            payload[80, 16] = own[1]
+            payload[96, 16] = own[2]
+
+    def write(payload, out):
+        for (start, size), value in payload.items():
+            out[pl.ds(start, size), :] = value
+
+    odd = lax.rem(lax.axis_index("depth"), 2)
+
+    @pl.when(odd == 0)
+    def _():
+        write(payloads[0], across_odd)
+        write(payloads[1], across_even)
+
+    @pl.when(odd == 1)
+    def _():
+        write(payloads[0], across_even)
+        write(payloads[1], across_odd)
 
 
 def along_sum(x, matrix):
@@ -225,60 +258,72 @@
             still[f, z] = others[f][:ROWS]
 
 
-def react_kernel(side, spreads, rates, outer, late, still, pairs, rims_own, payload, *refs):
+def react_kernel(step, spreads, rates, outer, late, still, pairs, rims_own, payload, *refs):
     result, near_late, own_late, done, sems = refs[-5:]
+    odd = lax.rem(lax.axis_index("depth"), 2)
+    side = odd if step == 0 else 1 - odd
+
+    def inward(i):
+        return i + side * (3 - 2 * i)
+
+    def pairs_of(z):
+        return pairs[pl.ds(pl.multiple_of(ROWS * z, ROWS), ROWS), :].astype(F32)
 
     def sent(i):
         return payload[pl.ds(16 * i, 16), :].astype(F32)
 
-    rows = sent(10)
-    pair_rim, lines = rows[:8], rows[8:]
+    def known(i):
+        return sent(7 + i)
+
+    packed, lines = sent(4)[:8], sent(4)[8:]
 
     def implanted(i, x):
         line = lines[i : i + 1]
         dose = line[:, 128:129] + line[:, 256:257] + line[:, 384:385]
         return dose * along_sum(x, along_matrix(line[:, :128]))
 
-    rims = sent(4)
-    pair = jnp.concatenate([sent(7), pair_rim], 0)
+    pair = jnp.concatenate([known(0), unpacked_rim(packed, 2)], 0)
     silicon = (pair > 0.0).astype(F32)
     near = [
-        silicon * implanted(0, jnp.concatenate([sent(0), rims[:8]], 0)),
-        silicon * implanted(1, jnp.concatenate([sent(1), rims[8:]], 0)),
+        silicon * implanted(0, jnp.concatenate([sent(0), unpacked_rim(packed, 0)], 0)),
+        silicon * implanted(1, jnp.concatenate([sent(1), unpacked_rim(packed, 1)], 0)),
         pair,
     ]
     silicon = silicon[:ROWS]
     arsenic = silicon * implanted(2, sent(2))
-    clusters = silicon * (sent(8) + implanted(3, sent(3)))
-    far_pair = sent(9)
+    clusters = silicon * (known(1) + implanted(3, sent(3)))
+    far_pair = known(2)
     far_silicon = (far_pair > 0.0).astype(F32)
     far = [far_silicon * implanted(4, sent(5)), far_silicon * implanted(5, sent(6)), far_pair]
     beside = [outer[f, side] for f in range(3)]
-    mobile, _ = substep(spreads, rates, silicon, near, far, beside, arsenic, clusters, ROWS)
-    z = 3 * side
-    own_pair = jnp.concatenate([pairs[tile(z), :].astype(F32), rims_own[0, z]], 0)
+    z = inward(0)
+    own_pair = jnp.concatenate([pairs_of(z), rims_own[0, z]], 0)
     own_silicon = (own_pair > 0.0).astype(F32)
     for f in range(3):
-        near_late[f] = mobile[f]
         own_late[f] = late[f, z] + own_silicon * (spreads[f] * near[f])
 
-    def layer(f, at):
-        if at in (-1, LAYERS):
-            return near_late[f]
-        return own_late[f] if at == z else late[f, at]
-
-    for i in range(2):
-        at = 2 * side + i
-        silicon = (pairs[tile(at), :].astype(F32) > 0.0).astype(F32)
-        centers = [layer(f, at) for f in range(3)]
-        belows = [layer(f, at - 1) for f in range(3)]
-        aboves = [layer(f, at + 1) for f in range(3)]
-        mobile, others = substep(spreads, rates, silicon, centers, belows, aboves, still[0, at], still[1, at], ROWS)
+    def copy(f, i):
+        return pltpu.make_async_copy(done.at[f, i], result.at[f, inward(i)], sems.at[f, i])
+
+    for i in (1, 0):
+        at, beyond = inward(i), inward(i + 1)
+        if i == 0:
+            mobile, _ = substep(spreads, rates, silicon, near, far, beside, arsenic, clusters, ROWS)
+            for f in range(3):
+                near_late[f] = mobile[f]
+        own_silicon = (pairs_of(at) > 0.0).astype(F32)
+        centers = [late[f, at] if i else own_late[f] for f in range(3)]
+        outers = [own_late[f] if i else near_late[f] for f in range(3)]
+        inners = [late[f, beyond] for f in range(3)]
+        mobile, others = substep(
+            spreads, rates, own_silicon, centers, outers, inners, still[0, at], still[1, at], ROWS
+        )
         for f, new in enumerate((others[0], *mobile, others[1])):
             done[f, i] = new
-        pltpu.make_async_copy(done.at[:, i], result.at[:, at], sems.at[i]).start()
-    for i in range(2):
-        pltpu.make_async_copy(done.at[:, i], result.at[:, 2 * side + i], sems.at[i]).wait()
+            copy(f, i).start()
+    for i in (1, 0):
+        for f in range(5):
+            copy(f, i).wait()
 
 
 def moved(array, axis, size, source):
@@ -307,61 +352,45 @@
     def shared(array):
         return lax.all_gather(array, "lat", axis_index_groups=couples)
 
+    core = lax.rem(lax.axis_index("lat"), 2)
     silicon = fin_mask.astype(BF16)
     source = silicon * stopping_power
     pair = silicon * pairs_before
-    edges = [pair[:, :2], clusters_before[:, :1], pair[:, 3:5], clusters_before[:, 15:], pair[:, 14:]]
-    edges = jnp.concatenate(edges, 1).reshape(32, LENGTH)
-    others = moved(edges, "lat", LATS, lanes(-1, 1))
+    source, pair = lax.optimization_barrier((source.reshape(64, LENGTH), pair))
+    mine = shared(source).reshape(128, LENGTH)
+    far = moved(mine, "lat", LATS, lanes(-4, 4))
+    clusters, _ = lax.optimization_barrier((clusters_before, mine))
+    first = [pair[:, :2], clusters[:, :1], clusters[:, :1]]
+    last = [clusters[:, 15:], clusters[:, 15:], pair[:, 14:]]
+    first, last = (jnp.concatenate(rows, 1).reshape(16, LENGTH) for rows in (first, last))
+    outward, inward = jnp.where(core == 0, first, last), jnp.where(core == 0, last, first)
     pair = pair.reshape(64, LENGTH)
-    mine = shared(source.reshape(64, LENGTH)).reshape(128, LENGTH)
-    near = moved(mine, "lat", LATS, lanes(-2, 2))
-    far = moved(mine, "lat", LATS, lanes(-4, 4))
-    corner = jnp.pad(source[:, :2], ((0, 0), (0, 2), (0, 0))).reshape(16, LENGTH)
+    received = moved(jnp.concatenate([mine, outward], 0), "lat", LATS, lanes(-1, 1))
+    corner = jnp.pad(source.reshape(LAYERS, ROWS, LENGTH)[:, :2], ((0, 0), (0, 2), (0, 0))).reshape(16, LENGTH)
     corner = moved(corner, "lat", LATS, lambda i: None if i % 2 == 0 else i + 5)
-    edges, corner = lax.optimization_barrier((edges, corner))
-    edges = shared(edges)
-    early_down, early_up = call(
-        early_kernel,
-        (shape((64, LENGTH), BF16), shape((64, LENGTH), BF16)),
-        (layer_doses, pair, clusters_before, taps_along),
-        scalars=1,
-        scratch=[pltpu.VMEM((16, 128), F32), pltpu.VMEM((32, LENGTH), F32)],
+    across_bands, early_down, early_up = call(
+        prepare_kernel,
+        (shape((LAYERS, 4 * GROUP, 256), F32), shape((64, LENGTH), BF16), shape((64, LENGTH), BF16)),
+        (tilt_shift, layer_doses, taps_across, taps_along, pair, clusters_before),
+        scalars=2,
+        scratch=[pltpu.VMEM((16, 128), F32), pltpu.VMEM((16, 128), F32), pltpu.VMEM((32, LENGTH), F32)],
     )
-    across_bands = call(
-        band_kernel,
-        shape((LAYERS, 4 * GROUP, 256), F32),
-        (tilt_shift, taps_across),
-        scalars=1,
-        scratch=[pltpu.VMEM((16, 128), F32)],
-    )
-    near = shared(near)
+    near = shared(jnp.concatenate([received[:128], inward], 0))
     far, near, early_down, early_up = lax.optimization_barrier((far, near, early_down, early_up))
     far = shared(far)
-    others, far = lax.optimization_barrier((others, far))
-    spread, down, up, rims = call(
+    spread, to_even, to_odd, rims = call(
         across_kernel,
         (
             shape((LAYERS, 4 * GROUP, LENGTH), BF16),
-            shape((176, LENGTH), BF16),
-            shape((176, LENGTH), BF16),
+            shape((160, LENGTH), BF16),
+            shape((160, LENGTH), BF16),
             shape((2, LAYERS, 8, LENGTH), F32),
         ),
-        (
-            mine.reshape(2, 64, LENGTH),
-            near.reshape(2, 128, LENGTH),
-            far,
-            corner,
-            across_bands,
-            edges,
-            others,
-            early_down,
-            early_up,
-        ),
+        (mine.reshape(2, 64, LENGTH), near, received, far, corner, across_bands, early_down, early_up),
         scratch=[pltpu.VMEM((LAYERS, WINDOW, LENGTH), BF16)],
     )
-    below = moved(up, "depth", DEPTHS, lambda i: i - 1)
-    above = moved(down, "depth", DEPTHS, lambda i: i + 1)
+    from_odd = moved(to_odd, "depth", DEPTHS, lanes(-1, 1))
+    from_even = moved(to_even, "depth", DEPTHS, lanes(1, -1))
     outer, late, still = call(
         along_kernel,
         (
@@ -381,20 +410,20 @@
         pltpu.VMEM((3, ROWS, LENGTH), F32),
         pltpu.VMEM((3, GROUP, LENGTH), F32),
         pltpu.VMEM((5, 2, ROWS, LENGTH), F32),
-        pltpu.SemaphoreType.DMA((2,)),
+        pltpu.SemaphoreType.DMA((5, 2)),
     ]
     given = (diffusivity, reaction_rates, outer, late, still, pair, rims)
-    for side, payload in enumerate((below, above)):
-        args = (*given, payload) if side == 0 else (*given, payload, result)
+    for step, payload in enumerate((from_odd, from_even)):
+        args = (*given, payload) if step == 0 else (*given, payload, result)
         result = call(
-            functools.partial(react_kernel, side),
+            functools.partial(react_kernel, step),
             shape((5, LAYERS, ROWS, LENGTH), F32),
             args,
             scalars=2,
             hbm=(8,),
             hbm_out=True,
             scratch=scratch,
-            aliases={8: 0} if side else {},
+            aliases={8: 0} if step else {},
         )
     return result
 

time: 50.6 us -> 47.1 us (0.931)
  the two profiles are of different devices: /device:TPU:62 before, /device:TPU:320 now
where the time goes in v3:
time: 47.1 us; the launch traced here: 46.8 us
  starting transfers between devices  20.1 us (43%)
  waiting for transfers between devices  9.54 us (20%)
  Pallas kernels  8.05 us (17%)
  blocking collectives  6.39 us (14%)
  other arithmetic  1.43 us (3%)
  local copies, waits for them, and re-layouts  1.02 us (2%)
    ppermute x5, starting transfers between devices, moved(): return lax.ppermute(array, axis, route)  20.1 us
    ppermute x5, waiting for transfers between devices, moved(): return lax.ppermute(array, axis, route)  9.54 us
    pallas_call x5, Pallas kernels, call(): pl.pallas_call(kernel, out_shape=outs, in_specs=[pl.BlockSpec(memory_spac...  8.05 us
    all_gather x3, blocking collectives, shared(): return lax.all_gather(array, 'lat', axis_index_groups=couples)  6.39 us
    mul x1, other arithmetic, body(): pair = silicon * pairs_before  1.17 us
  transfers between devices with their start and end apart: 5, of which 3 were waited for; matrix products, arithmetic and copies ran while one was open for 0% of the time, Pallas kernels for 12%

profile of v3, /device:TPU:320, one launch (start us, length us, event | category | flops | bytes accessed | tf_op | source)
XLA Modules:
  0.0 46.8 jit_solution(18116466264924187253)
XLA Ops:
  0.0 0.0 copy-start.7
  0.0 0.0 copy-start
  0.0 0.0 copy-start.2
  0.0 0.0 copy-start.1
  0.0 0.0 copy-start.6
  0.0 0.0 copy-start.5
  0.0 1.2 %convert_multiply_fusion = (bf16[4,16,1024]{2,1,0:T(8,128)(2,1)S(1)}, bf16[4,16,1024]{2,1,0:T(8,128)(2,1)S(1)}) fusion(bf16[4,16,1024]{2,1,0:T(8,128)(2,1)} %param.12, s32[4,16,1024]{2,1,0:T(8,128)} %param.10, bf16[4,16,1024]{2,1,0:T(8,128)(2,1)} %param.11), kind=kLoop, calls=%fused_computation.2 | loop fusion | flops 196608 | bytes 786432 | tf_op jit(solution)/shard_map/mul | solution.py:358
  1.3 2.0 %all-gather = bf16[128,1024]{1,0:T(8,128)(2,1)S(1)} all-gather(bf16[64,1024]{1,0:T(8,128)(2,1)S(1)} %bitcast.13), channel_id=2, replica_groups={{0,1},{2,3},{4,5},{6,7},{8,9},{10,11},{12,13},{14,15},{16,17},{18,19},{..., dimensions={0}, use_global_device_ids=true | all-gather | bytes 393216 | tf_op jit(solution)/shard_map/all_gather | solution.py:353
  3.3 0.9 %fusion.1 = (bf16[4,1,1024]{2,1,0:T(2,128)(2,1)S(1)}, bf16[4,1,1024]{2,1,0:T(2,128)(2,1)S(1)}) fusion(bf16[4,16,1024]{2,1,0:T(8,128)(2,1)} %clusters.3), kind=kLoop, calls=%fused_computation.10 | loop fusion | bytes 32768 | tf_op jit(solution)/shard_map/slice | solution.py:363
  4.2 0.1 broadcast_select_fusion.1
  4.3 4.2 %collective-permute-start.1 = (bf16[144,1024]{1,0:T(8,128)(2,1)S(1)}, bf16[144,1024]{1,0:T(8,128)(2,1)S(1)}, u32[]{:S(2)}, u32[]{:S(2)}) collective-permute-start(bf16[144,1024]{1,0:T(8,128)(2,1)S(1)} %pad_maximum_fusion), channel_id=1, source_target_pairs={{2,1},{1,2},{4,3},{3,4},{6,5},{5,6},{8,7},{7,8},{10,9},{9,10},{12,... | collective-permute-start | bytes 884744 | tf_op jit(solution)/shard_map/ppermute | solution.py:331
  8.6 2.4 %collective-permute-start = (bf16[128,1024]{1,0:T(8,128)(2,1)S(1)}, bf16[128,1024]{1,0:T(8,128)(2,1)S(1)}, u32[]{:S(2)}, u32[]{:S(2)}) collective-permute-start(bf16[128,1024]{1,0:T(8,128)(2,1)S(1)} %all-gather), channel_id=1, source_target_pairs={{5,1},{7,3},{0,4},{9,5},{2,6},{11,7},{4,8},{13,9},{6,10},{15,11},{... | collective-permute-start | bytes 786440 | tf_op jit(solution)/shard_map/ppermute | solution.py:331
  11.0 0.0 copy-done.7
  11.0 0.1 slice_select_fusion
  11.1 6.7 %collective-permute-start.2 = (bf16[16,1024]{1,0:T(8,128)(2,1)S(1)}, bf16[16,1024]{1,0:T(8,128)(2,1)S(1)}, u32[]{:S(2)}, u32[]{:S(2)}) collective-permute-start(bf16[16,1024]{1,0:T(8,128)(2,1)S(1)} %reshape.25), channel_id=1, source_target_pairs={{6,1},{8,3},{10,5},{12,7},{14,9},{16,11},{18,13},{20,15},{22,17},{... | collective-permute-start | bytes 98312 | tf_op jit(solution)/shard_map/ppermute | solution.py:331
  17.8 0.0 copy-done
  17.8 0.0 copy-done.2
  17.8 0.0 copy-done.1
  17.8 0.0 copy-done.6
  17.9 0.0 copy-done.5
  17.9 1.1 %shard_map.100 = (f32[4,96,256]{2,1,0:T(8,128)S(1)}, bf16[64,1024]{1,0:T(8,128)(2,1)S(1)}, bf16[64,1024]{1,0:T(8,128)(2,1)S(1)}) custom-call(s32[4]{0:T(128)S(1)} %copy-done.6, f32[4,4]{1,0:T(4,128)S(1)} %copy-done.2, bf16[4,4,97]{2,1,0:T(4,128)(2,1)S(1)} %copy-done.5, bf16[4,4,97]{2,1,0:T(4,128)(2,1)S(1)} %copy-done.1, bf16[64,1024]{1,0:T(8,128)(2,1)S(1)} %bitcast.6, ...), custom_call_target="tpu_custom_call" | custom-call | flops 1000000 | bytes 2000000 | tf_op jit(solution)/shard_map/pallas_call | solution.py:29
  19.0 0.0 collective-permute-done.1.received
  19.1 2.2 %all-gather.1 = bf16[288,1024]{1,0:T(8,128)(2,1)S(1)} all-gather(bf16[144,1024]{1,0:T(8,128)(2,1)S(1)} %pad_maximum_fusion.1), channel_id=3, replica_groups={{0,1},{2,3},{4,5},{6,7},{8,9},{10,11},{12,13},{14,15},{16,17},{18,19},{..., dimensions={0}, use_global_device_ids=true | all-gather | bytes 884736 | tf_op jit(solution)/shard_map/all_gather | solution.py:353
  21.3 4.7 %collective-permute-done = bf16[128,1024]{1,0:T(8,128)(2,1)S(1)} collective-permute-done((bf16[128,1024]{1,0:T(8,128)(2,1)S(1)}, bf16[128,1024]{1,0:T(8,128)(2,1)S(1)}, u32[]{:S(2)}, u32[]{:S(2)}) %collective-permute-start) | collective-permute-done | bytes 262176 | tf_op jit(solution)/shard_map/ppermute | solution.py:331
  26.0 2.2 %all-gather.2 = bf16[256,1024]{1,0:T(8,128)(2,1)S(1)} all-gather(bf16[128,1024]{1,0:T(8,128)(2,1)S(1)} %collective-permute-done), channel_id=4, replica_groups={{0,1},{2,3},{4,5},{6,7},{8,9},{10,11},{12,13},{14,15},{16,17},{18,19},{..., dimensions={0}, use_global_device_ids=true | all-gather | bytes 786432 | tf_op jit(solution)/shard_map/all_gather | solution.py:353
  28.2 0.0 copy-start.3
  28.2 0.0 copy-start.4
  28.2 0.0 collective-permute-done.2.corner
  28.2 0.4 shard_map.101
  28.7 4.6 %collective-permute-start.4 = (bf16[160,1024]{1,0:T(8,128)(2,1)S(1)}, bf16[160,1024]{1,0:T(8,128)(2,1)S(1)}, u32[]{:S(2)}, u32[]{:S(2)}) collective-permute-start(bf16[160,1024]{1,0:T(8,128)(2,1)S(1)} %get-tuple-element.38), channel_id=1, source_target_pairs={{128,64},{64,128},{256,192},{192,256},{384,320},{320,384},{129,65}... | collective-permute-start | bytes 983048 | tf_op jit(solution)/shard_map/ppermute | solution.py:331
  33.3 2.2 %collective-permute-start.3 = (bf16[160,1024]{1,0:T(8,128)(2,1)S(1)}, bf16[160,1024]{1,0:T(8,128)(2,1)S(1)}, u32[]{:S(2)}, u32[]{:S(2)}) collective-permute-start(bf16[160,1024]{1,0:T(8,128)(2,1)S(1)} %get-tuple-element.37), channel_id=1, source_target_pairs={{64,0},{0,64},{192,128},{128,192},{320,256},{256,320},{448,384},{3... | collective-permute-start | bytes 983048 | tf_op jit(solution)/shard_map/ppermute | solution.py:331
  35.5 0.0 copy-done.3
  35.5 0.0 copy-done.4
  35.5 2.2 %shard_map.102 = (f32[3,2,16,1024]{3,2,1,0:T(8,128)S(1)}, f32[3,4,24,1024]{3,2,1,0:T(8,128)S(1)}, f32[2,4,16,1024]{3,2,1,0:T(8,128)S(1)}) custom-call(f32[3]{0:T(128)S(1)} %copy-done.3, f32[5]{0:T(128)S(1)} %copy-done.4, f32[4,4]{1,0:T(4,128)S(1)} %copy-done.2, bf16[4,96,1024]{2,1,0:T(8,128)(2,1)S(1)} %get-tuple-element.32.spread, ...), custom_call_target="tpu_custom_call" | custom-call | flops 1000000 | bytes 2000000 | tf_op jit(solution)/shard_map/pallas_call | solution.py:29
  37.7 4.7 %collective-permute-done.4.payload = bf16[160,1024]{1,0:T(8,128)(2,1)S(1)} collective-permute-done((bf16[160,1024]{1,0:T(8,128)(2,1)S(1)}, bf16[160,1024]{1,0:T(8,128)(2,1)S(1)}, u32[]{:S(2)}, u32[]{:S(2)}) %collective-permute-start.4) | collective-permute-done | bytes 327712 | tf_op jit(solution)/shard_map/ppermute | solution.py:331
  42.4 2.1 %shard_map.103.refs_0_ = f32[5,4,16,1024]{3,2,1,0:T(8,128)} custom-call(f32[3]{0:T(128)S(1)} %copy-done.3, f32[5]{0:T(128)S(1)} %copy-done.4, f32[3,2,16,1024]{3,2,1,0:T(8,128)S(1)} %get-tuple-element.34.outer, f32[3,4,24,1024]{3,2,1,0:T(8,128)S(1)} %get-tuple-element.35.late, f32[2,4,16,1024]{3,2,1,0:T(8,128)S(1)} %get-tuple-element.36.still, ...), custom_call_target="tpu_custom_call" | custom-call | flops 1000000 | bytes 2000000 | tf_op jit(solution)/shard_map/pallas_call | solution.py:29
  44.5 0.1 collective-permute-done.3.payload
  44.7 2.1 %shard_map.104 = f32[5,4,16,1024]{3,2,1,0:T(8,128)} custom-call(f32[3]{0:T(128)S(1)} %copy-done.3, f32[5]{0:T(128)S(1)} %copy-done.4, f32[3,2,16,1024]{3,2,1,0:T(8,128)S(1)} %get-tuple-element.34.outer, f32[3,4,24,1024]{3,2,1,0:T(8,128)S(1)} %get-tuple-element.35.late, ...), custom_call_target="tpu_custom_call", output_to_operand_aliasing={{}: (8, {})} | custom-call | flops 1000000 | bytes 2000000 | tf_op jit(solution)/shard_map/pallas_call | solution.py:29
  (7 shorter events, 0.1 us)
Async XLA Ops:
  0.0 11.0 %copy-start.7 = (pred[4]{0:T(512)(128)(4,1)S(1)}, pred[4]{0:T(512)(128)(4,1)}, u32[]{:S(2)}) copy-start(pred[4]{0:T(512)(128)(4,1)} %constant.12.clone.1) | copy-start | bytes 16
  0.0 17.8 %copy-start = (bf16[4,16,1024]{2,1,0:T(8,128)(2,1)S(1)}, bf16[4,16,1024]{2,1,0:T(8,128)(2,1)}, u32[]{:S(2)}) copy-start(bf16[4,16,1024]{2,1,0:T(8,128)(2,1)} %clusters.3) | copy-start | bytes 393220
  0.0 17.8 %copy-start.2 = (f32[4,4]{1,0:T(4,128)S(1)}, f32[4,4]{1,0:T(4,128)}, u32[]{:S(2)}) copy-start(f32[4,4]{1,0:T(4,128)} %doses.3) | copy-start | bytes 196
  0.0 17.8 %copy-start.1 = (bf16[4,4,97]{2,1,0:T(4,128)(2,1)S(1)}, bf16[4,4,97]{2,1,0:T(4,128)(2,1)}, u32[]{:S(2)}) copy-start(bf16[4,4,97]{2,1,0:T(4,128)(2,1)} %taps_along.3) | copy-start | bytes 9316
  0.0 17.8 %copy-start.6 = (s32[4]{0:T(128)S(1)}, s32[4]{0:T(128)}, u32[]{:S(2)}) copy-start(s32[4]{0:T(128)} %tilt.1) | copy-start | bytes 52
  0.0 17.8 %copy-start.5 = (bf16[4,4,97]{2,1,0:T(4,128)(2,1)S(1)}, bf16[4,4,97]{2,1,0:T(4,128)(2,1)}, u32[]{:S(2)}) copy-start(bf16[4,4,97]{2,1,0:T(4,128)(2,1)} %taps_across.1) | copy-start | bytes 9316
  4.3 14.7 %collective-permute-start.1 = (bf16[144,1024]{1,0:T(8,128)(2,1)S(1)}, bf16[144,1024]{1,0:T(8,128)(2,1)S(1)}, u32[]{:S(2)}, u32[]{:S(2)}) collective-permute-start(bf16[144,1024]{1,0:T(8,128)(2,1)S(1)} %pad_maximum_fusion), channel_id=1, source_target_pairs={{2,1},{1,2},{4,3},{3,4},{6,5},{5,6},{8,7},{7,8},{10,9},{9,10},{12,... | collective-permute-start | bytes 884744 | tf_op jit(solution)/shard_map/ppermute | solution.py:331
  8.6 17.5 %collective-permute-start = (bf16[128,1024]{1,0:T(8,128)(2,1)S(1)}, bf16[128,1024]{1,0:T(8,128)(2,1)S(1)}, u32[]{:S(2)}, u32[]{:S(2)}) collective-permute-start(bf16[128,1024]{1,0:T(8,128)(2,1)S(1)} %all-gather), channel_id=1, source_target_pairs={{5,1},{7,3},{0,4},{9,5},{2,6},{11,7},{4,8},{13,9},{6,10},{15,11},{... | collective-permute-start | bytes 786440 | tf_op jit(solution)/shard_map/ppermute | solution.py:331
  11.1 17.1 %collective-permute-start.2 = (bf16[16,1024]{1,0:T(8,128)(2,1)S(1)}, bf16[16,1024]{1,0:T(8,128)(2,1)S(1)}, u32[]{:S(2)}, u32[]{:S(2)}) collective-permute-start(bf16[16,1024]{1,0:T(8,128)(2,1)S(1)} %reshape.25), channel_id=1, source_target_pairs={{6,1},{8,3},{10,5},{12,7},{14,9},{16,11},{18,13},{20,15},{22,17},{... | collective-permute-start | bytes 98312 | tf_op jit(solution)/shard_map/ppermute | solution.py:331
  28.2 7.3 %copy-start.3 = (f32[3]{0:T(128)S(1)}, f32[3]{0:T(128)}, u32[]{:S(2)}) copy-start(f32[3]{0:T(128)} %spreads.5) | copy-start | bytes 40
  28.2 7.3 %copy-start.4 = (f32[5]{0:T(128)S(1)}, f32[5]{0:T(128)}, u32[]{:S(2)}) copy-start(f32[5]{0:T(128)} %rates.5) | copy-start | bytes 64
  28.7 13.8 %collective-permute-start.4 = (bf16[160,1024]{1,0:T(8,128)(2,1)S(1)}, bf16[160,1024]{1,0:T(8,128)(2,1)S(1)}, u32[]{:S(2)}, u32[]{:S(2)}) collective-permute-start(bf16[160,1024]{1,0:T(8,128)(2,1)S(1)} %get-tuple-element.38), channel_id=1, source_target_pairs={{128,64},{64,128},{256,192},{192,256},{384,320},{320,384},{129,65}... | collective-permute-start | bytes 983048 | tf_op jit(solution)/shard_map/ppermute | solution.py:331
  33.3 11.4 %collective-permute-start.3 = (bf16[160,1024]{1,0:T(8,128)(2,1)S(1)}, bf16[160,1024]{1,0:T(8,128)(2,1)S(1)}, u32[]{:S(2)}, u32[]{:S(2)}) collective-permute-start(bf16[160,1024]{1,0:T(8,128)(2,1)S(1)} %get-tuple-element.37), channel_id=1, source_target_pairs={{64,0},{0,64},{192,128},{128,192},{320,256},{256,320},{448,384},{3... | collective-permute-start | bytes 983048 | tf_op jit(solution)/shard_map/ppermute | solution.py:331

commit v4 on v3

--- a/solution.py
+++ b/solution.py
@@ -21,7 +21,7 @@
 MEMORY = 32 * 1024 * 1024
 
 
-def call(kernel, outs, args, scalars=0, hbm=(), hbm_out=False, scratch=(), aliases={}, flops=1000000, size=2000000):
+def call(kernel, outs, args, scalars=0, hbm=(), hbm_out=False, scratch=(), flops=1000000, size=2000000):
     def space(i):
         return pltpu.SMEM if i < scalars else pltpu.HBM if i in hbm else pltpu.VMEM
 
@@ -32,7 +32,6 @@
         in_specs=[pl.BlockSpec(memory_space=space(i)) for i in range(len(args))],
         out_specs=jax.tree.map(lambda _: pl.BlockSpec(memory_space=out_space), outs),
         scratch_shapes=list(scratch),
-        input_output_aliases=aliases,
         compiler_params=pltpu.CompilerParams(vmem_limit_bytes=MEMORY),
         cost_estimate=pl.CostEstimate(flops=flops, bytes_accessed=size, transcendentals=0),
     )(*args)
@@ -77,7 +76,7 @@
 SENT = ((1, 0), (2, 0), (0, 0), (3, 0), (1, 1), (2, 1))
 
 
-def prepare_kernel(tilt, doses, taps_across, taps_along, pair, clusters, across_bands, down, up, across, taps, lines):
+def prepare_kernel(tilt, doses, taps_across, taps_along, pair, clusters, across_bands, down, up, early_even, across, taps, lines):
     wide_taps(taps_across, across)
     lane = lax.broadcasted_iota(jnp.int32, (GROUP, 256), 1)
     group = lax.broadcasted_iota(jnp.int32, (8, 256), 0)
@@ -109,6 +108,15 @@
         out[pl.ds(16, 16), :] = clusters[near]
         out[pl.ds(32, 16), :] = pair[tile(far), :]
         out[pl.ds(48, 16), :] = lines[pl.ds(16 * side, 16), :].astype(BF16)
+    odd = lax.rem(lax.axis_index("depth"), 2)
+
+    @pl.when(odd == 0)
+    def _():
+        early_even[...] = up[pl.ds(0, 48), :]
+
+    @pl.when(odd == 1)
+    def _():
+        early_even[...] = down[pl.ds(0, 48), :]
 
 
 def packed_rims(fields):
@@ -169,7 +177,8 @@
 
     def write(payload, out):
         for (start, size), value in payload.items():
-            out[pl.ds(start, size), :] = value
+            if start < out.shape[0]:
+                out[pl.ds(start, size), :] = value
 
     odd = lax.rem(lax.axis_index("depth"), 2)
 
@@ -227,7 +236,7 @@
 NONE = (None, None, None)
 
 
-def along_kernel(spreads, rates, doses, spread, taps_along, pairs, clusters, rims, outer, late, still, fields, fixed, along):
+def along_kernel(spreads, rates, doses, spread, taps_along, pairs, clusters, rims, outer, late, still, inner, fields, fixed, along):
     wide_taps(taps_along, along)
     for z in range(LAYERS):
         x = spread[z].astype(F32)
@@ -256,16 +265,34 @@
                 outer[f, z // 3] = fields[f, z, :ROWS]
         for f in range(2):
             still[f, z] = others[f][:ROWS]
-
-
-def react_kernel(step, spreads, rates, outer, late, still, pairs, rims_own, payload, *refs):
-    result, near_late, own_late, done, sems = refs[-5:]
+    for z in (1, 2):
+        silicon = (pairs[tile(z), :].astype(F32) > 0.0).astype(F32)
+        centers, belows, aboves = ([late[f, at] for f in range(3)] for at in (z, z - 1, z + 1))
+        mobile, others = substep(spreads, rates, silicon, centers, belows, aboves, still[0, z], still[1, z], ROWS)
+        for f, new in enumerate((others[0], *mobile, others[1])):
+            inner[f, z - 1] = new
+
+
+def react_kernel(step, spreads, rates, outer, late, still, inner, pairs, rims_own, payload, *refs):
+    if step == 0:
+        done, near_late, own_late = refs
+    else:
+        early, earlier, result, near_late, own_late, done, sems = refs
     odd = lax.rem(lax.axis_index("depth"), 2)
     side = odd if step == 0 else 1 - odd
 
     def inward(i):
         return i + side * (3 - 2 * i)
 
+    def copy(half, f, i):
+        at = inward(i) if half else 3 - inward(i)
+        return pltpu.make_async_copy((earlier, done)[half].at[f, i], result.at[f, at], sems.at[half, f, i])
+
+    if step == 1:
+        for i in range(2):
+            for f in range(5):
+                copy(0, f, i).start()
+
     def pairs_of(z):
         return pairs[pl.ds(pl.multiple_of(ROWS * z, ROWS), ROWS), :].astype(F32)
 
@@ -273,7 +300,7 @@
         return payload[pl.ds(16 * i, 16), :].astype(F32)
 
     def known(i):
-        return sent(7 + i)
+        return early[pl.ds(16 * i, 16), :].astype(F32) if step else sent(7 + i)
 
     packed, lines = sent(4)[:8], sent(4)[8:]
 
@@ -299,31 +326,34 @@
     z = inward(0)
     own_pair = jnp.concatenate([pairs_of(z), rims_own[0, z]], 0)
     own_silicon = (own_pair > 0.0).astype(F32)
+    inner_silicon = (pairs_of(inward(1)) > 0.0).astype(F32)
     for f in range(3):
-        own_late[f] = late[f, z] + own_silicon * (spreads[f] * near[f])
-
-    def copy(f, i):
-        return pltpu.make_async_copy(done.at[f, i], result.at[f, inward(i)], sems.at[f, i])
-
-    for i in (1, 0):
-        at, beyond = inward(i), inward(i + 1)
-        if i == 0:
-            mobile, _ = substep(spreads, rates, silicon, near, far, beside, arsenic, clusters, ROWS)
-            for f in range(3):
-                near_late[f] = mobile[f]
-        own_silicon = (pairs_of(at) > 0.0).astype(F32)
-        centers = [late[f, at] if i else own_late[f] for f in range(3)]
-        outers = [own_late[f] if i else near_late[f] for f in range(3)]
-        inners = [late[f, beyond] for f in range(3)]
-        mobile, others = substep(
-            spreads, rates, own_silicon, centers, outers, inners, still[0, at], still[1, at], ROWS
-        )
-        for f, new in enumerate((others[0], *mobile, others[1])):
-            done[f, i] = new
-            copy(f, i).start()
-    for i in (1, 0):
+        change = own_silicon * (spreads[f] * near[f])
+        own_late[f] = late[f, z] + change
+        done[f + 1, 1] = inner[f + 1, side] + inner_silicon * (spreads[f] * change[:ROWS])
+    for f in (0, 4):
+        done[f, 1] = inner[f, side]
+    if step == 1:
         for f in range(5):
-            copy(f, i).wait()
+            copy(1, f, 1).start()
+    mobile, _ = substep(spreads, rates, silicon, near, far, beside, arsenic, clusters, ROWS)
+    for f in range(3):
+        near_late[f] = mobile[f]
+    centers = [own_late[f] for f in range(3)]
+    outers = [near_late[f] for f in range(3)]
+    inners = [late[f, inward(1)] for f in range(3)]
+    mobile, others = substep(
+        spreads, rates, own_silicon[:ROWS], centers, outers, inners, still[0, z], still[1, z], ROWS
+    )
+    for f, new in enumerate((others[0], *mobile, others[1])):
+        done[f, 0] = new
+        if step == 1:
+            copy(1, f, 0).start()
+    if step == 1:
+        for half in range(2):
+            for i in range(2):
+                for f in range(5):
+                    copy(half, f, i).wait()
 
 
 def moved(array, axis, size, source):
@@ -356,10 +386,10 @@
     silicon = fin_mask.astype(BF16)
     source = silicon * stopping_power
     pair = silicon * pairs_before
-    source, pair = lax.optimization_barrier((source.reshape(64, LENGTH), pair))
+    clusters = silicon * clusters_before
+    source, pair, clusters = lax.optimization_barrier((source.reshape(64, LENGTH), pair, clusters))
     mine = shared(source).reshape(128, LENGTH)
     far = moved(mine, "lat", LATS, lanes(-4, 4))
-    clusters, _ = lax.optimization_barrier((clusters_before, mine))
     first = [pair[:, :2], clusters[:, :1], clusters[:, :1]]
     last = [clusters[:, 15:], clusters[:, 15:], pair[:, 14:]]
     first, last = (jnp.concatenate(rows, 1).reshape(16, LENGTH) for rows in (first, last))
@@ -368,13 +398,19 @@
     received = moved(jnp.concatenate([mine, outward], 0), "lat", LATS, lanes(-1, 1))
     corner = jnp.pad(source.reshape(LAYERS, ROWS, LENGTH)[:, :2], ((0, 0), (0, 2), (0, 0))).reshape(16, LENGTH)
     corner = moved(corner, "lat", LATS, lambda i: None if i % 2 == 0 else i + 5)
-    across_bands, early_down, early_up = call(
+    across_bands, early_down, early_up, early_even = call(
         prepare_kernel,
-        (shape((LAYERS, 4 * GROUP, 256), F32), shape((64, LENGTH), BF16), shape((64, LENGTH), BF16)),
-        (tilt_shift, layer_doses, taps_across, taps_along, pair, clusters_before),
+        (
+            shape((LAYERS, 4 * GROUP, 256), F32),
+            shape((64, LENGTH), BF16),
+            shape((64, LENGTH), BF16),
+            shape((48, LENGTH), BF16),
+        ),
+        (tilt_shift, layer_doses, taps_across, taps_along, pair, clusters),
         scalars=2,
         scratch=[pltpu.VMEM((16, 128), F32), pltpu.VMEM((16, 128), F32), pltpu.VMEM((32, LENGTH), F32)],
     )
+    early_even = moved(early_even, "depth", DEPTHS, lanes(1, -1))
     near = shared(jnp.concatenate([received[:128], inward], 0))
     far, near, early_down, early_up = lax.optimization_barrier((far, near, early_down, early_up))
     far = shared(far)
@@ -382,23 +418,25 @@
         across_kernel,
         (
             shape((LAYERS, 4 * GROUP, LENGTH), BF16),
-            shape((160, LENGTH), BF16),
+            shape((112, LENGTH), BF16),
             shape((160, LENGTH), BF16),
             shape((2, LAYERS, 8, LENGTH), F32),
         ),
         (mine.reshape(2, 64, LENGTH), near, received, far, corner, across_bands, early_down, early_up),
         scratch=[pltpu.VMEM((LAYERS, WINDOW, LENGTH), BF16)],
     )
+    to_even, to_odd, early_even = lax.optimization_barrier((to_even, to_odd, early_even))
     from_odd = moved(to_odd, "depth", DEPTHS, lanes(-1, 1))
     from_even = moved(to_even, "depth", DEPTHS, lanes(1, -1))
-    outer, late, still = call(
+    outer, late, still, inner = call(
         along_kernel,
         (
             shape((3, 2, ROWS, LENGTH), F32),
             shape((3, LAYERS, GROUP, LENGTH), F32),
             shape((2, LAYERS, ROWS, LENGTH), F32),
+            shape((5, 2, ROWS, LENGTH), F32),
         ),
-        (diffusivity, reaction_rates, layer_doses, spread, taps_along, pair, clusters_before, rims),
+        (diffusivity, reaction_rates, layer_doses, spread, taps_along, pair, clusters, rims),
         scalars=3,
         scratch=[
             pltpu.VMEM((3, LAYERS, GROUP, LENGTH), F32),
@@ -406,26 +444,24 @@
             pltpu.VMEM((16, 128), F32),
         ],
     )
-    scratch = [
-        pltpu.VMEM((3, ROWS, LENGTH), F32),
-        pltpu.VMEM((3, GROUP, LENGTH), F32),
-        pltpu.VMEM((5, 2, ROWS, LENGTH), F32),
-        pltpu.SemaphoreType.DMA((5, 2)),
-    ]
-    given = (diffusivity, reaction_rates, outer, late, still, pair, rims)
-    for step, payload in enumerate((from_odd, from_even)):
-        args = (*given, payload) if step == 0 else (*given, payload, result)
-        result = call(
-            functools.partial(react_kernel, step),
-            shape((5, LAYERS, ROWS, LENGTH), F32),
-            args,
-            scalars=2,
-            hbm=(8,),
-            hbm_out=True,
-            scratch=scratch,
-            aliases={8: 0} if step else {},
-        )
-    return result
+    given = (diffusivity, reaction_rates, outer, late, still, inner, pair, rims)
+    scratch = [pltpu.VMEM((3, ROWS, LENGTH), F32), pltpu.VMEM((3, GROUP, LENGTH), F32)]
+    half = shape((5, 2, ROWS, LENGTH), F32)
+    earlier = call(
+        functools.partial(react_kernel, 0),
+        half,
+        (*given, from_odd),
+        scalars=2,
+        scratch=scratch,
+    )
+    return call(
+        functools.partial(react_kernel, 1),
+        shape((5, LAYERS, ROWS, LENGTH), F32),
+        (*given, from_even, early_even, earlier),
+        scalars=2,
+        hbm_out=True,
+        scratch=[*scratch, pltpu.VMEM(half.shape, F32), pltpu.SemaphoreType.DMA((2, 5, 2))],
+    )
 
 
 def solution(mesh):

time: 47.1 us -> 45.2 us (0.960)
  waiting for transfers between devices: 9.54 us -> 5.64 us
  starting transfers between devices: 20.1 us -> 23.5 us
  local copies, waits for them, and re-layouts: 1.02 us -> 0.15 us
  Pallas kernels: 8.05 us -> 7.57 us
    ppermute x5 -> x6, waiting for transfers between devices: 9.54 us -> 5.64 us  [moved(): return lax.ppermute(array, axis, route)]
    ppermute x5 -> x6, starting transfers between devices: 20.1 us -> 23.5 us  [moved(): return lax.ppermute(array, axis, route)]
    slice x2, local copies, waits for them, and re-layouts: 0.93 us -> 0.06 us  [body(): first = [pair[:, :2], clusters[:, :1], clusters[:, :1]]]
    pallas_call x5, Pallas kernels: 8.05 us -> 7.57 us  [call(): pl.pallas_call(kernel, out_shape=outs, in_specs=[pl.BlockSpec(memory_spac...]
  transfers between devices with their start and end apart: 5 -> 6, of which waited for: 3 -> 2; matrix products, arithmetic and copies ran while one was open for 0% -> 0% of each run, Pallas kernels for 12% -> 12%
where the time goes in v4:
time: 45.2 us; the launch traced here: 44.9 us
  starting transfers between devices  23.5 us (52%)
  Pallas kernels  7.57 us (17%)
  blocking collectives  6.39 us (14%)
  waiting for transfers between devices  5.64 us (12%)
  other arithmetic  1.45 us (3%)
    ppermute x6, starting transfers between devices, moved(): return lax.ppermute(array, axis, route)  23.5 us
    pallas_call x5, Pallas kernels, call(): pl.pallas_call(kernel, out_shape=outs, in_specs=[pl.BlockSpec(memory_spac...  7.57 us
    all_gather x3, blocking collectives, shared(): return lax.all_gather(array, 'lat', axis_index_groups=couples)  6.39 us
    ppermute x6, waiting for transfers between devices, moved(): return lax.ppermute(array, axis, route)  5.64 us
    mul x1, other arithmetic, body(): clusters = silicon * clusters_before  1.19 us
  transfers between devices with their start and end apart: 6, of which 2 were waited for; matrix products, arithmetic and copies ran while one was open for 0% of the time, Pallas kernels for 12%

profile of v4, /device:TPU:320, one launch (start us, length us, event | category | flops | bytes accessed | tf_op | source)
XLA Modules:
  0.0 44.9 jit_solution(10549664904694287723)
XLA Ops:
  0.0 0.0 copy-start.6
  0.0 0.0 copy-start.1
  0.0 0.0 copy-start
  0.0 0.0 copy-start.5
  0.0 0.0 copy-start.4
  0.0 1.2 %convert_multiply_fusion = (bf16[4,16,1024]{2,1,0:T(8,128)(2,1)S(1)}, bf16[4,16,1024]{2,1,0:T(8,128)(2,1)S(1)}, bf16[4,16,1024]{2,1,0:T(8,128)(2,1)S(1)}) fusion(bf16[4,16,1024]{2,1,0:T(8,128)(2,1)} %param.13, s32[4,16,1024]{2,1,0:T(8,128)} %param.10, bf16[4,16,1024]{2,1,0:T(8,128)(2,1)} %param.12, bf16[4,16,1024]{2,1,0:T(8,128)(2,1)} %param.11), kind=kLoop, calls=%fused_computation.7 | loop fusion | flops 262144 | bytes 1048576 | tf_op jit(solution)/shard_map/mul | solution.py:389
  1.3 0.1 broadcast_select_fusion.1
  1.5 2.0 %all-gather = bf16[128,1024]{1,0:T(8,128)(2,1)S(1)} all-gather(bf16[64,1024]{1,0:T(8,128)(2,1)S(1)} %bitcast.13), channel_id=2, replica_groups={{0,1},{2,3},{4,5},{6,7},{8,9},{10,11},{12,13},{14,15},{16,17},{18,19},{..., dimensions={0}, use_global_device_ids=true | all-gather | bytes 393216 | tf_op jit(solution)/shard_map/all_gather | solution.py:383
  3.5 4.2 %collective-permute-start.1 = (bf16[144,1024]{1,0:T(8,128)(2,1)S(1)}, bf16[144,1024]{1,0:T(8,128)(2,1)S(1)}, u32[]{:S(2)}, u32[]{:S(2)}) collective-permute-start(bf16[144,1024]{1,0:T(8,128)(2,1)S(1)} %pad_maximum_fusion), channel_id=1, source_target_pairs={{2,1},{1,2},{4,3},{3,4},{6,5},{5,6},{8,7},{7,8},{10,9},{9,10},{12,... | collective-permute-start | bytes 884744 | tf_op jit(solution)/shard_map/ppermute | solution.py:361
  7.7 2.4 %collective-permute-start = (bf16[128,1024]{1,0:T(8,128)(2,1)S(1)}, bf16[128,1024]{1,0:T(8,128)(2,1)S(1)}, u32[]{:S(2)}, u32[]{:S(2)}) collective-permute-start(bf16[128,1024]{1,0:T(8,128)(2,1)S(1)} %all-gather), channel_id=1, source_target_pairs={{5,1},{7,3},{0,4},{9,5},{2,6},{11,7},{4,8},{13,9},{6,10},{15,11},{... | collective-permute-start | bytes 786440 | tf_op jit(solution)/shard_map/ppermute | solution.py:361
  10.1 0.0 copy-done.6
  10.1 0.1 slice_select_fusion
  10.2 6.7 %collective-permute-start.2 = (bf16[16,1024]{1,0:T(8,128)(2,1)S(1)}, bf16[16,1024]{1,0:T(8,128)(2,1)S(1)}, u32[]{:S(2)}, u32[]{:S(2)}) collective-permute-start(bf16[16,1024]{1,0:T(8,128)(2,1)S(1)} %reshape.25), channel_id=1, source_target_pairs={{6,1},{8,3},{10,5},{12,7},{14,9},{16,11},{18,13},{20,15},{22,17},{... | collective-permute-start | bytes 98312 | tf_op jit(solution)/shard_map/ppermute | solution.py:361
  16.9 0.0 copy-done.1
  16.9 0.0 copy-done
  17.0 0.0 copy-done.5
  17.0 0.0 copy-done.4
  17.0 1.2 %shard_map.100 = (f32[4,96,256]{2,1,0:T(8,128)S(1)}, bf16[64,1024]{1,0:T(8,128)(2,1)S(1)}, bf16[64,1024]{1,0:T(8,128)(2,1)S(1)}, bf16[48,1024]{1,0:T(8,128)(2,1)S(1)}) custom-call(s32[4]{0:T(128)S(1)} %copy-done.5, f32[4,4]{1,0:T(4,128)S(1)} %copy-done.1, bf16[4,4,97]{2,1,0:T(4,128)(2,1)S(1)} %copy-done.4, bf16[4,4,97]{2,1,0:T(4,128)(2,1)S(1)} %copy-done, ...), custom_call_target="tpu_custom_call" | custom-call | flops 1000000 | bytes 2000000 | tf_op jit(solution)/shard_map/pallas_call | solution.py:29
  18.1 3.4 %collective-permute-start.3 = (bf16[48,1024]{1,0:T(8,128)(2,1)S(1)}, bf16[48,1024]{1,0:T(8,128)(2,1)S(1)}, u32[]{:S(2)}, u32[]{:S(2)}) collective-permute-start(bf16[48,1024]{1,0:T(8,128)(2,1)S(1)} %get-tuple-element.45), channel_id=1, source_target_pairs={{64,0},{0,64},{192,128},{128,192},{320,256},{256,320},{448,384},{3... | collective-permute-start | bytes 294920 | tf_op jit(solution)/shard_map/ppermute | solution.py:361
  21.6 0.0 collective-permute-done.1.received
  21.6 2.2 %all-gather.1 = bf16[288,1024]{1,0:T(8,128)(2,1)S(1)} all-gather(bf16[144,1024]{1,0:T(8,128)(2,1)S(1)} %pad_maximum_fusion.1), channel_id=3, replica_groups={{0,1},{2,3},{4,5},{6,7},{8,9},{10,11},{12,13},{14,15},{16,17},{18,19},{..., dimensions={0}, use_global_device_ids=true | all-gather | bytes 884736 | tf_op jit(solution)/shard_map/all_gather | solution.py:383
  23.9 1.3 %collective-permute-done = bf16[128,1024]{1,0:T(8,128)(2,1)S(1)} collective-permute-done((bf16[128,1024]{1,0:T(8,128)(2,1)S(1)}, bf16[128,1024]{1,0:T(8,128)(2,1)S(1)}, u32[]{:S(2)}, u32[]{:S(2)}) %collective-permute-start) | collective-permute-done | bytes 262176 | tf_op jit(solution)/shard_map/ppermute | solution.py:361
  25.2 2.2 %all-gather.2 = bf16[256,1024]{1,0:T(8,128)(2,1)S(1)} all-gather(bf16[128,1024]{1,0:T(8,128)(2,1)S(1)} %collective-permute-done), channel_id=4, replica_groups={{0,1},{2,3},{4,5},{6,7},{8,9},{10,11},{12,13},{14,15},{16,17},{18,19},{..., dimensions={0}, use_global_device_ids=true | all-gather | bytes 786432 | tf_op jit(solution)/shard_map/all_gather | solution.py:383
  27.3 0.0 copy-start.2
  27.4 0.0 copy-start.3
  27.4 0.0 collective-permute-done.2.corner
  27.4 0.4 shard_map.101
  27.8 0.0 collective-permute-done.3.refs_0_
  27.8 4.6 %collective-permute-start.5 = (bf16[160,1024]{1,0:T(8,128)(2,1)S(1)}, bf16[160,1024]{1,0:T(8,128)(2,1)S(1)}, u32[]{:S(2)}, u32[]{:S(2)}) collective-permute-start(bf16[160,1024]{1,0:T(8,128)(2,1)S(1)} %get-tuple-element.48), channel_id=1, source_target_pairs={{128,64},{64,128},{256,192},{192,256},{384,320},{320,384},{129,65}... | collective-permute-start | bytes 983048 | tf_op jit(solution)/shard_map/ppermute | solution.py:361
  32.4 2.2 %collective-permute-start.4 = (bf16[112,1024]{1,0:T(8,128)(2,1)S(1)}, bf16[112,1024]{1,0:T(8,128)(2,1)S(1)}, u32[]{:S(2)}, u32[]{:S(2)}) collective-permute-start(bf16[112,1024]{1,0:T(8,128)(2,1)S(1)} %get-tuple-element.46), channel_id=1, source_target_pairs={{64,0},{0,64},{192,128},{128,192},{320,256},{256,320},{448,384},{3... | collective-permute-start | bytes 688136 | tf_op jit(solution)/shard_map/ppermute | solution.py:361
  34.6 0.0 copy-done.2
  34.6 0.0 copy-done.3
  34.6 2.6 %shard_map.102 = (f32[3,2,16,1024]{3,2,1,0:T(8,128)S(1)}, f32[3,4,24,1024]{3,2,1,0:T(8,128)S(1)}, f32[2,4,16,1024]{3,2,1,0:T(8,128)S(1)}, f32[5,2,16,1024]{3,2,1,0:T(8,128)S(1)}) custom-call(f32[3]{0:T(128)S(1)} %copy-done.2, f32[5]{0:T(128)S(1)} %copy-done.3, f32[4,4]{1,0:T(4,128)S(1)} %copy-done.1, bf16[4,96,1024]{2,1,0:T(8,128)(2,1)S(1)} %get-tuple-element.37.spread, ...), custom_call_target="tpu_custom_call" | custom-call | flops 1000000 | bytes 2000000 | tf_op jit(solution)/shard_map/pallas_call | solution.py:29
  37.3 4.3 %collective-permute-done.5.payload = bf16[160,1024]{1,0:T(8,128)(2,1)S(1)} collective-permute-done((bf16[160,1024]{1,0:T(8,128)(2,1)S(1)}, bf16[160,1024]{1,0:T(8,128)(2,1)S(1)}, u32[]{:S(2)}, u32[]{:S(2)}) %collective-permute-start.5) | collective-permute-done | bytes 327712 | tf_op jit(solution)/shard_map/ppermute | solution.py:361
  41.6 1.3 %shard_map.103.refs_1_ = f32[5,2,16,1024]{3,2,1,0:T(8,128)S(1)} custom-call(f32[3]{0:T(128)S(1)} %copy-done.2, f32[5]{0:T(128)S(1)} %copy-done.3, f32[3,2,16,1024]{3,2,1,0:T(8,128)S(1)} %get-tuple-element.39.outer, f32[3,4,24,1024]{3,2,1,0:T(8,128)S(1)} %get-tuple-element.40.late, f32[2,4,16,1024]{3,2,1,0:T(8,128)S(1)} %get-tuple-element.41.still, ...), custom_call_target="tpu_custom_call" | custom-call | flops 1000000 | bytes 2000000 | tf_op jit(solution)/shard_map/pallas_call | solution.py:29
  42.8 0.0 collective-permute-done.4.payload
  42.9 2.1 %shard_map.104 = f32[5,4,16,1024]{3,2,1,0:T(8,128)} custom-call(f32[3]{0:T(128)S(1)} %copy-done.2, f32[5]{0:T(128)S(1)} %copy-done.3, f32[3,2,16,1024]{3,2,1,0:T(8,128)S(1)} %get-tuple-element.39.outer, f32[3,4,24,1024]{3,2,1,0:T(8,128)S(1)} %get-tuple-element.40.late, f32[2,4,16,1024]{3,2,1,0:T(8,128)S(1)} %get-tuple-element.41.still, ...), custom_call_target="tpu_custom_call" | custom-call | flops 1000000 | bytes 2000000 | tf_op jit(solution)/shard_map/pallas_call | solution.py:29
  (8 shorter events, 0.2 us)
Async XLA Ops:
  0.0 10.1 %copy-start.6 = (pred[4]{0:T(512)(128)(4,1)S(1)}, pred[4]{0:T(512)(128)(4,1)}, u32[]{:S(2)}) copy-start(pred[4]{0:T(512)(128)(4,1)} %constant.12.clone.1) | copy-start | bytes 16
  0.0 16.9 %copy-start.1 = (f32[4,4]{1,0:T(4,128)S(1)}, f32[4,4]{1,0:T(4,128)}, u32[]{:S(2)}) copy-start(f32[4,4]{1,0:T(4,128)} %doses.3) | copy-start | bytes 196
  0.0 16.9 %copy-start = (bf16[4,4,97]{2,1,0:T(4,128)(2,1)S(1)}, bf16[4,4,97]{2,1,0:T(4,128)(2,1)}, u32[]{:S(2)}) copy-start(bf16[4,4,97]{2,1,0:T(4,128)(2,1)} %taps_along.3) | copy-start | bytes 9316
  0.0 16.9 %copy-start.5 = (s32[4]{0:T(128)S(1)}, s32[4]{0:T(128)}, u32[]{:S(2)}) copy-start(s32[4]{0:T(128)} %tilt.1) | copy-start | bytes 52
  0.0 16.9 %copy-start.4 = (bf16[4,4,97]{2,1,0:T(4,128)(2,1)S(1)}, bf16[4,4,97]{2,1,0:T(4,128)(2,1)}, u32[]{:S(2)}) copy-start(bf16[4,4,97]{2,1,0:T(4,128)(2,1)} %taps_across.1) | copy-start | bytes 9316
  3.5 18.1 %collective-permute-start.1 = (bf16[144,1024]{1,0:T(8,128)(2,1)S(1)}, bf16[144,1024]{1,0:T(8,128)(2,1)S(1)}, u32[]{:S(2)}, u32[]{:S(2)}) collective-permute-start(bf16[144,1024]{1,0:T(8,128)(2,1)S(1)} %pad_maximum_fusion), channel_id=1, source_target_pairs={{2,1},{1,2},{4,3},{3,4},{6,5},{5,6},{8,7},{7,8},{10,9},{9,10},{12,... | collective-permute-start | bytes 884744 | tf_op jit(solution)/shard_map/ppermute | solution.py:361
  7.7 17.5 %collective-permute-start = (bf16[128,1024]{1,0:T(8,128)(2,1)S(1)}, bf16[128,1024]{1,0:T(8,128)(2,1)S(1)}, u32[]{:S(2)}, u32[]{:S(2)}) collective-permute-start(bf16[128,1024]{1,0:T(8,128)(2,1)S(1)} %all-gather), channel_id=1, source_target_pairs={{5,1},{7,3},{0,4},{9,5},{2,6},{11,7},{4,8},{13,9},{6,10},{15,11},{... | collective-permute-start | bytes 786440 | tf_op jit(solution)/shard_map/ppermute | solution.py:361
  10.2 17.1 %collective-permute-start.2 = (bf16[16,1024]{1,0:T(8,128)(2,1)S(1)}, bf16[16,1024]{1,0:T(8,128)(2,1)S(1)}, u32[]{:S(2)}, u32[]{:S(2)}) collective-permute-start(bf16[16,1024]{1,0:T(8,128)(2,1)S(1)} %reshape.25), channel_id=1, source_target_pairs={{6,1},{8,3},{10,5},{12,7},{14,9},{16,11},{18,13},{20,15},{22,17},{... | collective-permute-start | bytes 98312 | tf_op jit(solution)/shard_map/ppermute | solution.py:361
  18.1 9.7 %collective-permute-start.3 = (bf16[48,1024]{1,0:T(8,128)(2,1)S(1)}, bf16[48,1024]{1,0:T(8,128)(2,1)S(1)}, u32[]{:S(2)}, u32[]{:S(2)}) collective-permute-start(bf16[48,1024]{1,0:T(8,128)(2,1)S(1)} %get-tuple-element.45), channel_id=1, source_target_pairs={{64,0},{0,64},{192,128},{128,192},{320,256},{256,320},{448,384},{3... | collective-permute-start | bytes 294920 | tf_op jit(solution)/shard_map/ppermute | solution.py:361
  27.3 7.3 %copy-start.2 = (f32[3]{0:T(128)S(1)}, f32[3]{0:T(128)}, u32[]{:S(2)}) copy-start(f32[3]{0:T(128)} %spreads.5) | copy-start | bytes 40
  27.4 7.3 %copy-start.3 = (f32[5]{0:T(128)S(1)}, f32[5]{0:T(128)}, u32[]{:S(2)}) copy-start(f32[5]{0:T(128)} %rates.5) | copy-start | bytes 64
  27.8 13.8 %collective-permute-start.5 = (bf16[160,1024]{1,0:T(8,128)(2,1)S(1)}, bf16[160,1024]{1,0:T(8,128)(2,1)S(1)}, u32[]{:S(2)}, u32[]{:S(2)}) collective-permute-start(bf16[160,1024]{1,0:T(8,128)(2,1)S(1)} %get-tuple-element.48), channel_id=1, source_target_pairs={{128,64},{64,128},{256,192},{192,256},{384,320},{320,384},{129,65}... | collective-permute-start | bytes 983048 | tf_op jit(solution)/shard_map/ppermute | solution.py:361
  32.4 10.4 %collective-permute-start.4 = (bf16[112,1024]{1,0:T(8,128)(2,1)S(1)}, bf16[112,1024]{1,0:T(8,128)(2,1)S(1)}, u32[]{:S(2)}, u32[]{:S(2)}) collective-permute-start(bf16[112,1024]{1,0:T(8,128)(2,1)S(1)} %get-tuple-element.46), channel_id=1, source_target_pairs={{64,0},{0,64},{192,128},{128,192},{320,256},{256,320},{448,384},{3... | collective-permute-start | bytes 688136 | tf_op jit(solution)/shard_map/ppermute | solution.py:361

commit v5 on v4

--- a/solution.py
+++ b/solution.py
@@ -1,5 +1,3 @@
-import functools
-
 import jax
 import jax.numpy as jnp
 from jax import lax
@@ -356,6 +354,13 @@
                     copy(half, f, i).wait()
 
 
+def both_kernel(*refs):
+    given, (from_odd, from_even, early, result) = refs[:8], refs[8:12]
+    near_odd, own_odd, near_even, own_even, earlier, done, sems = refs[12:]
+    react_kernel(0, *given, from_odd, earlier, near_odd, own_odd)
+    react_kernel(1, *given, from_even, early, earlier, result, near_even, own_even, done, sems)
+
+
 def moved(array, axis, size, source):
     route = [(source(i), i) for i in range(size) if source(i) is not None and 0 <= source(i) < size]
     return lax.ppermute(array, axis, route)
@@ -444,23 +449,15 @@
             pltpu.VMEM((16, 128), F32),
         ],
     )
-    given = (diffusivity, reaction_rates, outer, late, still, inner, pair, rims)
-    scratch = [pltpu.VMEM((3, ROWS, LENGTH), F32), pltpu.VMEM((3, GROUP, LENGTH), F32)]
-    half = shape((5, 2, ROWS, LENGTH), F32)
-    earlier = call(
-        functools.partial(react_kernel, 0),
-        half,
-        (*given, from_odd),
-        scalars=2,
-        scratch=scratch,
-    )
+    side_scratch = [pltpu.VMEM((3, ROWS, LENGTH), F32), pltpu.VMEM((3, GROUP, LENGTH), F32)]
+    half = pltpu.VMEM((5, 2, ROWS, LENGTH), F32)
     return call(
-        functools.partial(react_kernel, 1),
+        both_kernel,
         shape((5, LAYERS, ROWS, LENGTH), F32),
-        (*given, from_even, early_even, earlier),
+        (diffusivity, reaction_rates, outer, late, still, inner, pair, rims, from_odd, from_even, early_even),
         scalars=2,
         hbm_out=True,
-        scratch=[*scratch, pltpu.VMEM(half.shape, F32), pltpu.SemaphoreType.DMA((2, 5, 2))],
+        scratch=[*side_scratch, *side_scratch, half, half, pltpu.SemaphoreType.DMA((2, 5, 2))],
     )
 
 

time: 45.2 us -> 44.8 us (level)
  Pallas kernels: 7.57 us -> 6.98 us
    pallas_call x5 -> x4, Pallas kernels: 7.57 us -> 6.98 us  [call(): pl.pallas_call(kernel, out_shape=outs, in_specs=[pl.BlockSpec(memory_spac...]
  transfers between devices with their start and end apart: 6 -> 6, of which waited for: 2 -> 2; matrix products, arithmetic and copies ran while one was open for 0% -> 0% of each run, Pallas kernels for 12% -> 9%
where the time goes in v5:
time: 44.8 us; the launch traced here: 44.5 us
  starting transfers between devices  23.5 us (52%)
  Pallas kernels  6.98 us (16%)
  blocking collectives  6.39 us (14%)
  waiting for transfers between devices  5.78 us (13%)
  other arithmetic  1.45 us (3%)
    ppermute x6, starting transfers between devices, moved(): return lax.ppermute(array, axis, route)  23.5 us
    pallas_call x4, Pallas kernels, call(): pl.pallas_call(kernel, out_shape=outs, in_specs=[pl.BlockSpec(memory_spac...  6.98 us
    all_gather x3, blocking collectives, shared(): return lax.all_gather(array, 'lat', axis_index_groups=couples)  6.39 us
    ppermute x6, waiting for transfers between devices, moved(): return lax.ppermute(array, axis, route)  5.78 us
    mul x1, other arithmetic, body(): clusters = silicon * clusters_before  1.19 us
  transfers between devices with their start and end apart: 6, of which 2 were waited for; matrix products, arithmetic and copies ran while one was open for 0% of the time, Pallas kernels for 9%

profile of v5, /device:TPU:320, one launch (start us, length us, event | category | flops | bytes accessed | tf_op | source)
XLA Modules:
  0.0 44.5 jit_solution(14503718881184569972)
XLA Ops:
  0.0 0.0 copy-start.6
  0.0 0.0 copy-start.1
  0.0 0.0 copy-start
  0.0 0.0 copy-start.5
  0.0 0.0 copy-start.2
  0.0 1.2 %convert_multiply_fusion = (bf16[4,16,1024]{2,1,0:T(8,128)(2,1)S(1)}, bf16[4,16,1024]{2,1,0:T(8,128)(2,1)S(1)}, bf16[4,16,1024]{2,1,0:T(8,128)(2,1)S(1)}) fusion(bf16[4,16,1024]{2,1,0:T(8,128)(2,1)} %param.13, s32[4,16,1024]{2,1,0:T(8,128)} %param.10, bf16[4,16,1024]{2,1,0:T(8,128)(2,1)} %param.12, bf16[4,16,1024]{2,1,0:T(8,128)(2,1)} %param.11), kind=kLoop, calls=%fused_computation.7 | loop fusion | flops 262144 | bytes 1048576 | tf_op jit(solution)/shard_map/mul | solution.py:394
  1.3 0.1 broadcast_select_fusion.1
  1.5 2.0 %all-gather = bf16[128,1024]{1,0:T(8,128)(2,1)S(1)} all-gather(bf16[64,1024]{1,0:T(8,128)(2,1)S(1)} %bitcast.12), channel_id=2, replica_groups={{0,1},{2,3},{4,5},{6,7},{8,9},{10,11},{12,13},{14,15},{16,17},{18,19},{..., dimensions={0}, use_global_device_ids=true | all-gather | bytes 393216 | tf_op jit(solution)/shard_map/all_gather | solution.py:388
  3.5 4.2 %collective-permute-start.1 = (bf16[144,1024]{1,0:T(8,128)(2,1)S(1)}, bf16[144,1024]{1,0:T(8,128)(2,1)S(1)}, u32[]{:S(2)}, u32[]{:S(2)}) collective-permute-start(bf16[144,1024]{1,0:T(8,128)(2,1)S(1)} %pad_maximum_fusion), channel_id=1, source_target_pairs={{2,1},{1,2},{4,3},{3,4},{6,5},{5,6},{8,7},{7,8},{10,9},{9,10},{12,... | collective-permute-start | bytes 884744 | tf_op jit(solution)/shard_map/ppermute | solution.py:366
  7.7 2.4 %collective-permute-start = (bf16[128,1024]{1,0:T(8,128)(2,1)S(1)}, bf16[128,1024]{1,0:T(8,128)(2,1)S(1)}, u32[]{:S(2)}, u32[]{:S(2)}) collective-permute-start(bf16[128,1024]{1,0:T(8,128)(2,1)S(1)} %all-gather), channel_id=1, source_target_pairs={{5,1},{7,3},{0,4},{9,5},{2,6},{11,7},{4,8},{13,9},{6,10},{15,11},{... | collective-permute-start | bytes 786440 | tf_op jit(solution)/shard_map/ppermute | solution.py:366
  10.1 0.0 copy-done.6
  10.1 0.1 slice_select_fusion
  10.2 6.7 %collective-permute-start.2 = (bf16[16,1024]{1,0:T(8,128)(2,1)S(1)}, bf16[16,1024]{1,0:T(8,128)(2,1)S(1)}, u32[]{:S(2)}, u32[]{:S(2)}) collective-permute-start(bf16[16,1024]{1,0:T(8,128)(2,1)S(1)} %reshape.25), channel_id=1, source_target_pairs={{6,1},{8,3},{10,5},{12,7},{14,9},{16,11},{18,13},{20,15},{22,17},{... | collective-permute-start | bytes 98312 | tf_op jit(solution)/shard_map/ppermute | solution.py:366
  16.9 0.0 copy-done.1
  16.9 0.0 copy-done
  17.0 0.0 copy-done.5
  17.0 0.0 copy-done.2
  17.0 1.2 %shard_map.100 = (f32[4,96,256]{2,1,0:T(8,128)S(1)}, bf16[64,1024]{1,0:T(8,128)(2,1)S(1)}, bf16[64,1024]{1,0:T(8,128)(2,1)S(1)}, bf16[48,1024]{1,0:T(8,128)(2,1)S(1)}) custom-call(s32[4]{0:T(128)S(1)} %copy-done.5, f32[4,4]{1,0:T(4,128)S(1)} %copy-done.1, bf16[4,4,97]{2,1,0:T(4,128)(2,1)S(1)} %copy-done.2, bf16[4,4,97]{2,1,0:T(4,128)(2,1)S(1)} %copy-done, ...), custom_call_target="tpu_custom_call" | custom-call | flops 1000000 | bytes 2000000 | tf_op jit(solution)/shard_map/pallas_call | solution.py:27
  18.1 3.4 %collective-permute-start.3 = (bf16[48,1024]{1,0:T(8,128)(2,1)S(1)}, bf16[48,1024]{1,0:T(8,128)(2,1)S(1)}, u32[]{:S(2)}, u32[]{:S(2)}) collective-permute-start(bf16[48,1024]{1,0:T(8,128)(2,1)S(1)} %get-tuple-element.45), channel_id=1, source_target_pairs={{64,0},{0,64},{192,128},{128,192},{320,256},{256,320},{448,384},{3... | collective-permute-start | bytes 294920 | tf_op jit(solution)/shard_map/ppermute | solution.py:366
  21.6 0.0 collective-permute-done.1.received
  21.6 2.2 %all-gather.1 = bf16[288,1024]{1,0:T(8,128)(2,1)S(1)} all-gather(bf16[144,1024]{1,0:T(8,128)(2,1)S(1)} %pad_maximum_fusion.1), channel_id=3, replica_groups={{0,1},{2,3},{4,5},{6,7},{8,9},{10,11},{12,13},{14,15},{16,17},{18,19},{..., dimensions={0}, use_global_device_ids=true | all-gather | bytes 884736 | tf_op jit(solution)/shard_map/all_gather | solution.py:388
  23.9 1.3 %collective-permute-done = bf16[128,1024]{1,0:T(8,128)(2,1)S(1)} collective-permute-done((bf16[128,1024]{1,0:T(8,128)(2,1)S(1)}, bf16[128,1024]{1,0:T(8,128)(2,1)S(1)}, u32[]{:S(2)}, u32[]{:S(2)}) %collective-permute-start) | collective-permute-done | bytes 262176 | tf_op jit(solution)/shard_map/ppermute | solution.py:366
  25.2 2.2 %all-gather.2 = bf16[256,1024]{1,0:T(8,128)(2,1)S(1)} all-gather(bf16[128,1024]{1,0:T(8,128)(2,1)S(1)} %collective-permute-done), channel_id=4, replica_groups={{0,1},{2,3},{4,5},{6,7},{8,9},{10,11},{12,13},{14,15},{16,17},{18,19},{..., dimensions={0}, use_global_device_ids=true | all-gather | bytes 786432 | tf_op jit(solution)/shard_map/all_gather | solution.py:388
  27.3 0.0 copy-start.3
  27.4 0.0 copy-start.4
  27.4 0.0 collective-permute-done.2.corner
  27.4 0.4 shard_map.101
  27.8 0.0 collective-permute-done.3.refs_10_
  27.8 4.6 %collective-permute-start.4 = (bf16[160,1024]{1,0:T(8,128)(2,1)S(1)}, bf16[160,1024]{1,0:T(8,128)(2,1)S(1)}, u32[]{:S(2)}, u32[]{:S(2)}) collective-permute-start(bf16[160,1024]{1,0:T(8,128)(2,1)S(1)} %get-tuple-element.46), channel_id=1, source_target_pairs={{128,64},{64,128},{256,192},{192,256},{384,320},{320,384},{129,65}... | collective-permute-start | bytes 983048 | tf_op jit(solution)/shard_map/ppermute | solution.py:366
  32.4 2.2 %collective-permute-start.5 = (bf16[112,1024]{1,0:T(8,128)(2,1)S(1)}, bf16[112,1024]{1,0:T(8,128)(2,1)S(1)}, u32[]{:S(2)}, u32[]{:S(2)}) collective-permute-start(bf16[112,1024]{1,0:T(8,128)(2,1)S(1)} %get-tuple-element.47), channel_id=1, source_target_pairs={{64,0},{0,64},{192,128},{128,192},{320,256},{256,320},{448,384},{3... | collective-permute-start | bytes 688136 | tf_op jit(solution)/shard_map/ppermute | solution.py:366
  34.6 0.0 copy-done.3
  34.6 0.0 copy-done.4
  34.6 2.6 %shard_map.102 = (f32[3,2,16,1024]{3,2,1,0:T(8,128)S(1)}, f32[3,4,24,1024]{3,2,1,0:T(8,128)S(1)}, f32[2,4,16,1024]{3,2,1,0:T(8,128)S(1)}, f32[5,2,16,1024]{3,2,1,0:T(8,128)S(1)}) custom-call(f32[3]{0:T(128)S(1)} %copy-done.3, f32[5]{0:T(128)S(1)} %copy-done.4, f32[4,4]{1,0:T(4,128)S(1)} %copy-done.1, bf16[4,96,1024]{2,1,0:T(8,128)(2,1)S(1)} %get-tuple-element.37.spread, ...), custom_call_target="tpu_custom_call" | custom-call | flops 1000000 | bytes 2000000 | tf_op jit(solution)/shard_map/pallas_call | solution.py:27
  37.2 4.4 %collective-permute-done.5.refs_9_ = bf16[112,1024]{1,0:T(8,128)(2,1)S(1)} collective-permute-done((bf16[112,1024]{1,0:T(8,128)(2,1)S(1)}, bf16[112,1024]{1,0:T(8,128)(2,1)S(1)}, u32[]{:S(2)}, u32[]{:S(2)}) %collective-permute-start.5) | collective-permute-done | bytes 229408 | tf_op jit(solution)/shard_map/ppermute | solution.py:366
  41.7 0.0 collective-permute-done.4.refs_8_
  41.7 2.8 %shard_map.103 = f32[5,4,16,1024]{3,2,1,0:T(8,128)} custom-call(f32[3]{0:T(128)S(1)} %copy-done.3, f32[5]{0:T(128)S(1)} %copy-done.4, f32[3,2,16,1024]{3,2,1,0:T(8,128)S(1)} %get-tuple-element.39.refs_2_, f32[3,4,24,1024]{3,2,1,0:T(8,128)S(1)} %get-tuple-element.40.refs_3_, f32[2,4,16,1024]{3,2,1,0:T(8,128)S(1)} %get-tuple-element.41.refs_4_, ...), custom_call_target="tpu_custom_call" | custom-call | flops 1000000 | bytes 2000000 | tf_op jit(solution)/shard_map/pallas_call | solution.py:27
  (8 shorter events, 0.2 us)
Async XLA Ops:
  0.0 10.1 %copy-start.6 = (pred[4]{0:T(512)(128)(4,1)S(1)}, pred[4]{0:T(512)(128)(4,1)}, u32[]{:S(2)}) copy-start(pred[4]{0:T(512)(128)(4,1)} %constant.12.clone.1) | copy-start | bytes 16
  0.0 16.9 %copy-start.1 = (f32[4,4]{1,0:T(4,128)S(1)}, f32[4,4]{1,0:T(4,128)}, u32[]{:S(2)}) copy-start(f32[4,4]{1,0:T(4,128)} %doses.3) | copy-start | bytes 196
  0.0 16.9 %copy-start = (bf16[4,4,97]{2,1,0:T(4,128)(2,1)S(1)}, bf16[4,4,97]{2,1,0:T(4,128)(2,1)}, u32[]{:S(2)}) copy-start(bf16[4,4,97]{2,1,0:T(4,128)(2,1)} %taps_along.3) | copy-start | bytes 9316
  0.0 16.9 %copy-start.5 = (s32[4]{0:T(128)S(1)}, s32[4]{0:T(128)}, u32[]{:S(2)}) copy-start(s32[4]{0:T(128)} %tilt.1) | copy-start | bytes 52
  0.0 16.9 %copy-start.2 = (bf16[4,4,97]{2,1,0:T(4,128)(2,1)S(1)}, bf16[4,4,97]{2,1,0:T(4,128)(2,1)}, u32[]{:S(2)}) copy-start(bf16[4,4,97]{2,1,0:T(4,128)(2,1)} %taps_across.1) | copy-start | bytes 9316
  3.5 18.1 %collective-permute-start.1 = (bf16[144,1024]{1,0:T(8,128)(2,1)S(1)}, bf16[144,1024]{1,0:T(8,128)(2,1)S(1)}, u32[]{:S(2)}, u32[]{:S(2)}) collective-permute-start(bf16[144,1024]{1,0:T(8,128)(2,1)S(1)} %pad_maximum_fusion), channel_id=1, source_target_pairs={{2,1},{1,2},{4,3},{3,4},{6,5},{5,6},{8,7},{7,8},{10,9},{9,10},{12,... | collective-permute-start | bytes 884744 | tf_op jit(solution)/shard_map/ppermute | solution.py:366
  7.7 17.5 %collective-permute-start = (bf16[128,1024]{1,0:T(8,128)(2,1)S(1)}, bf16[128,1024]{1,0:T(8,128)(2,1)S(1)}, u32[]{:S(2)}, u32[]{:S(2)}) collective-permute-start(bf16[128,1024]{1,0:T(8,128)(2,1)S(1)} %all-gather), channel_id=1, source_target_pairs={{5,1},{7,3},{0,4},{9,5},{2,6},{11,7},{4,8},{13,9},{6,10},{15,11},{... | collective-permute-start | bytes 786440 | tf_op jit(solution)/shard_map/ppermute | solution.py:366
  10.2 17.1 %collective-permute-start.2 = (bf16[16,1024]{1,0:T(8,128)(2,1)S(1)}, bf16[16,1024]{1,0:T(8,128)(2,1)S(1)}, u32[]{:S(2)}, u32[]{:S(2)}) collective-permute-start(bf16[16,1024]{1,0:T(8,128)(2,1)S(1)} %reshape.25), channel_id=1, source_target_pairs={{6,1},{8,3},{10,5},{12,7},{14,9},{16,11},{18,13},{20,15},{22,17},{... | collective-permute-start | bytes 98312 | tf_op jit(solution)/shard_map/ppermute | solution.py:366
  18.1 9.7 %collective-permute-start.3 = (bf16[48,1024]{1,0:T(8,128)(2,1)S(1)}, bf16[48,1024]{1,0:T(8,128)(2,1)S(1)}, u32[]{:S(2)}, u32[]{:S(2)}) collective-permute-start(bf16[48,1024]{1,0:T(8,128)(2,1)S(1)} %get-tuple-element.45), channel_id=1, source_target_pairs={{64,0},{0,64},{192,128},{128,192},{320,256},{256,320},{448,384},{3... | collective-permute-start | bytes 294920 | tf_op jit(solution)/shard_map/ppermute | solution.py:366
  27.3 7.3 %copy-start.3 = (f32[3]{0:T(128)S(1)}, f32[3]{0:T(128)}, u32[]{:S(2)}) copy-start(f32[3]{0:T(128)} %refs_0_.1) | copy-start | bytes 40
  27.4 7.3 %copy-start.4 = (f32[5]{0:T(128)S(1)}, f32[5]{0:T(128)}, u32[]{:S(2)}) copy-start(f32[5]{0:T(128)} %refs_1_.1) | copy-start | bytes 64
  27.8 13.9 %collective-permute-start.4 = (bf16[160,1024]{1,0:T(8,128)(2,1)S(1)}, bf16[160,1024]{1,0:T(8,128)(2,1)S(1)}, u32[]{:S(2)}, u32[]{:S(2)}) collective-permute-start(bf16[160,1024]{1,0:T(8,128)(2,1)S(1)} %get-tuple-element.46), channel_id=1, source_target_pairs={{128,64},{64,128},{256,192},{192,256},{384,320},{320,384},{129,65}... | collective-permute-start | bytes 983048 | tf_op jit(solution)/shard_map/ppermute | solution.py:366
  32.4 9.3 %collective-permute-start.5 = (bf16[112,1024]{1,0:T(8,128)(2,1)S(1)}, bf16[112,1024]{1,0:T(8,128)(2,1)S(1)}, u32[]{:S(2)}, u32[]{:S(2)}) collective-permute-start(bf16[112,1024]{1,0:T(8,128)(2,1)S(1)} %get-tuple-element.47), channel_id=1, source_target_pairs={{64,0},{0,64},{192,128},{128,192},{320,256},{256,320},{448,384},{3... | collective-permute-start | bytes 688136 | tf_op jit(solution)/shard_map/ppermute | solution.py:366

commit v6 on v5

--- a/solution.py
+++ b/solution.py
@@ -273,7 +273,7 @@
 
 def react_kernel(step, spreads, rates, outer, late, still, inner, pairs, rims_own, payload, *refs):
     if step == 0:
-        done, near_late, own_late = refs
+        done, near_late, own_late, result, sems = refs
     else:
         early, earlier, result, near_late, own_late, done, sems = refs
     odd = lax.rem(lax.axis_index("depth"), 2)
@@ -284,12 +284,11 @@
 
     def copy(half, f, i):
         at = inward(i) if half else 3 - inward(i)
-        return pltpu.make_async_copy((earlier, done)[half].at[f, i], result.at[f, at], sems.at[half, f, i])
-
-    if step == 1:
-        for i in range(2):
-            for f in range(5):
-                copy(0, f, i).start()
+        place = done if half else earlier
+        return pltpu.make_async_copy(place.at[f, i], result.at[f, at], sems.at[half, f, i])
+
+    def send(f, i):
+        pltpu.make_async_copy(done.at[f, i], result.at[f, inward(i)], sems.at[step, f, i]).start()
 
     def pairs_of(z):
         return pairs[pl.ds(pl.multiple_of(ROWS * z, ROWS), ROWS), :].astype(F32)
@@ -331,9 +330,8 @@
         done[f + 1, 1] = inner[f + 1, side] + inner_silicon * (spreads[f] * change[:ROWS])
     for f in (0, 4):
         done[f, 1] = inner[f, side]
-    if step == 1:
-        for f in range(5):
-            copy(1, f, 1).start()
+    for f in range(5):
+        send(f, 1)
     mobile, _ = substep(spreads, rates, silicon, near, far, beside, arsenic, clusters, ROWS)
     for f in range(3):
         near_late[f] = mobile[f]
@@ -345,8 +343,7 @@
     )
     for f, new in enumerate((others[0], *mobile, others[1])):
         done[f, 0] = new
-        if step == 1:
-            copy(1, f, 0).start()
+        send(f, 0)
     if step == 1:
         for half in range(2):
             for i in range(2):
@@ -357,7 +354,7 @@
 def both_kernel(*refs):
     given, (from_odd, from_even, early, result) = refs[:8], refs[8:12]
     near_odd, own_odd, near_even, own_even, earlier, done, sems = refs[12:]
-    react_kernel(0, *given, from_odd, earlier, near_odd, own_odd)
+    react_kernel(0, *given, from_odd, earlier, near_odd, own_odd, result, sems)
     react_kernel(1, *given, from_even, early, earlier, result, near_even, own_even, done, sems)
 
 

time: 44.8 us -> 44.7 us (level)
  no operation moved by 1% of the time
where the time goes in v6:
time: 44.7 us; the launch traced here: 44.5 us
  starting transfers between devices  23.5 us (53%)
  Pallas kernels  6.94 us (16%)
  blocking collectives  6.39 us (14%)
  waiting for transfers between devices  5.78 us (13%)
  other arithmetic  1.45 us (3%)
    ppermute x6, starting transfers between devices, moved(): return lax.ppermute(array, axis, route)  23.5 us
    pallas_call x4, Pallas kernels, call(): pl.pallas_call(kernel, out_shape=outs, in_specs=[pl.BlockSpec(memory_spac...  6.94 us
    all_gather x3, blocking collectives, shared(): return lax.all_gather(array, 'lat', axis_index_groups=couples)  6.39 us
    ppermute x6, waiting for transfers between devices, moved(): return lax.ppermute(array, axis, route)  5.78 us
    mul x1, other arithmetic, body(): clusters = silicon * clusters_before  1.19 us
  transfers between devices with their start and end apart: 6, of which 2 were waited for; matrix products, arithmetic and copies ran while one was open for 0% of the time, Pallas kernels for 9%

profile of v6, /device:TPU:320, one launch (start us, length us, event | category | flops | bytes accessed | tf_op | source)
XLA Modules:
  0.0 44.5 jit_solution(8552257594097449837)
XLA Ops:
  0.0 0.0 copy-start.6
  0.0 0.0 copy-start.1
  0.0 0.0 copy-start
  0.0 0.0 copy-start.5
  0.0 0.0 copy-start.2
  0.0 1.2 %convert_multiply_fusion = (bf16[4,16,1024]{2,1,0:T(8,128)(2,1)S(1)}, bf16[4,16,1024]{2,1,0:T(8,128)(2,1)S(1)}, bf16[4,16,1024]{2,1,0:T(8,128)(2,1)S(1)}) fusion(bf16[4,16,1024]{2,1,0:T(8,128)(2,1)} %param.13, s32[4,16,1024]{2,1,0:T(8,128)} %param.10, bf16[4,16,1024]{2,1,0:T(8,128)(2,1)} %param.12, bf16[4,16,1024]{2,1,0:T(8,128)(2,1)} %param.11), kind=kLoop, calls=%fused_computation.7 | loop fusion | flops 262144 | bytes 1048576 | tf_op jit(solution)/shard_map/mul | solution.py:391
  1.3 0.1 broadcast_select_fusion.1
  1.5 2.0 %all-gather = bf16[128,1024]{1,0:T(8,128)(2,1)S(1)} all-gather(bf16[64,1024]{1,0:T(8,128)(2,1)S(1)} %bitcast.12), channel_id=2, replica_groups={{0,1},{2,3},{4,5},{6,7},{8,9},{10,11},{12,13},{14,15},{16,17},{18,19},{..., dimensions={0}, use_global_device_ids=true | all-gather | bytes 393216 | tf_op jit(solution)/shard_map/all_gather | solution.py:385
  3.5 4.2 %collective-permute-start.1 = (bf16[144,1024]{1,0:T(8,128)(2,1)S(1)}, bf16[144,1024]{1,0:T(8,128)(2,1)S(1)}, u32[]{:S(2)}, u32[]{:S(2)}) collective-permute-start(bf16[144,1024]{1,0:T(8,128)(2,1)S(1)} %pad_maximum_fusion), channel_id=1, source_target_pairs={{2,1},{1,2},{4,3},{3,4},{6,5},{5,6},{8,7},{7,8},{10,9},{9,10},{12,... | collective-permute-start | bytes 884744 | tf_op jit(solution)/shard_map/ppermute | solution.py:363
  7.7 2.4 %collective-permute-start = (bf16[128,1024]{1,0:T(8,128)(2,1)S(1)}, bf16[128,1024]{1,0:T(8,128)(2,1)S(1)}, u32[]{:S(2)}, u32[]{:S(2)}) collective-permute-start(bf16[128,1024]{1,0:T(8,128)(2,1)S(1)} %all-gather), channel_id=1, source_target_pairs={{5,1},{7,3},{0,4},{9,5},{2,6},{11,7},{4,8},{13,9},{6,10},{15,11},{... | collective-permute-start | bytes 786440 | tf_op jit(solution)/shard_map/ppermute | solution.py:363
  10.1 0.0 copy-done.6
  10.1 0.1 slice_select_fusion
  10.2 6.7 %collective-permute-start.2 = (bf16[16,1024]{1,0:T(8,128)(2,1)S(1)}, bf16[16,1024]{1,0:T(8,128)(2,1)S(1)}, u32[]{:S(2)}, u32[]{:S(2)}) collective-permute-start(bf16[16,1024]{1,0:T(8,128)(2,1)S(1)} %reshape.25), channel_id=1, source_target_pairs={{6,1},{8,3},{10,5},{12,7},{14,9},{16,11},{18,13},{20,15},{22,17},{... | collective-permute-start | bytes 98312 | tf_op jit(solution)/shard_map/ppermute | solution.py:363
  16.9 0.0 copy-done.1
  16.9 0.0 copy-done
  17.0 0.0 copy-done.5
  17.0 0.0 copy-done.2
  17.0 1.2 %shard_map.100 = (f32[4,96,256]{2,1,0:T(8,128)S(1)}, bf16[64,1024]{1,0:T(8,128)(2,1)S(1)}, bf16[64,1024]{1,0:T(8,128)(2,1)S(1)}, bf16[48,1024]{1,0:T(8,128)(2,1)S(1)}) custom-call(s32[4]{0:T(128)S(1)} %copy-done.5, f32[4,4]{1,0:T(4,128)S(1)} %copy-done.1, bf16[4,4,97]{2,1,0:T(4,128)(2,1)S(1)} %copy-done.2, bf16[4,4,97]{2,1,0:T(4,128)(2,1)S(1)} %copy-done, ...), custom_call_target="tpu_custom_call" | custom-call | flops 1000000 | bytes 2000000 | tf_op jit(solution)/shard_map/pallas_call | solution.py:27
  18.1 3.4 %collective-permute-start.3 = (bf16[48,1024]{1,0:T(8,128)(2,1)S(1)}, bf16[48,1024]{1,0:T(8,128)(2,1)S(1)}, u32[]{:S(2)}, u32[]{:S(2)}) collective-permute-start(bf16[48,1024]{1,0:T(8,128)(2,1)S(1)} %get-tuple-element.45), channel_id=1, source_target_pairs={{64,0},{0,64},{192,128},{128,192},{320,256},{256,320},{448,384},{3... | collective-permute-start | bytes 294920 | tf_op jit(solution)/shard_map/ppermute | solution.py:363
  21.6 0.0 collective-permute-done.1.received
  21.6 2.2 %all-gather.1 = bf16[288,1024]{1,0:T(8,128)(2,1)S(1)} all-gather(bf16[144,1024]{1,0:T(8,128)(2,1)S(1)} %pad_maximum_fusion.1), channel_id=3, replica_groups={{0,1},{2,3},{4,5},{6,7},{8,9},{10,11},{12,13},{14,15},{16,17},{18,19},{..., dimensions={0}, use_global_device_ids=true | all-gather | bytes 884736 | tf_op jit(solution)/shard_map/all_gather | solution.py:385
  23.9 1.3 %collective-permute-done = bf16[128,1024]{1,0:T(8,128)(2,1)S(1)} collective-permute-done((bf16[128,1024]{1,0:T(8,128)(2,1)S(1)}, bf16[128,1024]{1,0:T(8,128)(2,1)S(1)}, u32[]{:S(2)}, u32[]{:S(2)}) %collective-permute-start) | collective-permute-done | bytes 262176 | tf_op jit(solution)/shard_map/ppermute | solution.py:363
  25.2 2.2 %all-gather.2 = bf16[256,1024]{1,0:T(8,128)(2,1)S(1)} all-gather(bf16[128,1024]{1,0:T(8,128)(2,1)S(1)} %collective-permute-done), channel_id=4, replica_groups={{0,1},{2,3},{4,5},{6,7},{8,9},{10,11},{12,13},{14,15},{16,17},{18,19},{..., dimensions={0}, use_global_device_ids=true | all-gather | bytes 786432 | tf_op jit(solution)/shard_map/all_gather | solution.py:385
  27.3 0.0 copy-start.3
  27.4 0.0 copy-start.4
  27.4 0.0 collective-permute-done.2.corner
  27.4 0.4 shard_map.101
  27.8 0.0 collective-permute-done.3.refs_10_
  27.8 4.6 %collective-permute-start.4 = (bf16[160,1024]{1,0:T(8,128)(2,1)S(1)}, bf16[160,1024]{1,0:T(8,128)(2,1)S(1)}, u32[]{:S(2)}, u32[]{:S(2)}) collective-permute-start(bf16[160,1024]{1,0:T(8,128)(2,1)S(1)} %get-tuple-element.46), channel_id=1, source_target_pairs={{128,64},{64,128},{256,192},{192,256},{384,320},{320,384},{129,65}... | collective-permute-start | bytes 983048 | tf_op jit(solution)/shard_map/ppermute | solution.py:363
  32.4 2.2 %collective-permute-start.5 = (bf16[112,1024]{1,0:T(8,128)(2,1)S(1)}, bf16[112,1024]{1,0:T(8,128)(2,1)S(1)}, u32[]{:S(2)}, u32[]{:S(2)}) collective-permute-start(bf16[112,1024]{1,0:T(8,128)(2,1)S(1)} %get-tuple-element.47), channel_id=1, source_target_pairs={{64,0},{0,64},{192,128},{128,192},{320,256},{256,320},{448,384},{3... | collective-permute-start | bytes 688136 | tf_op jit(solution)/shard_map/ppermute | solution.py:363
  34.6 0.0 copy-done.3
  34.6 0.0 copy-done.4
  34.6 2.6 %shard_map.102 = (f32[3,2,16,1024]{3,2,1,0:T(8,128)S(1)}, f32[3,4,24,1024]{3,2,1,0:T(8,128)S(1)}, f32[2,4,16,1024]{3,2,1,0:T(8,128)S(1)}, f32[5,2,16,1024]{3,2,1,0:T(8,128)S(1)}) custom-call(f32[3]{0:T(128)S(1)} %copy-done.3, f32[5]{0:T(128)S(1)} %copy-done.4, f32[4,4]{1,0:T(4,128)S(1)} %copy-done.1, bf16[4,96,1024]{2,1,0:T(8,128)(2,1)S(1)} %get-tuple-element.37.spread, ...), custom_call_target="tpu_custom_call" | custom-call | flops 1000000 | bytes 2000000 | tf_op jit(solution)/shard_map/pallas_call | solution.py:27
  37.2 4.4 %collective-permute-done.5.refs_9_ = bf16[112,1024]{1,0:T(8,128)(2,1)S(1)} collective-permute-done((bf16[112,1024]{1,0:T(8,128)(2,1)S(1)}, bf16[112,1024]{1,0:T(8,128)(2,1)S(1)}, u32[]{:S(2)}, u32[]{:S(2)}) %collective-permute-start.5) | collective-permute-done | bytes 229408 | tf_op jit(solution)/shard_map/ppermute | solution.py:363
  41.7 0.0 collective-permute-done.4.refs_8_
  41.7 2.8 %shard_map.103 = f32[5,4,16,1024]{3,2,1,0:T(8,128)} custom-call(f32[3]{0:T(128)S(1)} %copy-done.3, f32[5]{0:T(128)S(1)} %copy-done.4, f32[3,2,16,1024]{3,2,1,0:T(8,128)S(1)} %get-tuple-element.39.refs_2_, f32[3,4,24,1024]{3,2,1,0:T(8,128)S(1)} %get-tuple-element.40.refs_3_, f32[2,4,16,1024]{3,2,1,0:T(8,128)S(1)} %get-tuple-element.41.refs_4_, ...), custom_call_target="tpu_custom_call" | custom-call | flops 1000000 | bytes 2000000 | tf_op jit(solution)/shard_map/pallas_call | solution.py:27
  (8 shorter events, 0.2 us)
Async XLA Ops:
  0.0 10.1 %copy-start.6 = (pred[4]{0:T(512)(128)(4,1)S(1)}, pred[4]{0:T(512)(128)(4,1)}, u32[]{:S(2)}) copy-start(pred[4]{0:T(512)(128)(4,1)} %constant.12.clone.1) | copy-start | bytes 16
  0.0 16.9 %copy-start.1 = (f32[4,4]{1,0:T(4,128)S(1)}, f32[4,4]{1,0:T(4,128)}, u32[]{:S(2)}) copy-start(f32[4,4]{1,0:T(4,128)} %doses.3) | copy-start | bytes 196
  0.0 16.9 %copy-start = (bf16[4,4,97]{2,1,0:T(4,128)(2,1)S(1)}, bf16[4,4,97]{2,1,0:T(4,128)(2,1)}, u32[]{:S(2)}) copy-start(bf16[4,4,97]{2,1,0:T(4,128)(2,1)} %taps_along.3) | copy-start | bytes 9316
  0.0 16.9 %copy-start.5 = (s32[4]{0:T(128)S(1)}, s32[4]{0:T(128)}, u32[]{:S(2)}) copy-start(s32[4]{0:T(128)} %tilt.1) | copy-start | bytes 52
  0.0 16.9 %copy-start.2 = (bf16[4,4,97]{2,1,0:T(4,128)(2,1)S(1)}, bf16[4,4,97]{2,1,0:T(4,128)(2,1)}, u32[]{:S(2)}) copy-start(bf16[4,4,97]{2,1,0:T(4,128)(2,1)} %taps_across.1) | copy-start | bytes 9316
  3.5 18.1 %collective-permute-start.1 = (bf16[144,1024]{1,0:T(8,128)(2,1)S(1)}, bf16[144,1024]{1,0:T(8,128)(2,1)S(1)}, u32[]{:S(2)}, u32[]{:S(2)}) collective-permute-start(bf16[144,1024]{1,0:T(8,128)(2,1)S(1)} %pad_maximum_fusion), channel_id=1, source_target_pairs={{2,1},{1,2},{4,3},{3,4},{6,5},{5,6},{8,7},{7,8},{10,9},{9,10},{12,... | collective-permute-start | bytes 884744 | tf_op jit(solution)/shard_map/ppermute | solution.py:363
  7.7 17.5 %collective-permute-start = (bf16[128,1024]{1,0:T(8,128)(2,1)S(1)}, bf16[128,1024]{1,0:T(8,128)(2,1)S(1)}, u32[]{:S(2)}, u32[]{:S(2)}) collective-permute-start(bf16[128,1024]{1,0:T(8,128)(2,1)S(1)} %all-gather), channel_id=1, source_target_pairs={{5,1},{7,3},{0,4},{9,5},{2,6},{11,7},{4,8},{13,9},{6,10},{15,11},{... | collective-permute-start | bytes 786440 | tf_op jit(solution)/shard_map/ppermute | solution.py:363
  10.2 17.1 %collective-permute-start.2 = (bf16[16,1024]{1,0:T(8,128)(2,1)S(1)}, bf16[16,1024]{1,0:T(8,128)(2,1)S(1)}, u32[]{:S(2)}, u32[]{:S(2)}) collective-permute-start(bf16[16,1024]{1,0:T(8,128)(2,1)S(1)} %reshape.25), channel_id=1, source_target_pairs={{6,1},{8,3},{10,5},{12,7},{14,9},{16,11},{18,13},{20,15},{22,17},{... | collective-permute-start | bytes 98312 | tf_op jit(solution)/shard_map/ppermute | solution.py:363
  18.1 9.7 %collective-permute-start.3 = (bf16[48,1024]{1,0:T(8,128)(2,1)S(1)}, bf16[48,1024]{1,0:T(8,128)(2,1)S(1)}, u32[]{:S(2)}, u32[]{:S(2)}) collective-permute-start(bf16[48,1024]{1,0:T(8,128)(2,1)S(1)} %get-tuple-element.45), channel_id=1, source_target_pairs={{64,0},{0,64},{192,128},{128,192},{320,256},{256,320},{448,384},{3... | collective-permute-start | bytes 294920 | tf_op jit(solution)/shard_map/ppermute | solution.py:363
  27.3 7.3 %copy-start.3 = (f32[3]{0:T(128)S(1)}, f32[3]{0:T(128)}, u32[]{:S(2)}) copy-start(f32[3]{0:T(128)} %refs_0_.1) | copy-start | bytes 40
  27.4 7.3 %copy-start.4 = (f32[5]{0:T(128)S(1)}, f32[5]{0:T(128)}, u32[]{:S(2)}) copy-start(f32[5]{0:T(128)} %refs_1_.1) | copy-start | bytes 64
  27.8 13.9 %collective-permute-start.4 = (bf16[160,1024]{1,0:T(8,128)(2,1)S(1)}, bf16[160,1024]{1,0:T(8,128)(2,1)S(1)}, u32[]{:S(2)}, u32[]{:S(2)}) collective-permute-start(bf16[160,1024]{1,0:T(8,128)(2,1)S(1)} %get-tuple-element.46), channel_id=1, source_target_pairs={{128,64},{64,128},{256,192},{192,256},{384,320},{320,384},{129,65}... | collective-permute-start | bytes 983048 | tf_op jit(solution)/shard_map/ppermute | solution.py:363
  32.4 9.3 %collective-permute-start.5 = (bf16[112,1024]{1,0:T(8,128)(2,1)S(1)}, bf16[112,1024]{1,0:T(8,128)(2,1)S(1)}, u32[]{:S(2)}, u32[]{:S(2)}) collective-permute-start(bf16[112,1024]{1,0:T(8,128)(2,1)S(1)} %get-tuple-element.47), channel_id=1, source_target_pairs={{64,0},{0,64},{192,128},{128,192},{320,256},{256,320},{448,384},{3... | collective-permute-start | bytes 688136 | tf_op jit(solution)/shard_map/ppermute | solution.py:363
